TPU v7x, 512 devices: a whole 4x4x16 slice. The times are simulated.
512 devices in a mesh: img: 16 (over z), tile: 32 (over x, y, core).
Axes of the slice: x: 4, y: 4, z: 16, core: 2. Of those that a mesh axis runs over, the one named last changes fastest.
Arguments:
- features: bfloat16 [16, 512, 64, 256], P('img', 'tile'), may hold values from -6 to 6
- weight: bfloat16 [3, 3, 256, 256], replicated, may hold values from -0.125 to 0.125
- pool_grad: bfloat16 [16, 512, 7, 7, 256], P('img', 'tile'), may hold values from -6 to 6
- hard_index: int32 [16, 512], P('img', 'tile'), may hold values from 0 to 19999, as said below
- boxes: int32 [16, 20000, 4], P('img'), may hold values from 0 to 498, as said below
Outputs:
- x_grad: bfloat16 [16, 512, 64, 256], P('img', 'tile')
- weight_grad: float32 [256, 3, 3, 256], P('tile')
Inputs may be any that keep to these rules, and one draw needn't show every extreme that they name: `hard_index`: among the 16 entries of one tile index's block, at most 2 choose boxes whose top row lies in any one tile (rows t * 16 to t * 16 + 15); in every image some tile receives exactly 2 from every block.
All inputs are finite; a program needn't handle non-finite values.
Results may differ from a plain program's by a relative error of at most 0.0058.
Values may be sent and summed in bfloat16 or wider, within the bound.
No kernel may reach another device: no remote copies, remote signals or barrier semaphores. Data moves between devices by JAX's collectives and lax.ppermute only.
A program may use at most 64 MiB of HBM per device.

v0:
```python
import jax
import jax.numpy as jnp
from jax import lax
from jax.sharding import PartitionSpec as P

C = 256
TR = 16
MW = 64
ROI_DEV = 16
CAP = 2
REACH = 14
BINS = 7


FRAC_ROW = 0.25
FRAC_COL = 0.75


def from_behind(value, axis, steps):
    count = lax.axis_size(axis)
    initial, last = (max(0, -steps), min(count, count - steps))
    return lax.ppermute(value, axis, [(source, source + steps) for source in range(initial, last)])


def extended_2(cells, sides, width):
    for axis, dim in sides:
        count = lax.axis_size(axis)
        ends = count - 1
        head = lax.slice_in_dim(cells, 0, width, axis=dim)
        tail = lax.slice_in_dim(cells, cells.shape[dim] - width, cells.shape[dim], axis=dim)
        cells = jnp.concatenate(
            [
                lax.ppermute(tail, axis, [(i, (i + 1) % count) for i in range(ends)]),
                cells,
                lax.ppermute(head, axis, [((i + 1) % count, i) for i in range(ends)]),
            ],
            axis=dim,
        )
    return cells


def bin_weights(start, step, length, frac):
    places = start[:, None] + jnp.arange(BINS, dtype=jnp.int32)[None, :] * step[:, None]
    grid = jnp.arange(length, dtype=jnp.int32)[None, None, :]
    near = jnp.where(grid == places[:, :, None], 1.0 - frac, 0.0)
    beyond = jnp.where(grid == places[:, :, None] + 1, frac, 0.0)
    return (near + beyond).astype(jnp.float32)


def body(features, weight, pool_grad, hard_index, boxes):
    tile_count = lax.axis_size("tile")
    image_count = lax.axis_size("img")
    chosen = boxes[0][hard_index[0]]
    top_row = chosen[:, 0]
    owners = top_row // TR
    local_top = top_row - owners * TR
    member = (owners[:, None] == jnp.arange(tile_count, dtype=jnp.int32)[None, :]).astype(jnp.int32)
    ranking = jnp.sum(jnp.cumsum(member, axis=0) * member, axis=1) - 1
    slot_place = owners * CAP + ranking
    slot_total = tile_count * CAP
    placing = jnp.arange(slot_total, dtype=jnp.int32)[:, None] == slot_place[None, :]
    flat_grad = pool_grad[0].reshape(ROI_DEV, BINS * BINS * C)
    send_grad = jnp.dot(
        placing.astype(jnp.bfloat16), flat_grad, preferred_element_type=jnp.float32
    ).astype(jnp.bfloat16)
    geometry = jnp.stack([local_top, chosen[:, 1], chosen[:, 2], chosen[:, 3]], axis=1).astype(
        jnp.float32
    )
    send_geom = jnp.dot(placing.astype(jnp.float32), geometry).astype(jnp.bfloat16)
    got_grad, got_geom = (
        lax.all_to_all(
            send_grad.reshape(tile_count, CAP, BINS * BINS * C),
            "tile",
            split_axis=0,
            concat_axis=0,
            tiled=True,
        ),
        lax.all_to_all(
            send_geom.reshape(tile_count, CAP, 4), "tile", split_axis=0, concat_axis=0, tiled=True
        ),
    )
    got_grad = got_grad.reshape(slot_total, BINS, BINS, C)
    got_geom = got_geom.reshape(slot_total, 4).astype(jnp.int32)
    ext_rows = TR + REACH - 1
    row_weight = bin_weights(got_geom[:, 0], got_geom[:, 2], ext_rows, FRAC_ROW).astype(
        jnp.bfloat16
    )
    col_weight = bin_weights(got_geom[:, 1], got_geom[:, 3], MW, FRAC_COL).astype(jnp.bfloat16)
    block_size = 16
    block_count = slot_total // block_size

    def add_block(running, pieces):
        grad_block, row_block, col_block = pieces
        spread = jnp.einsum(
            "sijc,sjw->siwc", grad_block, col_block, preferred_element_type=jnp.float32
        ).astype(jnp.bfloat16)
        update = jnp.einsum(
            "kr,kf->rf",
            row_block.reshape(block_size * BINS, ext_rows),
            spread.reshape(block_size * BINS, MW * C),
            preferred_element_type=jnp.float32,
        )
        return (running + update, None)

    extended, unused_out = lax.scan(
        add_block,
        jnp.zeros((ext_rows, MW * C), jnp.float32),
        (
            got_grad.reshape(block_count, block_size, BINS, BINS, C),
            row_weight.reshape(block_count, block_size, BINS, ext_rows),
            col_weight.reshape(block_count, block_size, BINS, MW),
        ),
    )
    extended = extended.reshape(ext_rows, MW, C)
    carried = from_behind(extended[TR:], "tile", 1)
    own_rows = jnp.concatenate([extended[: REACH - 1] + carried, extended[REACH - 1 : TR]], axis=0)
    framed = extended_2(own_rows.astype(jnp.bfloat16), (("tile", 0),), 1)
    padded = jnp.pad(framed, ((0, 0), (1, 1), (0, 0)))
    windows = jnp.stack(
        [
            padded[2 - row_off : 2 - row_off + TR, 2 - col_off : 2 - col_off + MW]
            for row_off in range(3)
            for col_off in range(3)
        ],
        axis=2,
    )
    x_grad = jnp.einsum(
        "hwkd,kcd->hwc", windows, weight.reshape(9, C, C), preferred_element_type=jnp.float32
    ).astype(jnp.bfloat16)[None]
    flat_in = features[0].reshape(TR * MW, C)
    flat_windows = windows.reshape(TR * MW, 9, C)
    summed = lax.psum(
        jnp.einsum(
            "qc,qkd->ckd", flat_in, flat_windows, preferred_element_type=jnp.float32
        ).reshape(C, 3, 3, C),
        "img",
    )
    weight_grad = lax.psum_scatter(summed, "tile", scatter_dimension=0, tiled=True) / image_count
    return (x_grad, weight_grad)


def solution(mesh):
    return jax.shard_map(
        body,
        mesh=mesh,
        in_specs=(
            P("img", "tile", None, None),
            P(),
            P("img", "tile", None, None, None),
            P("img", "tile"),
            P("img", None, None),
        ),
        out_specs=(P("img", "tile", None, None), P("tile", None, None, None)),
        check_vma=False,
    )
```

profile of v0, /device:TPU:2, one launch (start us, length us, event | category | flops | bytes accessed | tf_op | source)
XLA Modules:
  0.0 427.1 jit_solution(12905283870724772626)
XLA Ops:
  7.2 6.5 %copy.79 = s32[1,20000,4]{2,1,0:T(8,128)} copy(s32[1,20000,4]{1,2,0:T(4,128)} %param.11) | data formatting | bytes 640000 | tf_op args[4]
  13.9 4.5 %gather_fusion = s32[16,4]{1,0:T(8,128)S(1)} fusion(s32[20000,4]{1,0:T(8,128)} %bitcast.121, s32[1024]{0:T(1024)S(1)} %pad_clamp_fusion), kind=kCustom, calls=%fused_computation | custom fusion | bytes 576 | tf_op jit(solution)/shard_map/gather | solution.py:53
  19.9 9.4 %all-to-all-start = ((bf16[32,2,4]{2,1,0:T(2,128)(2,1)}), bf16[32,2,4]{2,1,0:T(2,128)(2,1)S(1)}, u32[]{:S(2)}, u32[]{:S(2)}) async-start(bf16[32,2,4]{2,1,0:T(2,128)(2,1)} %bitcast.2), calls=%async_computation | async-start | bytes 32768 | tf_op jit(solution)/shard_map/all_to_all | solution.py:78
  32.1 3.5 all-to-all-done
  35.5 5.8 %all-to-all-start.1 = ((bf16[32,2,12544]{2,1,0:T(2,128)(2,1)}), bf16[32,2,12544]{2,1,0:T(2,128)(2,1)}, u32[]{:S(2)}, u32[]{:S(2)}) async-start(bf16[32,2,12544]{2,1,0:T(2,128)(2,1)} %reshape.314), calls=%async_computation.1 | async-start | bytes 3211264 | tf_op jit(solution)/shard_map/all_to_all | solution.py:71
  43.2 18.7 %all-to-all-done.1 = bf16[32,2,12544]{2,1,0:T(2,128)(2,1)} async-done(((bf16[32,2,12544]{2,1,0:T(2,128)(2,1)}), bf16[32,2,12544]{2,1,0:T(2,128)(2,1)}, u32[]{:S(2)}, u32[]{:S(2)}) %all-to-all-start.1) | async-done | bytes 1605664 | tf_op jit(solution)/shard_map/all_to_all | solution.py:71
  61.9 5.0 %reshape_reshape.3 = bf16[4,16,7,7,256]{4,3,2,1,0:T(8,128)(2,1)} reshape(bf16[32,2,12544]{2,1,0:T(2,128)(2,1)} %all-to-all-done.1) | data formatting | bytes 3211264 | tf_op jit(solution)/shard_map/reshape;reshape | solution.py:109
  66.9 40.2 %while.11 = (s32[]{:T(128)}, f32[29,16384]{1,0:T(8,128)S(1)}, bf16[4,16,7,29]{3,2,1,0:T(8,128)(2,1)}, bf16[4,16,7,64]{3,2,1,0:T(8,128)(2,1)S(1)}, bf16[4,16,7,7,256]{4,3,2,1,0:T(8,128)(2,1)}, /*index=5*/s32[]{:T(128)}, s32[]{:T(128)}) while((s32[]{:T(128)}, f32[29,16384]{1,0:T(8,128)S(1)}, bf16[4,16,7,29]{3,2,1,0:T(8,128)(2,1)}, ...), condition=%wide.region_3.4_spmd.clone, body=%wide.region_2.3_spmd.clone.sunk | while | flops 134905856 | bytes 19006276 | solution.py:105
  69.9 4.3 %copy.117 = bf16[14,8,64,256]{3,1,2,0:T(8,128)(2,1)} copy(bf16[14,8,64,256]{3,2,1,0:T(8,128)(2,1)S(1)} %bitcast.118) | data formatting | bytes 7340032 | tf_op jit(solution)/shard_map/while
  74.2 2.8 convolution_add_fusion.2
  80.0 4.3 %copy.117 = bf16[14,8,64,256]{3,1,2,0:T(8,128)(2,1)} copy(bf16[14,8,64,256]{3,2,1,0:T(8,128)(2,1)S(1)} %bitcast.118) | data formatting | bytes 7340032 | tf_op jit(solution)/shard_map/while
  84.3 2.8 convolution_add_fusion.2
  90.0 4.3 %copy.117 = bf16[14,8,64,256]{3,1,2,0:T(8,128)(2,1)} copy(bf16[14,8,64,256]{3,2,1,0:T(8,128)(2,1)S(1)} %bitcast.118) | data formatting | bytes 7340032 | tf_op jit(solution)/shard_map/while
  94.3 2.8 convolution_add_fusion.2
  100.1 4.3 %copy.117 = bf16[14,8,64,256]{3,1,2,0:T(8,128)(2,1)} copy(bf16[14,8,64,256]{3,2,1,0:T(8,128)(2,1)S(1)} %bitcast.118) | data formatting | bytes 7340032 | tf_op jit(solution)/shard_map/while
  104.4 2.8 convolution_add_fusion.2
  110.5 13.3 %collective-permute-done = f32[13,64,256]{2,1,0:T(8,128)S(1)} collective-permute-done((f32[13,64,256]{2,1,0:T(8,128)S(1)}, f32[13,64,256]{2,1,0:T(8,128)S(1)}, u32[]{:S(2)}, u32[]{:S(2)}) %collective-permute-start) | collective-permute-done | bytes 852000 | tf_op jit(solution)/shard_map/ppermute | solution.py:22
  126.0 2.6 collective-permute-start.1
  129.6 3.7 collective-permute-done.1
  172.3 5.1 %fusion.28 = f32[9,256,256]{2,1,0:T(8,128)} fusion(bf16[1024,9,256]{0,2,1:T(8,128)(2,1)} %constant_dynamic-update-slice_fusion, bf16[1024,256,1]{1,0,2:T(8,128)(2,1)S(1)} %bitcast.142), kind=kOutput, calls=%fused_computation.96 | convolution fusion | flops 1207959552 | bytes 7602176 | tf_op jit(solution)/shard_map/qc,qkd->ckd/dot_general | solution.py:133
  177.4 3.1 copy.104
  181.4 101.6 %reduce-scatter.2.cloned.1.call-done = f32[8,3,3,256]{3,0,2,1:T(8,128)} async-done(((f32[256,3,3,256]{3,0,2,1:T(8,128)}), f32[8,3,3,256]{3,0,2,1:T(8,128)}) %reduce-scatter.2.cloned.1.call-update) | async-done | bytes 73744 | tf_op jit(solution)/shard_map/reduce_scatter | solution.py:138
  283.1 4.5 %fusion.7 = bf16[1,16,64,256]{3,2,1,0:T(8,128)(2,1)} fusion(bf16[16,64,9,256]{3,1,2,0:T(8,128)(2,1)} %bitcast_dynamic-update-slice_fusion.7, bf16[9,256,256,1]{2,1,0,3:T(8,128)(2,1)S(1)} %bitcast.117), kind=kOutput, calls=%fused_computation.15 | convolution fusion | flops 1208221696 | bytes 6422528 | tf_op jit(solution)/shard_map/hwkd,kcd->hwc/dot_general | solution.py:127
  287.6 131.1 %all-reduce.3.cloned.1.call-done = f32[8,3,3,256]{3,0,2,1:T(8,128)} async-done(((f32[8,3,3,256]{3,0,2,1:T(8,128)}), f32[8,3,3,256]{3,0,2,1:T(8,128)}) %all-reduce.3.cloned.1.call-update) | async-done | bytes 73744 | tf_op jit(solution)/shard_map/psum | solution.py:132
  (101 shorter events, 66.0 us)
Async XLA Ops:
  7.2 275.9 %copy-start = (bf16[3,3,256,256]{3,2,1,0:T(8,128)(2,1)S(1)}, bf16[3,3,256,256]{3,2,1,0:T(8,128)(2,1)}, u32[]{:S(2)}) copy-start(bf16[3,3,256,256]{3,2,1,0:T(8,128)(2,1)} %param.8) | copy-start | bytes 3538948
  7.2 6.5 %copy-start.5 = (s32[1,16]{1,0:T(1,128)S(1)}, s32[1,16]{1,0:T(1,128)}, u32[]{:S(2)}) copy-start(s32[1,16]{1,0:T(1,128)} %param.10) | copy-start | bytes 196
  7.2 22.2 %copy-start.4 = (bf16[1,16,7,7,256]{4,1,3,2,0:T(8,128)(2,1)S(1)}, bf16[1,16,7,7,256]{4,1,3,2,0:T(8,128)(2,1)}, u32[]{:S(2)}) copy-start(bf16[1,16,7,7,256]{4,1,3,2,0:T(8,128)(2,1)} %param.9) | copy-start | bytes 1204228
  19.9 15.6 %all-to-all-start = ((bf16[32,2,4]{2,1,0:T(2,128)(2,1)}), bf16[32,2,4]{2,1,0:T(2,128)(2,1)S(1)}, u32[]{:S(2)}, u32[]{:S(2)}) async-start(bf16[32,2,4]{2,1,0:T(2,128)(2,1)} %bitcast.2), calls=%async_computation | async-start | bytes 32768 | tf_op jit(solution)/shard_map/all_to_all | solution.py:78
  35.5 26.4 %all-to-all-start.1 = ((bf16[32,2,12544]{2,1,0:T(2,128)(2,1)}), bf16[32,2,12544]{2,1,0:T(2,128)(2,1)}, u32[]{:S(2)}, u32[]{:S(2)}) async-start(bf16[32,2,12544]{2,1,0:T(2,128)(2,1)} %reshape.314), calls=%async_computation.1 | async-start | bytes 3211264 | tf_op jit(solution)/shard_map/all_to_all | solution.py:71
  41.3 241.8 %reduce-scatter.2.cloned.1.call-start = ((), (), s32[]{:S(2)}) async-start(), calls=%async_computation.3 | async-start | bytes 2433024 | tf_op jit(solution)/shard_map/reduce_scatter | solution.py:138
  107.7 16.1 %collective-permute-start = (f32[13,64,256]{2,1,0:T(8,128)S(1)}, f32[13,64,256]{2,1,0:T(8,128)S(1)}, u32[]{:S(2)}, u32[]{:S(2)}) collective-permute-start(f32[13,64,256]{2,1,0:T(8,128)S(1)} %slice.114), channel_id=1, source_target_pairs={{0,1},{1,2},{2,3},{3,4},{4,5},{5,6},{6,7},{7,8},{8,9},{9,10},{10,1... | collective-permute-start | bytes 2555912 | tf_op jit(solution)/shard_map/ppermute | solution.py:22
  124.1 5.6 %collective-permute-start.2 = (bf16[1,64,256]{2,1,0:T(8,128)(2,1)S(1)}, bf16[1,64,256]{2,1,0:T(8,128)(2,1)S(1)}, u32[]{:S(2)}, u32[]{:S(2)}) collective-permute-start(bf16[1,64,256]{2,1,0:T(8,128)(2,1)S(1)} %get-tuple-element.79), channel_id=1, source_target_pairs={{1,0},{2,1},{3,2},{4,3},{5,4},{6,5},{7,6},{8,7},{9,8},{10,9},{11,1... | collective-permute-start | bytes 98312 | tf_op jit(solution)/shard_map/ppermute | solution.py:35
  126.0 7.3 %collective-permute-start.1 = (bf16[1,64,256]{2,1,0:T(8,128)(2,1)S(1)}, bf16[1,64,256]{2,1,0:T(8,128)(2,1)S(1)}, u32[]{:S(2)}, u32[]{:S(2)}) collective-permute-start(bf16[1,64,256]{2,1,0:T(8,128)(2,1)S(1)} %get-tuple-element.78), channel_id=1, source_target_pairs={{0,1},{1,2},{2,3},{3,4},{4,5},{5,6},{6,7},{7,8},{8,9},{9,10},{10,1... | collective-permute-start | bytes 98312 | tf_op jit(solution)/shard_map/ppermute | solution.py:33
  157.2 12.7 %copy-start.1 = (bf16[1024,1,256]{0,2,1:T(8,128)(2,1)S(1)}, bf16[1024,1,256]{0,2,1:T(8,128)(2,1)}, u32[]{:S(2)}) copy-start(bf16[1024,1,256]{0,2,1:T(8,128)(2,1)} %copy.101) | copy-start | bytes 1572868
  160.3 10.4 %copy-start.2 = (bf16[1024,1,256]{0,2,1:T(8,128)(2,1)S(1)}, bf16[1024,1,256]{0,2,1:T(8,128)(2,1)}, u32[]{:S(2)}) copy-start(bf16[1024,1,256]{0,2,1:T(8,128)(2,1)} %copy.102) | copy-start | bytes 1572868
  160.3 11.2 %copy-start.3 = (bf16[1024,1,256]{0,2,1:T(8,128)(2,1)S(1)}, bf16[1024,1,256]{0,2,1:T(8,128)(2,1)}, u32[]{:S(2)}) copy-start(bf16[1024,1,256]{0,2,1:T(8,128)(2,1)} %copy.103) | copy-start | bytes 1572868
  160.3 12.1 %copy-start.6 = (bf16[1,16,64,256]{3,2,1,0:T(8,128)(2,1)S(1)}, bf16[1,16,64,256]{3,2,1,0:T(8,128)(2,1)}, u32[]{:S(2)}) copy-start(bf16[1,16,64,256]{3,2,1,0:T(8,128)(2,1)} %param.7) | copy-start | bytes 1572868
  180.6 238.2 %all-reduce.3.cloned.1.call-start = ((), (), s32[]{:S(2)}) async-start(), calls=%async_computation.4 | async-start | bytes 147456 | tf_op jit(solution)/shard_map/psum | solution.py:132
Sparse Core Ops, SparseCore 0:
  180.7 102.3 reduce-scatter.1
  285.5 133.2 all-reduce.2
where the time goes:
time: 429 us; the launch traced here: 427 us
  waiting for transfers between devices  272 us (63%)
  local copies, waits for them, and re-layouts  81.5 us (19%)
  matrix products  30.2 us (7%)
  starting transfers between devices  22.2 us (5%)
  between operations  14.3 us (3%)
  other arithmetic  6.86 us (2%)
    psum x1, waiting for transfers between devices, body(): lax.psum(jnp.einsum('qc,qkd->ckd', flat_in, flat_windows, preferred_eleme...  131 us
    reduce_scatter x1, waiting for transfers between devices, body(): lax.psum_scatter(summed, 'tile', scatter_dimension=0, tiled=True)  102 us
    unnamed x33, local copies, waits for them, and re-layouts  25 us
    all_to_all x1, waiting for transfers between devices, body(): lax.all_to_all(send_grad.reshape(tile_count, CAP, BINS * BINS * C), 'tile...  18.7 us
    while x4, local copies, waits for them, and re-layouts  17.2 us
    another operation x10, local copies, waits for them, and re-layouts, body(): jnp.stack([padded[2 - row_off:2 - row_off + TR, 2 - col_off:2 - col_off +...  17.1 us
    ppermute x1, waiting for transfers between devices, from_behind(): lax.ppermute(value, axis, [(source, source + steps) for source in range(i...  13.3 us
    dot_general x4, matrix products, add_block(): jnp.einsum('kr,kf->rf', row_block.reshape(block_size * BINS, ext_rows), s...  11 us
  transfers between devices with their start and end apart: 7, of which 6 were waited for; matrix products, arithmetic and copies ran while one was open for 3% of the time, Pallas kernels for 0%

commit v1 on v0

v1 whole, which is shorter than its diff:
```python
import jax
import jax.numpy as jnp
from jax import lax
from jax.experimental import pallas as pl
from jax.experimental.pallas import tpu as pltpu
from jax.sharding import Mesh, PartitionSpec as P

C = 256
TR = 16
MW = 64
ROI_DEV = 16
CAP = 2
REACH = 14
BINS = 7
CELLS = BINS * BINS
PROPS = 20000
TILES = 32
IMAGES = 16
EXT = TR + REACH - 1
SLOT = CELLS + 1
BLOCK = 104
SLOTS = TILES * CAP
KDIM = TILES * BLOCK
LANES = 128
WHOLE = PROPS // LANES * LANES
F32 = jnp.float32
BF16 = jnp.bfloat16
I32 = jnp.int32
VMEM_BYTES = 56 * 1024 * 1024
CIN = C // TILES
NPART = 9 * CIN


def vmem():
    return pl.BlockSpec(memory_space=pltpu.VMEM)


def iota(shape, dim):
    return lax.broadcasted_iota(I32, shape, dim)


def dispatch_kernel(index_ref, boxes_ref, grad_ref, out_ref):
    lane16 = iota((4, ROI_DEV), 1)
    lanes = iota((4, LANES), 1)
    tail = jnp.concatenate(
        [boxes_ref[:, WHOLE:], jnp.zeros((4, LANES - (PROPS - WHOLE)), I32)], axis=1
    )
    chosen = jnp.zeros((4, ROI_DEV), I32)
    for r in range(ROI_DEV):
        index = index_ref[0, r]
        block = index // LANES
        at = jnp.minimum(block, WHOLE // LANES - 1) * LANES
        row = jnp.where(
            block == WHOLE // LANES, tail, boxes_ref[:, pl.ds(pl.multiple_of(at, LANES), LANES)]
        )
        found = jnp.sum(jnp.where(lanes == index - block * LANES, row, 0), axis=1, keepdims=True)
        chosen = jnp.where(lane16 == r, found, chosen)
    chosen = chosen.astype(F32)
    top = chosen[0:1]
    owner = jnp.floor(top * (1.0 / TR))
    local_top = top - owner * TR
    diag = iota((ROI_DEV, ROI_DEV), 0) == iota((ROI_DEV, ROI_DEV), 1)

    def column(row):
        wide = jnp.broadcast_to(row, (ROI_DEV, ROI_DEV))
        return jnp.sum(jnp.where(diag, wide, 0.0), axis=1, keepdims=True)

    before = iota((ROI_DEV, ROI_DEV), 0) < iota((ROI_DEV, ROI_DEV), 1)
    same = column(owner) == owner
    rank = jnp.sum(jnp.where(before & same, 1.0, 0.0), axis=0, keepdims=True)
    field = iota((ROI_DEV, C), 1)
    box_rows = jnp.zeros((ROI_DEV, C), F32)
    for f, row in enumerate((local_top, chosen[1:2], chosen[2:3], chosen[3:4])):
        box_rows = jnp.where(field == f, column(row), box_rows)
    depth = SLOT * ROI_DEV
    wide = jnp.concatenate([owner, rank, jnp.zeros((6, ROI_DEV), F32)], axis=0).astype(BF16)
    spreading = iota((ROI_DEV, depth), 1) % ROI_DEV == iota((ROI_DEV, depth), 0)
    spread = jnp.dot(wide, spreading.astype(F32).astype(BF16), preferred_element_type=F32)
    cell = (iota((1, depth), 1) // ROI_DEV).astype(F32)
    goal = (spread[0:1] * BLOCK + spread[1:2] * SLOT + cell).astype(I32)
    source = jnp.concatenate(
        [grad_ref[...].reshape(CELLS * ROI_DEV, C), box_rows.astype(BF16)], axis=0
    )
    step = KDIM // 8
    for m in range(8):
        place = iota((step, depth), 0) + m * step == goal
        out_ref[m * 4 : m * 4 + 4] = (
            jnp.dot(place.astype(F32).astype(BF16), source, preferred_element_type=F32)
            .astype(BF16)
            .reshape(4, BLOCK, C)
        )


def dispatch(index, boxes_t, grads):
    return pl.pallas_call(
        dispatch_kernel,
        out_shape=jax.ShapeDtypeStruct((TILES, BLOCK, C), BF16),
        in_specs=[pl.BlockSpec(memory_space=pltpu.SMEM), vmem(), vmem()],
        out_specs=vmem(),
        compiler_params=pltpu.CompilerParams(vmem_limit_bytes=VMEM_BYTES),
        name="dispatch",
    )(index, boxes_t, grads)


def weights_of(got_ref, rows_ref, cols_ref):
    slot = iota((SLOTS, KDIM), 0)
    cell = iota((SLOTS, KDIM), 1)
    first = (slot // CAP) * BLOCK + (slot % CAP) * SLOT
    pick = (cell == first + CELLS).astype(F32).astype(BF16)
    box = jnp.dot(pick, got_ref[...].reshape(KDIM, C), preferred_element_type=F32)
    box = box[:, :LANES].T[:8].astype(BF16)
    cover = ((cell >= first) & (cell < first + CELLS)).astype(F32).astype(BF16)
    field = jnp.dot(box, cover, preferred_element_type=F32).astype(I32)
    within = iota((1, KDIM), 1) % BLOCK
    inside = within < CAP * SLOT
    within = within % SLOT
    inside = inside & (within < CELLS)
    row_bin = within // BINS
    col_bin = within - row_bin * BINS
    row = jnp.where(inside, field[0:1] + row_bin * field[2:3], -9)
    col = field[1:2] + col_bin * field[3:4]
    grid = iota((32, KDIM), 0)
    rows_ref[...] = jnp.where(grid == row, 0.75, jnp.where(grid == row + 1, 0.25, 0.0))
    grid = iota((MW, KDIM), 0)
    cols_ref[...] = jnp.where(grid == col, 0.25, jnp.where(grid == col + 1, 0.75, 0.0)).astype(BF16)


def rows_of(start, count, got_ref, rows_ref, cols_ref, left_ref):
    cols = cols_ref[...]
    for h in range(count):
        left_ref[h * MW : (h + 1) * MW] = cols * rows_ref[start + h : start + h + 1, :].astype(BF16)
    return jnp.dot(
        left_ref[: count * MW], got_ref[...].reshape(KDIM, C), preferred_element_type=F32
    )


def scatter_kernel(got_ref, own_ref, above_ref, below_ref, rows_ref, cols_ref, left_ref):
    weights_of(got_ref, rows_ref, cols_ref)
    for start, count in ((0, 8), (8, 8), (16, 8), (24, 5)):
        part = rows_of(start, count, got_ref, rows_ref, cols_ref, left_ref)
        if start < TR:
            own_ref[start * MW : (start + count) * MW] = part
        if start == 0:
            below_ref[...] = part[:MW].astype(BF16)
        if start == 8:
            above_ref[:MW] = part[7 * MW :].astype(BF16)
        if start == 16:
            own_ref[TR * MW :] = part[:MW]
            above_ref[MW : 9 * MW] = part.astype(BF16)
        if start == 24:
            above_ref[9 * MW :] = part.astype(BF16)


def scatter(got):
    return pl.pallas_call(
        scatter_kernel,
        out_shape=(
            jax.ShapeDtypeStruct(((TR + 1) * MW, C), F32),
            jax.ShapeDtypeStruct((REACH * MW, C), BF16),
            jax.ShapeDtypeStruct((MW, C), BF16),
        ),
        in_specs=[vmem()],
        out_specs=(vmem(), vmem(), vmem()),
        scratch_shapes=[
            pltpu.VMEM((32, KDIM), F32),
            pltpu.VMEM((MW, KDIM), BF16),
            pltpu.VMEM((8 * MW, KDIM), BF16),
        ],
        compiler_params=pltpu.CompilerParams(vmem_limit_bytes=VMEM_BYTES),
        name="scatter",
    )(got)


def filter_kernel(own_ref, above_ref, below_ref, features_ref, part_ref, shifted_ref):
    rows = (TR + 2) * MW
    whole = jnp.concatenate(
        [
            above_ref[:MW].astype(F32),
            own_ref[: (REACH - 1) * MW] + above_ref[MW:].astype(F32),
            own_ref[(REACH - 1) * MW : TR * MW],
            own_ref[TR * MW :] + below_ref[...].astype(F32),
        ],
        axis=0,
    )
    column = iota((rows, C), 0) % MW
    shifted_ref[0] = jnp.where(column == MW - 1, 0.0, pltpu.roll(whole, rows - 1, 0)).astype(BF16)
    shifted_ref[1] = whole.astype(BF16)
    shifted_ref[2] = jnp.where(column == 0, 0.0, pltpu.roll(whole, 1, 0)).astype(BF16)
    turned = features_ref[...].T
    for a in range(3):
        for e in range(3):
            part = jnp.dot(
                turned,
                shifted_ref[e, (2 - a) * MW : (2 - a + TR) * MW],
                preferred_element_type=F32,
            )
            at = (a * 3 + e) * CIN
            part_ref[:, at : at + CIN, :] = part.reshape(TILES, CIN, C).astype(BF16)


def filter_part(own, above, below, features):
    return pl.pallas_call(
        filter_kernel,
        out_shape=(
            jax.ShapeDtypeStruct((TILES, NPART, C), BF16),
            jax.ShapeDtypeStruct((3, (TR + 2) * MW, C), BF16),
        ),
        in_specs=[vmem()] * 4,
        out_specs=(vmem(), vmem()),
        compiler_params=pltpu.CompilerParams(vmem_limit_bytes=VMEM_BYTES),
        name="filter",
    )(own, above, below, features)


def input_kernel(shifted_ref, weight_ref, out_ref):
    total = jnp.zeros((TR * MW, C), F32)
    for a in range(3):
        for e in range(3):
            total = total + lax.dot_general(
                shifted_ref[e, (2 - a) * MW : (2 - a + TR) * MW],
                weight_ref[a * 3 + e],
                (((1,), (1,)), ((), ())),
                preferred_element_type=F32,
            )
    out_ref[...] = total.astype(BF16)


def input_part(shifted, weight):
    return pl.pallas_call(
        input_kernel,
        out_shape=jax.ShapeDtypeStruct((TR * MW, C), BF16),
        in_specs=[vmem()] * 2,
        out_specs=vmem(),
        compiler_params=pltpu.CompilerParams(vmem_limit_bytes=VMEM_BYTES),
        name="input",
        cost_estimate=pl.CostEstimate(
            flops=2 * TR * MW * 9 * C * C, bytes_accessed=4 << 20, transcendentals=0
        ),
    )(shifted, weight)


def body(features, weight, pool_grad, hard_index, boxes):
    grads = pool_grad[0].transpose(1, 2, 0, 3).reshape(CELLS, ROI_DEV, C)
    send = dispatch(hard_index, boxes[0].T, grads)
    got = lax.all_to_all(send, "tile", split_axis=0, concat_axis=0, tiled=True)
    own, above, below = scatter(got)
    up = [(t, t + 1) for t in range(TILES - 1)]
    above = lax.ppermute(above, "tile", up)
    below = lax.ppermute(below, "tile", [(b, a) for a, b in up])
    part, shifted = filter_part(own, above, below, features[0].reshape(TR * MW, C))
    parts = part.reshape(TILES, 4, NPART // 4, C).transpose(1, 0, 2, 3)
    parts = parts.reshape(4 * TILES, NPART // 4, C)
    parts = lax.all_to_all(parts, ("zl", "tile"), split_axis=0, concat_axis=0, tiled=True)
    x_grad = input_part(shifted, weight.reshape(9, C, C)).reshape(1, TR, MW, C)
    summed = jnp.sum(parts.astype(F32), axis=0).astype(BF16)
    copies = jnp.broadcast_to(summed[None], (IMAGES, NPART // 4, C))
    copies = lax.all_to_all(copies, ("zh", "zl"), split_axis=0, concat_axis=0, tiled=True)
    total = jnp.sum(copies.reshape(4, 4, NPART // 4, C).astype(F32), axis=0) * (1.0 / IMAGES)
    total = total.reshape(9, CIN, C).transpose(1, 0, 2).reshape(CIN, 3, 3, C)
    return x_grad, total


def solution(mesh):
    split = Mesh(mesh.devices.reshape(4, 4, TILES), ("zh", "zl", "tile"))
    images = ("zh", "zl")
    return jax.shard_map(
        body,
        mesh=split,
        in_specs=(
            P(images, "tile", None, None),
            P(),
            P(images, "tile", None, None, None),
            P(images, "tile"),
            P(images, None, None),
        ),
        out_specs=(P(images, "tile", None, None), P("tile", None, None, None)),
        check_vma=False,
    )
```

time: 429 us -> 144 us (0.34)
  the two profiles are of different devices: /device:TPU:2 before, /device:TPU:32 now
where the time goes in v1:
time: 144 us; the launch traced here: 143 us
  blocking collectives  85.2 us (59%)
  Pallas kernels  20 us (14%)
  starting transfers between devices  18.7 us (13%)
  waiting for transfers between devices  13.7 us (10%)
  local copies, waits for them, and re-layouts  4.56 us (3%)
    all_to_all x1, blocking collectives, body(): lax.all_to_all(parts, ('zl', 'tile'), split_axis=0, concat_axis=0, tiled=...  54 us
    all_to_all x1, blocking collectives, body(): got = lax.all_to_all(send, 'tile', split_axis=0, concat_axis=0, tiled=True)  31.2 us
    all_to_all x1, starting transfers between devices, body(): lax.all_to_all(copies, ('zh', 'zl'), split_axis=0, concat_axis=0, tiled=T...  14.8 us
    all_to_all x1, waiting for transfers between devices, body(): lax.all_to_all(copies, ('zh', 'zl'), split_axis=0, concat_axis=0, tiled=T...  11.7 us
    pallas_call x1, Pallas kernels, scatter(): pl.pallas_call(scatter_kernel, out_shape=(jax.ShapeDtypeStruct(((TR + 1)...  7.29 us
    pallas_call x1, Pallas kernels, dispatch(): pl.pallas_call(dispatch_kernel, out_shape=jax.ShapeDtypeStruct((TILES, BL...  4.59 us
    pallas_call x1, Pallas kernels, filter_part(): pl.pallas_call(filter_kernel, out_shape=(jax.ShapeDtypeStruct((TILES, NPA...  4.14 us
    pallas_call x1, Pallas kernels, input_part(): pl.pallas_call(input_kernel, out_shape=jax.ShapeDtypeStruct((TR * MW, C),...  4.01 us
  transfers between devices with their start and end apart: 3, of which 2 were waited for; matrix products, arithmetic and copies ran while one was open for 0% of the time, Pallas kernels for 3%

profile of v1, /device:TPU:32, one launch (start us, length us, event | category | flops | bytes accessed | tf_op | source)
XLA Modules:
  0.0 143.3 jit_solution(1307872666008152758)
XLA Ops:
  0.6 4.6 %dispatch.1 = bf16[32,104,256]{2,1,0:T(8,128)(2,1)} custom-call(s32[1,16]{1,0:T(1,128)} %index_ref.1, s32[4,20000]{1,0:T(4,128)} %bitcast.24, bf16[49,16,256]{2,1,0:T(8,128)(2,1)} %bitcast.23), custom_call_target="tpu_custom_call" | custom-call | tf_op jit(solution)/shard_map/dispatch/pallas_call | solution.py:95
  5.2 31.2 %all_to_all.15.got_ref = bf16[32,104,256]{2,1,0:T(8,128)(2,1)} all-to-all(bf16[32,104,256]{2,1,0:T(8,128)(2,1)} %dispatch.1), channel_id=1, replica_groups=mesh['zh'=4,'zl'=4,'tile'=32] {'tile'}, dimensions={0} | all-to-all | bytes 3407872 | tf_op jit(solution)/shard_map/all_to_all | solution.py:245
  36.4 7.3 %scatter.1 = (f32[1088,256]{1,0:T(8,128)}, bf16[896,256]{1,0:T(8,128)(2,1)}, bf16[64,256]{1,0:T(8,128)(2,1)}) custom-call(bf16[32,104,256]{2,1,0:T(8,128)(2,1)} %all_to_all.15.got_ref), custom_call_target="tpu_custom_call" | custom-call | tf_op jit(solution)/shard_map/scatter/pallas_call | solution.py:155
  43.7 2.6 %collective-permute-start = (bf16[896,256]{1,0:T(8,128)(2,1)}, bf16[896,256]{1,0:T(8,128)(2,1)S(1)}, u32[]{:S(2)}, u32[]{:S(2)}) collective-permute-start(bf16[896,256]{1,0:T(8,128)(2,1)} %get-tuple-element.8), channel_id=1, source_target_pairs={{0,1},{1,2},{2,3},{3,4},{4,5},{5,6},{6,7},{7,8},{8,9},{9,10},{10,1... | collective-permute-start | bytes 1376264 | tf_op jit(solution)/shard_map/ppermute | solution.py:248
  46.3 1.3 collective-permute-start.1
  47.6 2.0 %collective-permute-done.1.below_ref = bf16[64,256]{1,0:T(8,128)(2,1)S(1)} collective-permute-done((bf16[64,256]{1,0:T(8,128)(2,1)}, bf16[64,256]{1,0:T(8,128)(2,1)S(1)}, u32[]{:S(2)}, u32[]{:S(2)}) %collective-permute-start.1) | collective-permute-done | bytes 32800 | tf_op jit(solution)/shard_map/ppermute | solution.py:249
  49.6 0.0 copy-start.1
  49.6 0.0 collective-permute-done.above_ref
  49.6 0.0 copy-start
  49.6 0.6 copy-done.1
  50.2 0.2 copy-done
  50.4 4.1 %filter.1 = (bf16[32,72,256]{2,1,0:T(8,128)(2,1)}, bf16[3,1152,256]{2,1,0:T(8,128)(2,1)}) custom-call(f32[1088,256]{1,0:T(8,128)} %get-tuple-element.7.own_ref, bf16[896,256]{1,0:T(8,128)(2,1)} %copy-done, bf16[64,256]{1,0:T(8,128)(2,1)} %copy-done.1, bf16[1024,256]{1,0:T(8,128)(2,1)} %bitcast.22), custom_call_target="tpu_custom_call" | custom-call | tf_op jit(solution)/shard_map/filter/pallas_call | solution.py:202
  54.5 1.5 %copy.27 = bf16[32,72,256]{2,0,1:T(8,128)(2,1)S(1)} copy(bf16[32,72,256]{2,1,0:T(8,128)(2,1)} %get-tuple-element.11) | data formatting | bytes 2359296 | tf_op jit(solution)/shard_map/filter/pallas_call | solution.py:202
  56.1 0.1 copy.28
  56.2 0.7 copy.29
  56.9 54.0 %all_to_all.16 = bf16[128,18,256]{2,1,0:T(8,128)(2,1)S(1)} all-to-all(bf16[128,18,256]{2,1,0:T(8,128)(2,1)S(1)} %copy.29), channel_id=1, replica_groups=mesh['zh'=4,'zl'=4,'tile'=32] {'zl','tile'}, dimensions={0} | all-to-all | bytes 2359296 | tf_op jit(solution)/shard_map/all_to_all | solution.py:253
  110.9 0.3 reduce_sum.21
  111.2 0.7 broadcast_in_dim.2
  111.9 14.8 %all-to-all-start.2 = ((bf16[16,18,256]{2,1,0:T(8,128)(2,1)}), bf16[16,18,256]{2,1,0:T(8,128)(2,1)S(1)}, u32[]{:S(2)}, u32[]{:S(2)}) async-start(bf16[16,18,256]{2,1,0:T(8,128)(2,1)} %broadcast_in_dim.2), calls=%async_computation.2 | async-start | bytes 393216 | tf_op jit(solution)/shard_map/all_to_all | solution.py:257
  126.8 4.0 %input.1 = bf16[1024,256]{1,0:T(8,128)(2,1)} custom-call(bf16[3,1152,256]{2,1,0:T(8,128)(2,1)} %get-tuple-element.10.shifted_ref, bf16[9,256,256]{2,1,0:T(8,128)(2,1)} %bitcast.26), custom_call_target="tpu_custom_call" | custom-call | flops 1207959552 | bytes 4194304 | tf_op jit(solution)/shard_map/input/pallas_call | solution.py:229
  130.8 11.7 %all-to-all-done.2 = bf16[16,18,256]{2,1,0:T(8,128)(2,1)S(1)} async-done(((bf16[16,18,256]{2,1,0:T(8,128)(2,1)}), bf16[16,18,256]{2,1,0:T(8,128)(2,1)S(1)}, u32[]{:S(2)}, u32[]{:S(2)}) %all-to-all-start.2) | async-done | bytes 147488 | tf_op jit(solution)/shard_map/all_to_all | solution.py:257
  142.5 0.1 reshape.36
  142.6 0.1 reduce_sum.22
  142.7 0.6 mul.12
  (3 shorter events, 0.1 us)
Async XLA Ops:
  43.7 5.9 %collective-permute-start = (bf16[896,256]{1,0:T(8,128)(2,1)}, bf16[896,256]{1,0:T(8,128)(2,1)S(1)}, u32[]{:S(2)}, u32[]{:S(2)}) collective-permute-start(bf16[896,256]{1,0:T(8,128)(2,1)} %get-tuple-element.8), channel_id=1, source_target_pairs={{0,1},{1,2},{2,3},{3,4},{4,5},{5,6},{6,7},{7,8},{8,9},{9,10},{10,1... | collective-permute-start | bytes 1376264 | tf_op jit(solution)/shard_map/ppermute | solution.py:248
  46.3 3.3 %collective-permute-start.1 = (bf16[64,256]{1,0:T(8,128)(2,1)}, bf16[64,256]{1,0:T(8,128)(2,1)S(1)}, u32[]{:S(2)}, u32[]{:S(2)}) collective-permute-start(bf16[64,256]{1,0:T(8,128)(2,1)} %get-tuple-element.9), channel_id=1, source_target_pairs={{1,0},{2,1},{3,2},{4,3},{5,4},{6,5},{7,6},{8,7},{9,8},{10,9},{11,1... | collective-permute-start | bytes 98312 | tf_op jit(solution)/shard_map/ppermute | solution.py:249
  49.6 0.6 copy-start.1
  49.6 0.8 copy-start
  111.9 30.5 %all-to-all-start.2 = ((bf16[16,18,256]{2,1,0:T(8,128)(2,1)}), bf16[16,18,256]{2,1,0:T(8,128)(2,1)S(1)}, u32[]{:S(2)}, u32[]{:S(2)}) async-start(bf16[16,18,256]{2,1,0:T(8,128)(2,1)} %broadcast_in_dim.2), calls=%async_computation.2 | async-start | bytes 393216 | tf_op jit(solution)/shard_map/all_to_all | solution.py:257

commit v2 on v1

v2 whole, which is shorter than its diff:
```python
import functools

import jax
import jax.numpy as jnp
from jax import lax
from jax.experimental import pallas as pl
from jax.experimental.pallas import tpu as pltpu
from jax.sharding import Mesh, PartitionSpec as P

C = 256
TR = 16
MW = 64
ROI_DEV = 16
CAP = 2
REACH = 14
BINS = 7
CELLS = BINS * BINS
PROPS = 20000
TILES = 32
IMAGES = 16
EXT = TR + REACH - 1
REACHED = 32 * MW
SLOT = CELLS + 1
BLOCK = 104
SLOTS = TILES * CAP
KDIM = TILES * BLOCK
LANES = 128
WHOLE = PROPS // LANES * LANES
F32 = jnp.float32
BF16 = jnp.bfloat16
I32 = jnp.int32
CIN = C // TILES
NPART = 9 * CIN


def vmem():
    return pl.BlockSpec(memory_space=pltpu.VMEM)


def cost(flops, moved):
    return pl.CostEstimate(flops=flops, bytes_accessed=moved, transcendentals=0)


def iota(shape, dim):
    return lax.broadcasted_iota(I32, shape, dim)


def dispatch_kernel(
    index_hbm, boxes_hbm, grad_hbm, out_hbm, index_ref, boxes_ref, source_ref, sent_ref, sems
):
    copies = [
        pltpu.make_async_copy(index_hbm, index_ref, sems.at[0]),
        pltpu.make_async_copy(boxes_hbm, boxes_ref, sems.at[1]),
        pltpu.make_async_copy(grad_hbm, source_ref.at[:CELLS], sems.at[2]),
    ]
    for copy in copies:
        copy.start()
    copies[0].wait()
    copies[1].wait()
    lane16 = iota((4, ROI_DEV), 1)
    lanes = iota((4, LANES), 1)
    tail = jnp.concatenate(
        [boxes_ref[:, WHOLE:], jnp.zeros((4, LANES - (PROPS - WHOLE)), I32)], axis=1
    )
    chosen = jnp.zeros((4, ROI_DEV), I32)
    for r in range(ROI_DEV):
        index = index_ref[0, r]
        block = index // LANES
        at = jnp.minimum(block, WHOLE // LANES - 1) * LANES
        row = jnp.where(
            block == WHOLE // LANES, tail, boxes_ref[:, pl.ds(pl.multiple_of(at, LANES), LANES)]
        )
        found = jnp.sum(jnp.where(lanes == index - block * LANES, row, 0), axis=1, keepdims=True)
        chosen = jnp.where(lane16 == r, found, chosen)
    chosen = chosen.astype(F32)
    top = chosen[0:1]
    owner = jnp.floor(top * (1.0 / TR))
    local_top = top - owner * TR
    diag = iota((ROI_DEV, ROI_DEV), 0) == iota((ROI_DEV, ROI_DEV), 1)

    def column(row):
        wide = jnp.broadcast_to(row, (ROI_DEV, ROI_DEV))
        return jnp.sum(jnp.where(diag, wide, 0.0), axis=1, keepdims=True)

    before = iota((ROI_DEV, ROI_DEV), 0) < iota((ROI_DEV, ROI_DEV), 1)
    same = column(owner) == owner
    rank = jnp.sum(jnp.where(before & same, 1.0, 0.0), axis=0, keepdims=True)
    field = iota((ROI_DEV, C), 1)
    box_rows = jnp.zeros((ROI_DEV, C), F32)
    for f, row in enumerate((local_top, chosen[1:2], chosen[2:3], chosen[3:4])):
        box_rows = jnp.where(field == f, column(row), box_rows)
    source_ref[CELLS] = box_rows.astype(BF16)
    depth = SLOT * ROI_DEV
    wide = jnp.concatenate([owner, rank, jnp.zeros((6, ROI_DEV), F32)], axis=0).astype(BF16)
    spreading = iota((ROI_DEV, depth), 1) % ROI_DEV == iota((ROI_DEV, depth), 0)
    spread = jnp.dot(wide, spreading.astype(F32).astype(BF16), preferred_element_type=F32)
    cell = (iota((1, depth), 1) // ROI_DEV).astype(F32)
    goal = (spread[0:1] * BLOCK + spread[1:2] * SLOT + cell).astype(I32)
    copies[2].wait()
    source = source_ref[...].reshape(depth, C)
    step = KDIM // 8
    sent = []
    for m in range(8):
        part = pl.ds(m * (TILES // 8), TILES // 8)
        place = iota((step, depth), 0) == goal - m * step
        sent_ref[part] = (
            jnp.dot(place.astype(F32).astype(BF16), source, preferred_element_type=F32)
            .astype(BF16)
            .reshape(TILES // 8, BLOCK, C)
        )
        sent.append(pltpu.make_async_copy(sent_ref.at[part], out_hbm.at[part], sems.at[3 + m]))
        sent[-1].start()
    for copy in sent:
        copy.wait()


def dispatch(index, boxes_t, grads):
    return pl.pallas_call(
        dispatch_kernel,
        out_shape=jax.ShapeDtypeStruct((TILES, BLOCK, C), BF16),
        in_specs=[pl.BlockSpec(memory_space=pl.ANY)] * 3,
        out_specs=pl.BlockSpec(memory_space=pl.ANY),
        scratch_shapes=[
            pltpu.SMEM((1, ROI_DEV), I32),
            pltpu.VMEM((4, PROPS), I32),
            pltpu.VMEM((SLOT, ROI_DEV, C), BF16),
            pltpu.VMEM((TILES, BLOCK, C), BF16),
            pltpu.SemaphoreType.DMA((11,)),
        ],
        compiler_params=pltpu.CompilerParams(vmem_limit_bytes=60 << 20),
        name="dispatch",
        cost_estimate=cost(2 * KDIM * SLOT * ROI_DEV * C, 3 << 20),
    )(index, boxes_t, grads)


def weights_of(got_ref, rows_ref, cols_ref):
    slot = iota((SLOTS, KDIM), 0)
    cell = iota((SLOTS, KDIM), 1)
    first = (slot % TILES) * BLOCK + (slot // TILES) * SLOT
    box = jnp.concatenate(
        [got_ref[:, s * SLOT + CELLS, :LANES].astype(F32) for s in range(CAP)], axis=0
    )
    box = box.T[:8].astype(BF16)
    cover = ((cell >= first) & (cell < first + CELLS)).astype(F32).astype(BF16)
    field = jnp.dot(box, cover, preferred_element_type=F32).astype(I32)
    within = iota((1, KDIM), 1) % BLOCK
    inside = within < CAP * SLOT
    within = within % SLOT
    inside = inside & (within < CELLS)
    row_bin = within // BINS
    col_bin = within - row_bin * BINS
    row = jnp.where(inside, field[0:1] + row_bin * field[2:3], -9)
    col = field[1:2] + col_bin * field[3:4]
    grid = iota((32, KDIM), 0)
    rows_ref[...] = jnp.where(grid == row, 0.75, jnp.where(grid == row + 1, 0.25, 0.0))
    grid = iota((MW, KDIM), 0)
    cols_ref[...] = jnp.where(grid == col, 0.25, jnp.where(grid == col + 1, 0.75, 0.0)).astype(BF16)


def rows_of(start, count, got_ref, rows_ref, cols_ref, left_ref):
    cols = cols_ref[...]
    for h in range(count):
        left_ref[h * MW : (h + 1) * MW] = cols * rows_ref[start + h : start + h + 1, :].astype(BF16)
    return jnp.dot(
        left_ref[: count * MW], got_ref[...].reshape(KDIM, C), preferred_element_type=F32
    )


def turn_kernel(before_ref, own_ref, after_ref, out_ref):
    rows = jnp.concatenate(
        [before_ref[...], own_ref[...], after_ref[...], jnp.zeros((MW, C), BF16)], axis=0
    )
    out_ref[...] = rows.T


def turn(before, own, after):
    return pl.pallas_call(
        turn_kernel,
        out_shape=jax.ShapeDtypeStruct((C, REACHED), BF16),
        in_specs=[vmem()] * 3,
        out_specs=vmem(),
        compiler_params=pltpu.CompilerParams(vmem_limit_bytes=8 << 20),
        name="turn",
        cost_estimate=cost(TR * MW * C, 2 << 20),
    )(before, own, after)


def shifts(rows):
    count = rows.shape[0]
    column = iota((count, C), 0) % MW
    return (
        jnp.where(column == MW - 1, 0.0, pltpu.roll(rows, count - 1, 0)).astype(BF16),
        rows.astype(BF16),
        jnp.where(column == 0, 0.0, pltpu.roll(rows, 1, 0)).astype(BF16),
    )


def filter_kernel(
    got_ref, turned_ref, part_ref, own_ref, above_ref, below_ref,
    rows_ref, cols_ref, left_ref, shifted_ref,
):
    weights_of(got_ref, rows_ref, cols_ref)
    shifted_ref[:, : 2 * MW] = jnp.zeros((3, 2 * MW, C), BF16)
    shifted_ref[:, (2 + EXT) * MW :] = jnp.zeros((3, 3 * MW, C), BF16)
    for start, count in ((0, 8), (8, 8), (16, 8), (24, 5)):
        part = rows_of(start, count, got_ref, rows_ref, cols_ref, left_ref)
        for e, moved in enumerate(shifts(part)):
            shifted_ref[e, (2 + start) * MW : (2 + start + count) * MW] = moved
        if start < TR:
            own_ref[start * MW : (start + count) * MW] = part
        if start == 0:
            below_ref[...] = part[:MW].astype(BF16)
        if start == 8:
            above_ref[:MW] = part[7 * MW :].astype(BF16)
        if start == 16:
            own_ref[TR * MW :] = part[:MW]
            above_ref[MW : 9 * MW] = part.astype(BF16)
        if start == 24:
            above_ref[9 * MW :] = part.astype(BF16)
    for a in range(3):
        for e in range(3):
            part = jnp.dot(
                turned_ref[...],
                shifted_ref[e, (2 - a) * MW : (2 - a) * MW + REACHED],
                preferred_element_type=F32,
            )
            at = (a * 3 + e) * CIN
            part_ref[:, at : at + CIN, :] = part.reshape(TILES, CIN, C).astype(BF16)


def filter_part(got, turned):
    return pl.pallas_call(
        filter_kernel,
        out_shape=(
            jax.ShapeDtypeStruct((TILES, NPART, C), BF16),
            jax.ShapeDtypeStruct(((TR + 1) * MW, C), F32),
            jax.ShapeDtypeStruct((REACH * MW, C), BF16),
            jax.ShapeDtypeStruct((MW, C), BF16),
        ),
        in_specs=[vmem()] * 2,
        out_specs=(vmem(),) * 4,
        scratch_shapes=[
            pltpu.VMEM((32, KDIM), F32),
            pltpu.VMEM((MW, KDIM), BF16),
            pltpu.VMEM((8 * MW, KDIM), BF16),
            pltpu.VMEM((3, (EXT + 5) * MW, C), BF16),
        ],
        compiler_params=pltpu.CompilerParams(vmem_limit_bytes=30 << 20),
        name="filter",
        cost_estimate=cost(2 * EXT * MW * KDIM * C + 18 * REACHED * C * C, 4 << 20),
    )(got, turned)


def input_kernel(own_ref, above_ref, below_ref, weight_ref, out_ref, shifted_ref):
    whole = jnp.concatenate(
        [
            above_ref[:MW].astype(F32),
            own_ref[: (REACH - 1) * MW] + above_ref[MW:].astype(F32),
            own_ref[(REACH - 1) * MW : TR * MW],
            own_ref[TR * MW :] + below_ref[...].astype(F32),
        ],
        axis=0,
    )
    for e, moved in enumerate(shifts(whole)):
        shifted_ref[e] = moved
    total = jnp.zeros((TR * MW, C), F32)
    for a in range(3):
        for e in range(3):
            total = total + lax.dot_general(
                shifted_ref[e, (2 - a) * MW : (2 - a + TR) * MW],
                weight_ref[a * 3 + e],
                (((1,), (1,)), ((), ())),
                preferred_element_type=F32,
            )
    out_ref[...] = total.astype(BF16)


def input_part(own, above, below, weight):
    return pl.pallas_call(
        input_kernel,
        out_shape=jax.ShapeDtypeStruct((TR * MW, C), BF16),
        in_specs=[vmem()] * 4,
        out_specs=vmem(),
        scratch_shapes=[pltpu.VMEM((3, (TR + 2) * MW, C), BF16)],
        compiler_params=pltpu.CompilerParams(vmem_limit_bytes=16 << 20),
        name="input",
        cost_estimate=cost(18 * TR * MW * C * C, 4 << 20),
    )(own, above, below, weight)


def sum_kernel(scale, parts_ref, out_ref):
    total = parts_ref[0].astype(F32)
    for i in range(1, parts_ref.shape[0]):
        total = total + parts_ref[i].astype(F32)
    out_ref[...] = jnp.broadcast_to((total * scale).astype(out_ref.dtype), out_ref.shape)


def sum_parts(parts, shape, dtype, scale=1.0):
    return pl.pallas_call(
        functools.partial(sum_kernel, scale),
        out_shape=jax.ShapeDtypeStruct(shape, dtype),
        in_specs=[vmem()],
        out_specs=vmem(),
        compiler_params=pltpu.CompilerParams(vmem_limit_bytes=4 << 20),
        name="sum",
        cost_estimate=cost(parts.size, parts.size * 2),
    )(parts)


def exchange(parts, axis):
    return lax.all_to_all(parts, axis, split_axis=0, concat_axis=0, tiled=True)


def body(features, weight, pool_grad, hard_index, boxes):
    grads = pool_grad[0].transpose(1, 2, 0, 3).reshape(CELLS, ROI_DEV, C)
    send = dispatch(hard_index, boxes[0].T, grads)
    up = [(t, t + 1) for t in range(TILES - 1)]
    down = [(b, a) for a, b in up]
    feature_rows = features[0].reshape(TR * MW, C)
    before = lax.ppermute(feature_rows[(TR - 1) * MW :], "tile", up)
    after = lax.ppermute(feature_rows[: REACH * MW], "tile", down)
    got = exchange(send, "tile")
    turned = turn(before, feature_rows, after)
    part, own, above, below = filter_part(got, turned)
    parts = exchange(part, "tile")
    above = lax.ppermute(above, "tile", up)
    below = lax.ppermute(below, "tile", down)
    x_grad = input_part(own, above, below, weight.reshape(9, C, C)).reshape(1, TR, MW, C)
    parts = exchange(sum_parts(parts, (4, NPART, C), BF16), "zl")
    parts = exchange(sum_parts(parts, (4, NPART, C), BF16), "zh")
    total = sum_parts(parts, (NPART, C), F32, 1.0 / IMAGES)
    total = total.reshape(9, CIN, C).transpose(1, 0, 2).reshape(CIN, 3, 3, C)
    return x_grad, total


def solution(mesh):
    split = Mesh(mesh.devices.reshape(4, 4, TILES), ("zh", "zl", "tile"))
    images = ("zh", "zl")
    return jax.shard_map(
        body,
        mesh=split,
        in_specs=(
            P(images, "tile", None, None),
            P(),
            P(images, "tile", None, None, None),
            P(images, "tile"),
            P(images, None, None),
        ),
        out_specs=(P(images, "tile", None, None), P("tile", None, None, None)),
        check_vma=False,
    )
```

time: 144 us -> 113 us (0.78)
  blocking collectives: 85.2 us -> 26.9 us
  waiting for transfers between devices: 13.7 us -> 34.3 us
  starting transfers between devices: 18.7 us -> 33.3 us
  Pallas kernels: 20 us -> 15.8 us
  local copies, waits for them, and re-layouts: 4.56 us -> 1.3 us
    all_to_all x2 -> x1, blocking collectives: 85.2 us -> 26.9 us  [exchange(): return lax.all_to_all(parts, axis, split_axis=0, concat_axis=0, tiled=True)]
    all_to_all x1 -> x3, waiting for transfers between devices: 11.7 us -> 31.7 us  [exchange(): return lax.all_to_all(parts, axis, split_axis=0, concat_axis=0, tiled=True)]
    all_to_all x1 -> x3, starting transfers between devices: 14.8 us -> 26.2 us  [exchange(): return lax.all_to_all(parts, axis, split_axis=0, concat_axis=0, tiled=True)]
    pallas_call x1 -> x4, Pallas kernels: 7.29 us -> 2.52 us  [the longest x3 2.19 us: sum_parts(): pl.pallas_call(functools.partial(sum_kernel, scale), out_shape=jax.ShapeD...]
    ppermute x1 -> x3, starting transfers between devices: 1.29 us -> 5.6 us  [the longest x1 3.03 us: body(): before = lax.ppermute(feature_rows[(TR - 1) * MW:], 'tile', up)]
    pallas_call x1, Pallas kernels: 4.14 us -> 6.82 us  [filter_part(): pl.pallas_call(filter_kernel, out_shape=(jax.ShapeDtypeStruct((TILES, NPA...]
    pallas_call x1, Pallas kernels: 4.01 us -> 2.23 us  [input_part(): pl.pallas_call(input_kernel, out_shape=jax.ShapeDtypeStruct((TR * MW, C),...]
    pallas_call x1 -> x0, local copies, waits for them, and re-layouts: 1.54 us -> none  [filter_part(): pl.pallas_call(filter_kernel, out_shape=(jax.ShapeDtypeStruct((TILES, NPA...]
  transfers between devices with their start and end apart: 3 -> 7, of which waited for: 2 -> 5; matrix products, arithmetic and copies ran while one was open for 0% -> 0% of each run, Pallas kernels for 3% -> 3%
where the time goes in v2:
time: 113 us; the launch traced here: 112 us
  waiting for transfers between devices  34.3 us (30%)
  starting transfers between devices  33.3 us (29%)
  blocking collectives  26.9 us (24%)
  Pallas kernels  15.8 us (14%)
  local copies, waits for them, and re-layouts  1.3 us (1%)
    all_to_all x3, waiting for transfers between devices, exchange(): return lax.all_to_all(parts, axis, split_axis=0, concat_axis=0, tiled=True)  31.7 us
    all_to_all x1, blocking collectives, exchange(): return lax.all_to_all(parts, axis, split_axis=0, concat_axis=0, tiled=True)  26.9 us
    all_to_all x3, starting transfers between devices, exchange(): return lax.all_to_all(parts, axis, split_axis=0, concat_axis=0, tiled=True)  26.2 us
    pallas_call x1, Pallas kernels, filter_part(): pl.pallas_call(filter_kernel, out_shape=(jax.ShapeDtypeStruct((TILES, NPA...  6.82 us
    pallas_call x1, Pallas kernels, dispatch(): pl.pallas_call(dispatch_kernel, out_shape=jax.ShapeDtypeStruct((TILES, BL...  4.21 us
    ppermute x1, starting transfers between devices, body(): before = lax.ppermute(feature_rows[(TR - 1) * MW:], 'tile', up)  3.03 us
  transfers between devices with their start and end apart: 7, of which 5 were waited for; matrix products, arithmetic and copies ran while one was open for 0% of the time, Pallas kernels for 3%

profile of v2, /device:TPU:32, one launch (start us, length us, event | category | flops | bytes accessed | tf_op | source)
XLA Modules:
  0.0 112.4 jit_solution(14324554168365590732)
XLA Ops:
  0.6 4.2 %dispatch.1 = bf16[32,104,256]{2,1,0:T(8,128)(2,1)} custom-call(s32[1,16]{1,0:T(1,128)} %index_hbm.1, s32[4,20000]{1,0:T(4,128)} %bitcast.24, bf16[49,16,256]{2,1,0:T(8,128)(2,1)} %bitcast.23), custom_call_target="tpu_custom_call" | custom-call | flops 1363148800 | bytes 3145728 | tf_op jit(solution)/shard_map/dispatch/pallas_call | solution.py:118
  4.9 0.0 copy-start
  4.9 7.5 %all-to-all-start = ((bf16[32,104,256]{2,1,0:T(8,128)(2,1)}), bf16[32,104,256]{2,1,0:T(8,128)(2,1)S(1)}, u32[]{:S(2)}, u32[]{:S(2)}) async-start(bf16[32,104,256]{2,1,0:T(8,128)(2,1)} %dispatch.1), calls=%async_computation | async-start | bytes 3407872 | tf_op jit(solution)/shard_map/all_to_all | solution.py:311
  12.4 1.3 %collective-permute-start.1 = (bf16[896,256]{1,0:T(8,128)(2,1)S(1)}, bf16[896,256]{1,0:T(8,128)(2,1)S(1)}, u32[]{:S(2)}, u32[]{:S(2)}) collective-permute-start(bf16[896,256]{1,0:T(8,128)(2,1)S(1)} %bitcast.21), channel_id=1, source_target_pairs={{1,0},{2,1},{3,2},{4,3},{5,4},{6,5},{7,6},{8,7},{9,8},{10,9},{11,1... | collective-permute-start | bytes 1376264 | tf_op jit(solution)/shard_map/ppermute | solution.py:321
  13.7 3.0 %collective-permute-start = (bf16[64,256]{1,0:T(8,128)(2,1)S(1)}, bf16[64,256]{1,0:T(8,128)(2,1)S(1)}, u32[]{:S(2)}, u32[]{:S(2)}) collective-permute-start(bf16[64,256]{1,0:T(8,128)(2,1)S(1)} %slice_bitcast_fusion), channel_id=1, source_target_pairs={{0,1},{1,2},{2,3},{3,4},{4,5},{5,6},{6,7},{7,8},{8,9},{9,10},{10,1... | collective-permute-start | bytes 98312 | tf_op jit(solution)/shard_map/ppermute | solution.py:320
  16.7 0.8 collective-permute-done.before_ref
  17.6 0.0 collective-permute-done.1.after_ref
  17.6 0.3 turn.1.turned_ref
  17.9 19.0 %all-to-all-done.got_ref = bf16[32,104,256]{2,1,0:T(8,128)(2,1)S(1)} async-done(((bf16[32,104,256]{2,1,0:T(8,128)(2,1)}), bf16[32,104,256]{2,1,0:T(8,128)(2,1)S(1)}, u32[]{:S(2)}, u32[]{:S(2)}) %all-to-all-start) | async-done | bytes 1703968 | tf_op jit(solution)/shard_map/all_to_all | solution.py:311
  36.9 6.8 %filter.1 = (bf16[32,72,256]{2,1,0:T(8,128)(2,1)S(1)}, f32[1088,256]{1,0:T(8,128)S(1)}, bf16[896,256]{1,0:T(8,128)(2,1)S(1)}, bf16[64,256]{1,0:T(8,128)(2,1)S(1)}) custom-call(bf16[32,104,256]{2,1,0:T(8,128)(2,1)S(1)} %all-to-all-done.got_ref, bf16[256,2048]{1,0:T(8,128)(2,1)S(1)} %turn.1.turned_ref), custom_call_target="tpu_custom_call" | custom-call | flops 5578424320 | bytes 4194304 | tf_op jit(solution)/shard_map/filter/pallas_call | solution.py:232
  43.7 0.0 copy-start.2
  43.8 26.9 %all_to_all.20.parts_ref = bf16[32,72,256]{2,1,0:T(8,128)(2,1)S(1)} all-to-all(bf16[32,72,256]{2,1,0:T(8,128)(2,1)S(1)} %get-tuple-element.9), channel_id=1, replica_groups=mesh['zh'=4,'zl'=4,'tile'=32] {'tile'}, dimensions={0} | all-to-all | bytes 2359296 | tf_op jit(solution)/shard_map/all_to_all | solution.py:311
  70.7 0.8 sum.3
  71.5 6.0 %all-to-all-start.2 = ((bf16[4,72,256]{2,1,0:T(8,128)(2,1)}), bf16[4,72,256]{2,1,0:T(8,128)(2,1)S(1)}, u32[]{:S(2)}, u32[]{:S(2)}) async-start(bf16[4,72,256]{2,1,0:T(8,128)(2,1)} %sum.3), calls=%async_computation.2 | async-start | bytes 294912 | tf_op jit(solution)/shard_map/all_to_all | solution.py:311
  77.5 1.5 %collective-permute-start.2 = (bf16[896,256]{1,0:T(8,128)(2,1)}, bf16[896,256]{1,0:T(8,128)(2,1)S(1)}, u32[]{:S(2)}, u32[]{:S(2)}) collective-permute-start(bf16[896,256]{1,0:T(8,128)(2,1)} %copy-done.2), channel_id=1, source_target_pairs={{0,1},{1,2},{2,3},{3,4},{4,5},{5,6},{6,7},{7,8},{8,9},{9,10},{10,1... | collective-permute-start | bytes 1376264 | tf_op jit(solution)/shard_map/ppermute | solution.py:326
  79.0 3.9 %all-to-all-done.2.parts_ref = bf16[4,72,256]{2,1,0:T(8,128)(2,1)S(1)} async-done(((bf16[4,72,256]{2,1,0:T(8,128)(2,1)}), bf16[4,72,256]{2,1,0:T(8,128)(2,1)S(1)}, u32[]{:S(2)}, u32[]{:S(2)}) %all-to-all-start.2) | async-done | bytes 147488 | tf_op jit(solution)/shard_map/all_to_all | solution.py:311
  82.9 0.7 sum.4
  83.5 12.8 %all-to-all-start.3 = ((bf16[4,72,256]{2,1,0:T(8,128)(2,1)}), bf16[4,72,256]{2,1,0:T(8,128)(2,1)S(1)}, u32[]{:S(2)}, u32[]{:S(2)}) async-start(bf16[4,72,256]{2,1,0:T(8,128)(2,1)} %sum.4), calls=%async_computation.3 | async-start | bytes 294912 | tf_op jit(solution)/shard_map/all_to_all | solution.py:311
  96.3 1.3 %collective-permute-start.3 = (bf16[64,256]{1,0:T(8,128)(2,1)S(1)}, bf16[64,256]{1,0:T(8,128)(2,1)S(1)}, u32[]{:S(2)}, u32[]{:S(2)}) collective-permute-start(bf16[64,256]{1,0:T(8,128)(2,1)S(1)} %get-tuple-element.8), channel_id=1, source_target_pairs={{1,0},{2,1},{3,2},{4,3},{5,4},{6,5},{7,6},{8,7},{9,8},{10,9},{11,1... | collective-permute-start | bytes 98312 | tf_op jit(solution)/shard_map/ppermute | solution.py:327
  97.6 1.8 %collective-permute-done.3.below_ref = bf16[64,256]{1,0:T(8,128)(2,1)S(1)} collective-permute-done((bf16[64,256]{1,0:T(8,128)(2,1)S(1)}, bf16[64,256]{1,0:T(8,128)(2,1)S(1)}, u32[]{:S(2)}, u32[]{:S(2)}) %collective-permute-start.3) | collective-permute-done | bytes 32800 | tf_op jit(solution)/shard_map/ppermute | solution.py:327
  99.4 1.2 %copy-done.4 = f32[1088,256]{1,0:T(8,128)S(1)} copy-done((f32[1088,256]{1,0:T(8,128)S(1)}, f32[1088,256]{1,0:T(8,128)}, u32[]{:S(2)}) %copy-start.4) | copy-done | bytes 1114136
  100.7 2.2 %input.1 = bf16[1024,256]{1,0:T(8,128)(2,1)} custom-call(f32[1088,256]{1,0:T(8,128)S(1)} %copy-done.4, bf16[896,256]{1,0:T(8,128)(2,1)S(1)} %collective-permute-done.2.above_ref, bf16[64,256]{1,0:T(8,128)(2,1)S(1)} %collective-permute-done.3.below_ref, bf16[9,256,256]{2,1,0:T(8,128)(2,1)S(1)} %bitcast.20), custom_call_target="tpu_custom_call" | custom-call | flops 1207959552 | bytes 4194304 | tf_op jit(solution)/shard_map/input/pallas_call | solution.py:279
  102.9 8.8 %all-to-all-done.3.parts_ref = bf16[4,72,256]{2,1,0:T(8,128)(2,1)S(1)} async-done(((bf16[4,72,256]{2,1,0:T(8,128)(2,1)}), bf16[4,72,256]{2,1,0:T(8,128)(2,1)S(1)}, u32[]{:S(2)}, u32[]{:S(2)}) %all-to-all-start.3) | async-done | bytes 147488 | tf_op jit(solution)/shard_map/all_to_all | solution.py:311
  111.8 0.7 sum.5
  (10 shorter events, 0.1 us)
Async XLA Ops:
  4.9 7.5 %copy-start = (bf16[1,16,64,256]{3,2,1,0:T(8,128)(2,1)S(1)}, bf16[1,16,64,256]{3,2,1,0:T(8,128)(2,1)}, u32[]{:S(2)}) copy-start(bf16[1,16,64,256]{3,2,1,0:T(8,128)(2,1)} %param.5) | copy-start | bytes 1572868
  4.9 32.0 %all-to-all-start = ((bf16[32,104,256]{2,1,0:T(8,128)(2,1)}), bf16[32,104,256]{2,1,0:T(8,128)(2,1)S(1)}, u32[]{:S(2)}, u32[]{:S(2)}) async-start(bf16[32,104,256]{2,1,0:T(8,128)(2,1)} %dispatch.1), calls=%async_computation | async-start | bytes 3407872 | tf_op jit(solution)/shard_map/all_to_all | solution.py:311
  12.4 5.2 %collective-permute-start.1 = (bf16[896,256]{1,0:T(8,128)(2,1)S(1)}, bf16[896,256]{1,0:T(8,128)(2,1)S(1)}, u32[]{:S(2)}, u32[]{:S(2)}) collective-permute-start(bf16[896,256]{1,0:T(8,128)(2,1)S(1)} %bitcast.21), channel_id=1, source_target_pairs={{1,0},{2,1},{3,2},{4,3},{5,4},{6,5},{7,6},{8,7},{9,8},{10,9},{11,1... | collective-permute-start | bytes 1376264 | tf_op jit(solution)/shard_map/ppermute | solution.py:321
  13.7 3.9 %collective-permute-start = (bf16[64,256]{1,0:T(8,128)(2,1)S(1)}, bf16[64,256]{1,0:T(8,128)(2,1)S(1)}, u32[]{:S(2)}, u32[]{:S(2)}) collective-permute-start(bf16[64,256]{1,0:T(8,128)(2,1)S(1)} %slice_bitcast_fusion), channel_id=1, source_target_pairs={{0,1},{1,2},{2,3},{3,4},{4,5},{5,6},{6,7},{7,8},{8,9},{9,10},{10,1... | collective-permute-start | bytes 98312 | tf_op jit(solution)/shard_map/ppermute | solution.py:320
  43.7 26.9 %copy-start.2 = (bf16[896,256]{1,0:T(8,128)(2,1)}, bf16[896,256]{1,0:T(8,128)(2,1)S(1)}, u32[]{:S(2)}) copy-start(bf16[896,256]{1,0:T(8,128)(2,1)S(1)} %get-tuple-element.7) | copy-start | bytes 1376260
  43.8 26.9 %copy-start.3 = (f32[1088,256]{1,0:T(8,128)}, f32[1088,256]{1,0:T(8,128)S(1)}, u32[]{:S(2)}) copy-start(f32[1088,256]{1,0:T(8,128)S(1)} %get-tuple-element.6.own_ref) | copy-start | bytes 3342340
  70.7 28.8 %copy-start.1 = (bf16[3,3,256,256]{3,2,1,0:T(8,128)(2,1)S(1)}, bf16[3,3,256,256]{3,2,1,0:T(8,128)(2,1)}, u32[]{:S(2)}) copy-start(bf16[3,3,256,256]{3,2,1,0:T(8,128)(2,1)} %param.6) | copy-start | bytes 3538948
  71.5 11.3 %all-to-all-start.2 = ((bf16[4,72,256]{2,1,0:T(8,128)(2,1)}), bf16[4,72,256]{2,1,0:T(8,128)(2,1)S(1)}, u32[]{:S(2)}, u32[]{:S(2)}) async-start(bf16[4,72,256]{2,1,0:T(8,128)(2,1)} %sum.3), calls=%async_computation.2 | async-start | bytes 294912 | tf_op jit(solution)/shard_map/all_to_all | solution.py:311
  77.5 21.9 %collective-permute-start.2 = (bf16[896,256]{1,0:T(8,128)(2,1)}, bf16[896,256]{1,0:T(8,128)(2,1)S(1)}, u32[]{:S(2)}, u32[]{:S(2)}) collective-permute-start(bf16[896,256]{1,0:T(8,128)(2,1)} %copy-done.2), channel_id=1, source_target_pairs={{0,1},{1,2},{2,3},{3,4},{4,5},{5,6},{6,7},{7,8},{8,9},{9,10},{10,1... | collective-permute-start | bytes 1376264 | tf_op jit(solution)/shard_map/ppermute | solution.py:326
  83.5 28.2 %all-to-all-start.3 = ((bf16[4,72,256]{2,1,0:T(8,128)(2,1)}), bf16[4,72,256]{2,1,0:T(8,128)(2,1)S(1)}, u32[]{:S(2)}, u32[]{:S(2)}) async-start(bf16[4,72,256]{2,1,0:T(8,128)(2,1)} %sum.4), calls=%async_computation.3 | async-start | bytes 294912 | tf_op jit(solution)/shard_map/all_to_all | solution.py:311
  96.3 3.1 %collective-permute-start.3 = (bf16[64,256]{1,0:T(8,128)(2,1)S(1)}, bf16[64,256]{1,0:T(8,128)(2,1)S(1)}, u32[]{:S(2)}, u32[]{:S(2)}) collective-permute-start(bf16[64,256]{1,0:T(8,128)(2,1)S(1)} %get-tuple-element.8), channel_id=1, source_target_pairs={{1,0},{2,1},{3,2},{4,3},{5,4},{6,5},{7,6},{8,7},{9,8},{10,9},{11,1... | collective-permute-start | bytes 98312 | tf_op jit(solution)/shard_map/ppermute | solution.py:327
  99.4 1.2 %copy-start.4 = (f32[1088,256]{1,0:T(8,128)S(1)}, f32[1088,256]{1,0:T(8,128)}, u32[]{:S(2)}) copy-start(f32[1088,256]{1,0:T(8,128)} %copy-done.3) | copy-start | bytes 3342340

commit v3 on v2

--- a/solution.py
+++ b/solution.py
@@ -17,6 +17,7 @@
 CELLS = BINS * BINS
 PROPS = 20000
 TILES = 32
+CHIPS = TILES // 2
 IMAGES = 16
 EXT = TR + REACH - 1
 REACHED = 32 * MW
@@ -30,6 +31,7 @@
 BF16 = jnp.bfloat16
 I32 = jnp.int32
 CIN = C // TILES
+TILE_AXES = ("chip", "core")
 NPART = 9 * CIN
 
 
@@ -196,7 +198,7 @@
 
 
 def filter_kernel(
-    got_ref, turned_ref, part_ref, own_ref, above_ref, below_ref,
+    core_ref, got_ref, turned_ref, keep_ref, give_ref, own_ref, above_ref, below_ref,
     rows_ref, cols_ref, left_ref, shifted_ref,
 ):
     weights_of(got_ref, rows_ref, cols_ref)
@@ -217,6 +219,7 @@
             above_ref[MW : 9 * MW] = part.astype(BF16)
         if start == 24:
             above_ref[9 * MW :] = part.astype(BF16)
+    first = core_ref[0] == 0
     for a in range(3):
         for e in range(3):
             part = jnp.dot(
@@ -224,21 +227,24 @@
                 shifted_ref[e, (2 - a) * MW : (2 - a) * MW + REACHED],
                 preferred_element_type=F32,
             )
+            part = part.reshape(CHIPS, 2, CIN, C)
             at = (a * 3 + e) * CIN
-            part_ref[:, at : at + CIN, :] = part.reshape(TILES, CIN, C).astype(BF16)
-
-
-def filter_part(got, turned):
+            keep_ref[:, at : at + CIN, :] = jnp.where(first, part[:, 0], part[:, 1])
+            give_ref[:, at : at + CIN, :] = jnp.where(first, part[:, 1], part[:, 0]).astype(BF16)
+
+
+def filter_part(core, got, turned):
     return pl.pallas_call(
         filter_kernel,
         out_shape=(
-            jax.ShapeDtypeStruct((TILES, NPART, C), BF16),
+            jax.ShapeDtypeStruct((CHIPS, NPART, C), F32),
+            jax.ShapeDtypeStruct((CHIPS, NPART, C), BF16),
             jax.ShapeDtypeStruct(((TR + 1) * MW, C), F32),
             jax.ShapeDtypeStruct((REACH * MW, C), BF16),
             jax.ShapeDtypeStruct((MW, C), BF16),
         ),
-        in_specs=[vmem()] * 2,
-        out_specs=(vmem(),) * 4,
+        in_specs=[pl.BlockSpec(memory_space=pltpu.SMEM), vmem(), vmem()],
+        out_specs=(vmem(),) * 5,
         scratch_shapes=[
             pltpu.VMEM((32, KDIM), F32),
             pltpu.VMEM((MW, KDIM), BF16),
@@ -248,7 +254,7 @@
         compiler_params=pltpu.CompilerParams(vmem_limit_bytes=30 << 20),
         name="filter",
         cost_estimate=cost(2 * EXT * MW * KDIM * C + 18 * REACHED * C * C, 4 << 20),
-    )(got, turned)
+    )(core, got, turned)
 
 
 def input_kernel(own_ref, above_ref, below_ref, weight_ref, out_ref, shifted_ref):
@@ -307,6 +313,22 @@
     )(parts)
 
 
+def pair_kernel(keep_ref, got_ref, out_ref):
+    out_ref[...] = (keep_ref[...] + got_ref[...].astype(F32)).astype(BF16)
+
+
+def sum_pair(keep, got):
+    return pl.pallas_call(
+        pair_kernel,
+        out_shape=jax.ShapeDtypeStruct(keep.shape, BF16),
+        in_specs=[vmem()] * 2,
+        out_specs=vmem(),
+        compiler_params=pltpu.CompilerParams(vmem_limit_bytes=4 << 20),
+        name="pair",
+        cost_estimate=cost(keep.size, keep.size * 8),
+    )(keep, got)
+
+
 def exchange(parts, axis):
     return lax.all_to_all(parts, axis, split_axis=0, concat_axis=0, tiled=True)
 
@@ -317,35 +339,40 @@
     up = [(t, t + 1) for t in range(TILES - 1)]
     down = [(b, a) for a, b in up]
     feature_rows = features[0].reshape(TR * MW, C)
-    before = lax.ppermute(feature_rows[(TR - 1) * MW :], "tile", up)
-    after = lax.ppermute(feature_rows[: REACH * MW], "tile", down)
-    got = exchange(send, "tile")
+    before = lax.ppermute(feature_rows[(TR - 1) * MW :], TILE_AXES, up)
+    after = lax.ppermute(feature_rows[: REACH * MW], TILE_AXES, down)
+    got = exchange(send, TILE_AXES)
     turned = turn(before, feature_rows, after)
-    part, own, above, below = filter_part(got, turned)
-    parts = exchange(part, "tile")
-    above = lax.ppermute(above, "tile", up)
-    below = lax.ppermute(below, "tile", down)
+    core = lax.axis_index("core").reshape(1)
+    keep, give, own, above, below = filter_part(core, got, turned)
+    taken = lax.ppermute(give, "core", [(0, 1), (1, 0)])
+    parts = exchange(sum_pair(keep, taken), "chip")
+    above = lax.ppermute(above, TILE_AXES, up)
+    below = lax.ppermute(below, TILE_AXES, down)
     x_grad = input_part(own, above, below, weight.reshape(9, C, C)).reshape(1, TR, MW, C)
     parts = exchange(sum_parts(parts, (4, NPART, C), BF16), "zl")
-    parts = exchange(sum_parts(parts, (4, NPART, C), BF16), "zh")
+    parts = sum_parts(parts, (1, NPART, C), BF16)
+    parts = lax.all_gather(parts, "zh", tiled=True, axis_index_groups=[[0, 1], [2, 3]])
+    parts = sum_parts(parts, (1, NPART, C), BF16)
+    parts = lax.all_gather(parts, "zh", tiled=True, axis_index_groups=[[0, 3], [1, 2]])
     total = sum_parts(parts, (NPART, C), F32, 1.0 / IMAGES)
     total = total.reshape(9, CIN, C).transpose(1, 0, 2).reshape(CIN, 3, 3, C)
     return x_grad, total
 
 
 def solution(mesh):
-    split = Mesh(mesh.devices.reshape(4, 4, TILES), ("zh", "zl", "tile"))
+    split = Mesh(mesh.devices.reshape(4, 4, CHIPS, 2), ("zh", "zl", "chip", "core"))
     images = ("zh", "zl")
     return jax.shard_map(
         body,
         mesh=split,
         in_specs=(
-            P(images, "tile", None, None),
+            P(images, TILE_AXES, None, None),
             P(),
-            P(images, "tile", None, None, None),
-            P(images, "tile"),
+            P(images, TILE_AXES, None, None, None),
+            P(images, TILE_AXES),
             P(images, None, None),
         ),
-        out_specs=(P(images, "tile", None, None), P("tile", None, None, None)),
+        out_specs=(P(images, TILE_AXES, None, None), P(TILE_AXES, None, None, None)),
         check_vma=False,
     )

time: 113 us -> 106 us (0.938)
  the two profiles are of different devices: /device:TPU:32 before, /device:TPU:34 now
where the time goes in v3:
time: 106 us
  blocking collectives  37.4 us (35%)
  starting transfers between devices  30.8 us (29%)
  waiting for transfers between devices  19.8 us (19%)
  Pallas kernels  15.2 us (14%)
  local copies, waits for them, and re-layouts  1.85 us (2%)
    all_to_all x1, blocking collectives, exchange(): return lax.all_to_all(parts, axis, split_axis=0, concat_axis=0, tiled=True)  18 us
    ppermute x1, waiting for transfers between devices, body(): before = lax.ppermute(feature_rows[(TR - 1) * MW:], TILE_AXES, up)  16.3 us
    all_to_all x2, starting transfers between devices, exchange(): return lax.all_to_all(parts, axis, split_axis=0, concat_axis=0, tiled=True)  13.8 us
    all_gather x1, blocking collectives, body(): lax.all_gather(parts, 'zh', tiled=True, axis_index_groups=[[0, 1], [2, 3]])  9.78 us
    all_gather x1, blocking collectives, body(): lax.all_gather(parts, 'zh', tiled=True, axis_index_groups=[[0, 3], [1, 2]])  9.67 us
    pallas_call x1, Pallas kernels, filter_part(): pl.pallas_call(filter_kernel, out_shape=(jax.ShapeDtypeStruct((CHIPS, NPA...  6.86 us
    ppermute x1, starting transfers between devices, body(): below = lax.ppermute(below, TILE_AXES, down)  5.75 us
    ppermute x1, starting transfers between devices, body(): after = lax.ppermute(feature_rows[:REACH * MW], TILE_AXES, down)  4.33 us
  transfers between devices with their start and end apart: 7, of which 3 were waited for; matrix products, arithmetic and copies ran while one was open for 0% of the time, Pallas kernels for 0%

profile of v3, /device:TPU:34, one launch (start us, length us, event | category | flops | bytes accessed | tf_op | source)
XLA Modules:
  0.0 105.9 jit_solution(9909950694936934581)
XLA Ops:
  0.6 4.2 %dispatch.1 = bf16[32,104,256]{2,1,0:T(8,128)(2,1)} custom-call(s32[1,16]{1,0:T(1,128)} %index_hbm.1, s32[4,20000]{1,0:T(4,128)} %bitcast.25, bf16[49,16,256]{2,1,0:T(8,128)(2,1)} %bitcast.24), custom_call_target="tpu_custom_call" | custom-call | flops 1363148800 | bytes 3145728 | tf_op jit(solution)/shard_map/dispatch/pallas_call | solution.py:120
  4.9 0.0 copy-start
  4.9 7.8 %all-to-all-start = ((bf16[32,104,256]{2,1,0:T(8,128)(2,1)}), bf16[32,104,256]{2,1,0:T(8,128)(2,1)S(1)}, u32[]{:S(2)}, u32[]{:S(2)}) async-start(bf16[32,104,256]{2,1,0:T(8,128)(2,1)} %dispatch.1), calls=%async_computation | async-start | bytes 3407872 | tf_op jit(solution)/shard_map/all_to_all | solution.py:333
  12.7 4.3 %collective-permute-start.1 = (bf16[896,256]{1,0:T(8,128)(2,1)S(1)}, bf16[896,256]{1,0:T(8,128)(2,1)S(1)}, u32[]{:S(2)}, u32[]{:S(2)}) collective-permute-start(bf16[896,256]{1,0:T(8,128)(2,1)S(1)} %bitcast.22), channel_id=1, source_target_pairs={{1,0},{2,1},{3,2},{4,3},{5,4},{6,5},{7,6},{8,7},{9,8},{10,9},{11,1... | collective-permute-start | bytes 1376264 | tf_op jit(solution)/shard_map/ppermute | solution.py:343
  17.0 1.9 %collective-permute-start = (bf16[64,256]{1,0:T(8,128)(2,1)S(1)}, bf16[64,256]{1,0:T(8,128)(2,1)S(1)}, u32[]{:S(2)}, u32[]{:S(2)}) collective-permute-start(bf16[64,256]{1,0:T(8,128)(2,1)S(1)} %slice_bitcast_fusion), channel_id=1, source_target_pairs={{0,1},{1,2},{2,3},{3,4},{4,5},{5,6},{6,7},{7,8},{8,9},{9,10},{10,1... | collective-permute-start | bytes 98312 | tf_op jit(solution)/shard_map/ppermute | solution.py:342
  19.0 16.3 %collective-permute-done.before_ref = bf16[64,256]{1,0:T(8,128)(2,1)S(1)} collective-permute-done((bf16[64,256]{1,0:T(8,128)(2,1)S(1)}, bf16[64,256]{1,0:T(8,128)(2,1)S(1)}, u32[]{:S(2)}, u32[]{:S(2)}) %collective-permute-start) | collective-permute-done | bytes 32800 | tf_op jit(solution)/shard_map/ppermute | solution.py:342
  35.2 1.9 %collective-permute-done.1.after_ref = bf16[896,256]{1,0:T(8,128)(2,1)S(1)} collective-permute-done((bf16[896,256]{1,0:T(8,128)(2,1)S(1)}, bf16[896,256]{1,0:T(8,128)(2,1)S(1)}, u32[]{:S(2)}, u32[]{:S(2)}) %collective-permute-start.1) | collective-permute-done | bytes 458784 | tf_op jit(solution)/shard_map/ppermute | solution.py:343
  37.2 0.8 copy-done.1
  37.9 1.0 copy-done.2
  39.0 0.3 turn.1.turned_ref
  39.3 6.9 %filter.1 = (f32[16,72,256]{2,1,0:T(8,128)S(1)}, bf16[16,72,256]{2,1,0:T(8,128)(2,1)S(1)}, f32[1088,256]{1,0:T(8,128)S(1)}, bf16[896,256]{1,0:T(8,128)(2,1)S(1)}, bf16[64,256]{1,0:T(8,128)(2,1)S(1)}) custom-call(s32[1]{0:T(128)} %bitcast.core_ref, bf16[32,104,256]{2,1,0:T(8,128)(2,1)S(1)} %all-to-all-done.got_ref, bf16[256,2048]{1,0:T(8,128)(2,1)S(1)} %turn.1.turned_ref), custom_call_target="tpu_custom_call" | custom-call | flops 5578424320 | bytes 4194304 | tf_op jit(solution)/shard_map/filter/pallas_call | solution.py:237
  46.2 0.0 copy-start.4
  46.2 3.1 %collective-permute-start.4 = (bf16[16,72,256]{2,1,0:T(8,128)(2,1)S(1)}, bf16[16,72,256]{2,1,0:T(8,128)(2,1)S(1)}, u32[]{:S(2)}, u32[]{:S(2)}) collective-permute-start(bf16[16,72,256]{2,1,0:T(8,128)(2,1)S(1)} %get-tuple-element.11), channel_id=1, source_target_pairs={{0,1},{1,0},{2,3},{3,2},{4,5},{5,4},{6,7},{7,6},{8,9},{9,8},{10,11... | collective-permute-start | bytes 1769480 | tf_op jit(solution)/shard_map/ppermute | solution.py:348
  49.3 1.6 %collective-permute-done.4.got_ref = bf16[16,72,256]{2,1,0:T(8,128)(2,1)S(1)} collective-permute-done((bf16[16,72,256]{2,1,0:T(8,128)(2,1)S(1)}, bf16[16,72,256]{2,1,0:T(8,128)(2,1)S(1)}, u32[]{:S(2)}, u32[]{:S(2)}) %collective-permute-start.4) | collective-permute-done | bytes 589856 | tf_op jit(solution)/shard_map/ppermute | solution.py:348
  51.0 0.1 pair.1
  51.1 18.0 %all_to_all.15.parts_ref = bf16[16,72,256]{2,1,0:T(8,128)(2,1)S(1)} all-to-all(bf16[16,72,256]{2,1,0:T(8,128)(2,1)S(1)} %pair.1), channel_id=1, replica_groups=mesh['zh'=4,'zl'=4,'chip'=16,'core'=2] {'chip'}, dimensions={0} | all-to-all | bytes 1179648 | tf_op jit(solution)/shard_map/all_to_all | solution.py:333
  69.1 0.7 sum.4
  69.9 6.0 %all-to-all-start.2 = ((bf16[4,72,256]{2,1,0:T(8,128)(2,1)}), bf16[4,72,256]{2,1,0:T(8,128)(2,1)S(1)}, u32[]{:S(2)}, u32[]{:S(2)}) async-start(bf16[4,72,256]{2,1,0:T(8,128)(2,1)} %sum.4), calls=%async_computation.2 | async-start | bytes 294912 | tf_op jit(solution)/shard_map/all_to_all | solution.py:333
  75.9 1.9 %collective-permute-start.2 = (bf16[896,256]{1,0:T(8,128)(2,1)}, bf16[896,256]{1,0:T(8,128)(2,1)S(1)}, u32[]{:S(2)}, u32[]{:S(2)}) collective-permute-start(bf16[896,256]{1,0:T(8,128)(2,1)} %copy-done.4), channel_id=1, source_target_pairs={{0,1},{1,2},{2,3},{3,4},{4,5},{5,6},{6,7},{7,8},{8,9},{9,10},{10,1... | collective-permute-start | bytes 1376264 | tf_op jit(solution)/shard_map/ppermute | solution.py:350
  77.8 5.8 %collective-permute-start.3 = (bf16[64,256]{1,0:T(8,128)(2,1)S(1)}, bf16[64,256]{1,0:T(8,128)(2,1)S(1)}, u32[]{:S(2)}, u32[]{:S(2)}) collective-permute-start(bf16[64,256]{1,0:T(8,128)(2,1)S(1)} %get-tuple-element.9), channel_id=1, source_target_pairs={{1,0},{2,1},{3,2},{4,3},{5,4},{6,5},{7,6},{8,7},{9,8},{10,9},{11,1... | collective-permute-start | bytes 98312 | tf_op jit(solution)/shard_map/ppermute | solution.py:351
  83.6 9.8 %all_gather.6.parts_ref = bf16[2,72,256]{2,1,0:T(8,128)(2,1)S(1)} all-gather(bf16[1,72,256]{2,1,0:T(8,128)(2,1)S(1)} %sum.5), channel_id=1, replica_groups={{0,128},{256,384},{1,129},{257,385},{2,130},{258,386},{3,131},{259,387}..., dimensions={0}, use_global_device_ids=true | all-gather | bytes 110592 | tf_op jit(solution)/shard_map/all_gather | solution.py:355
  93.4 9.7 %all_gather.7.parts_ref = bf16[2,72,256]{2,1,0:T(8,128)(2,1)S(1)} all-gather(bf16[1,72,256]{2,1,0:T(8,128)(2,1)S(1)} %sum.6), channel_id=1, replica_groups={{0,384},{128,256},{1,385},{129,257},{2,386},{130,258},{3,387},{131,259}..., dimensions={0}, use_global_device_ids=true | all-gather | bytes 110592 | tf_op jit(solution)/shard_map/all_gather | solution.py:357
  103.1 2.2 %input.1 = bf16[1024,256]{1,0:T(8,128)(2,1)} custom-call(f32[1088,256]{1,0:T(8,128)S(1)} %copy-done.6, bf16[896,256]{1,0:T(8,128)(2,1)S(1)} %collective-permute-done.2.above_ref, bf16[64,256]{1,0:T(8,128)(2,1)S(1)} %collective-permute-done.3.below_ref, bf16[9,256,256]{2,1,0:T(8,128)(2,1)S(1)} %bitcast.21), custom_call_target="tpu_custom_call" | custom-call | flops 1207959552 | bytes 4194304 | tf_op jit(solution)/shard_map/input/pallas_call | solution.py:285
  105.3 0.6 sum.7
  (18 shorter events, 0.1 us)
Async XLA Ops:
  4.9 7.8 %copy-start = (bf16[1,16,64,256]{3,2,1,0:T(8,128)(2,1)S(1)}, bf16[1,16,64,256]{3,2,1,0:T(8,128)(2,1)}, u32[]{:S(2)}) copy-start(bf16[1,16,64,256]{3,2,1,0:T(8,128)(2,1)} %param.5) | copy-start | bytes 1572868
  4.9 34.4 %all-to-all-start = ((bf16[32,104,256]{2,1,0:T(8,128)(2,1)}), bf16[32,104,256]{2,1,0:T(8,128)(2,1)S(1)}, u32[]{:S(2)}, u32[]{:S(2)}) async-start(bf16[32,104,256]{2,1,0:T(8,128)(2,1)} %dispatch.1), calls=%async_computation | async-start | bytes 3407872 | tf_op jit(solution)/shard_map/all_to_all | solution.py:333
  12.7 24.5 %collective-permute-start.1 = (bf16[896,256]{1,0:T(8,128)(2,1)S(1)}, bf16[896,256]{1,0:T(8,128)(2,1)S(1)}, u32[]{:S(2)}, u32[]{:S(2)}) collective-permute-start(bf16[896,256]{1,0:T(8,128)(2,1)S(1)} %bitcast.22), channel_id=1, source_target_pairs={{1,0},{2,1},{3,2},{4,3},{5,4},{6,5},{7,6},{8,7},{9,8},{10,9},{11,1... | collective-permute-start | bytes 1376264 | tf_op jit(solution)/shard_map/ppermute | solution.py:343
  17.0 18.2 %collective-permute-start = (bf16[64,256]{1,0:T(8,128)(2,1)S(1)}, bf16[64,256]{1,0:T(8,128)(2,1)S(1)}, u32[]{:S(2)}, u32[]{:S(2)}) collective-permute-start(bf16[64,256]{1,0:T(8,128)(2,1)S(1)} %slice_bitcast_fusion), channel_id=1, source_target_pairs={{0,1},{1,2},{2,3},{3,4},{4,5},{5,6},{6,7},{7,8},{8,9},{9,10},{10,1... | collective-permute-start | bytes 98312 | tf_op jit(solution)/shard_map/ppermute | solution.py:342
  37.2 0.8 copy-start.1
  37.9 1.0 copy-start.2
  46.2 4.9 %copy-start.4 = (bf16[896,256]{1,0:T(8,128)(2,1)}, bf16[896,256]{1,0:T(8,128)(2,1)S(1)}, u32[]{:S(2)}) copy-start(bf16[896,256]{1,0:T(8,128)(2,1)S(1)} %get-tuple-element.8) | copy-start | bytes 1376260
  46.2 4.9 %copy-start.5 = (f32[1088,256]{1,0:T(8,128)}, f32[1088,256]{1,0:T(8,128)S(1)}, u32[]{:S(2)}) copy-start(f32[1088,256]{1,0:T(8,128)S(1)} %get-tuple-element.7.own_ref) | copy-start | bytes 3342340
  46.2 4.8 %collective-permute-start.4 = (bf16[16,72,256]{2,1,0:T(8,128)(2,1)S(1)}, bf16[16,72,256]{2,1,0:T(8,128)(2,1)S(1)}, u32[]{:S(2)}, u32[]{:S(2)}) collective-permute-start(bf16[16,72,256]{2,1,0:T(8,128)(2,1)S(1)} %get-tuple-element.11), channel_id=1, source_target_pairs={{0,1},{1,0},{2,3},{3,2},{4,5},{5,4},{6,7},{7,6},{8,9},{9,8},{10,11... | collective-permute-start | bytes 1769480 | tf_op jit(solution)/shard_map/ppermute | solution.py:348
  51.1 51.9 %copy-start.3 = (bf16[3,3,256,256]{3,2,1,0:T(8,128)(2,1)S(1)}, bf16[3,3,256,256]{3,2,1,0:T(8,128)(2,1)}, u32[]{:S(2)}) copy-start(bf16[3,3,256,256]{3,2,1,0:T(8,128)(2,1)} %param.6) | copy-start | bytes 3538948
  69.1 33.9 %copy-start.6 = (f32[1088,256]{1,0:T(8,128)S(1)}, f32[1088,256]{1,0:T(8,128)}, u32[]{:S(2)}) copy-start(f32[1088,256]{1,0:T(8,128)} %copy-done.5) | copy-start | bytes 3342340
  69.9 13.7 %all-to-all-start.2 = ((bf16[4,72,256]{2,1,0:T(8,128)(2,1)}), bf16[4,72,256]{2,1,0:T(8,128)(2,1)S(1)}, u32[]{:S(2)}, u32[]{:S(2)}) async-start(bf16[4,72,256]{2,1,0:T(8,128)(2,1)} %sum.4), calls=%async_computation.2 | async-start | bytes 294912 | tf_op jit(solution)/shard_map/all_to_all | solution.py:333
  75.9 27.2 %collective-permute-start.2 = (bf16[896,256]{1,0:T(8,128)(2,1)}, bf16[896,256]{1,0:T(8,128)(2,1)S(1)}, u32[]{:S(2)}, u32[]{:S(2)}) collective-permute-start(bf16[896,256]{1,0:T(8,128)(2,1)} %copy-done.4), channel_id=1, source_target_pairs={{0,1},{1,2},{2,3},{3,4},{4,5},{5,6},{6,7},{7,8},{8,9},{9,10},{10,1... | collective-permute-start | bytes 1376264 | tf_op jit(solution)/shard_map/ppermute | solution.py:350
  77.8 25.3 %collective-permute-start.3 = (bf16[64,256]{1,0:T(8,128)(2,1)S(1)}, bf16[64,256]{1,0:T(8,128)(2,1)S(1)}, u32[]{:S(2)}, u32[]{:S(2)}) collective-permute-start(bf16[64,256]{1,0:T(8,128)(2,1)S(1)} %get-tuple-element.9), channel_id=1, source_target_pairs={{1,0},{2,1},{3,2},{4,3},{5,4},{6,5},{7,6},{8,7},{9,8},{10,9},{11,1... | collective-permute-start | bytes 98312 | tf_op jit(solution)/shard_map/ppermute | solution.py:351

commit v4 on v3

--- a/solution.py
+++ b/solution.py
@@ -20,7 +20,6 @@
 CHIPS = TILES // 2
 IMAGES = 16
 EXT = TR + REACH - 1
-REACHED = 32 * MW
 SLOT = CELLS + 1
 BLOCK = 104
 SLOTS = TILES * CAP
@@ -37,6 +36,10 @@
 
 def vmem():
     return pl.BlockSpec(memory_space=pltpu.VMEM)
+
+
+def hbm():
+    return pl.BlockSpec(memory_space=pltpu.HBM)
 
 
 def cost(flops, moved):
@@ -132,7 +135,7 @@
         compiler_params=pltpu.CompilerParams(vmem_limit_bytes=60 << 20),
         name="dispatch",
         cost_estimate=cost(2 * KDIM * SLOT * ROI_DEV * C, 3 << 20),
-    )(index, boxes_t, grads)
+    )(*(pltpu.with_memory_space_constraint(x, pltpu.HBM) for x in (index, boxes_t, grads)))
 
 
 def weights_of(got_ref, rows_ref, cols_ref):
@@ -168,50 +171,60 @@
     )
 
 
-def turn_kernel(before_ref, own_ref, after_ref, out_ref):
-    rows = jnp.concatenate(
-        [before_ref[...], own_ref[...], after_ref[...], jnp.zeros((MW, C), BF16)], axis=0
-    )
-    out_ref[...] = rows.T
-
-
-def turn(before, own, after):
+def shifts(rows, before, after):
+    count = rows.shape[0]
+    column = iota((count, C), 0) % MW
+    one_less = jnp.where(column == 0, 0.0, pltpu.roll(rows, 1, 0)).astype(BF16)
+    one_more = jnp.where(column == MW - 1, 0.0, pltpu.roll(rows, count - 1, 0)).astype(BF16)
+    return {before: one_less, 1: rows.astype(BF16), after: one_more}
+
+
+def turn_rows(rows, out_ref):
+    for e, moved in shifts(rows.astype(F32), 0, 2).items():
+        out_ref[e * C : (e + 1) * C] = moved.T
+
+
+def turn_kernel(rows_ref, out_hbm, out_ref, sem):
+    turn_rows(rows_ref[...], out_ref)
+    copy = pltpu.make_async_copy(out_ref, out_hbm, sem)
+    copy.start()
+    copy.wait()
+
+
+def turn(rows):
     return pl.pallas_call(
         turn_kernel,
-        out_shape=jax.ShapeDtypeStruct((C, REACHED), BF16),
-        in_specs=[vmem()] * 3,
-        out_specs=vmem(),
-        compiler_params=pltpu.CompilerParams(vmem_limit_bytes=8 << 20),
+        out_shape=pltpu.HBM((3 * C, TR * MW), BF16),
+        in_specs=[vmem()],
+        out_specs=hbm(),
+        scratch_shapes=[pltpu.VMEM((3 * C, TR * MW), BF16), pltpu.SemaphoreType.DMA],
+        compiler_params=pltpu.CompilerParams(vmem_limit_bytes=12 << 20),
         name="turn",
         cost_estimate=cost(TR * MW * C, 2 << 20),
-    )(before, own, after)
-
-
-def shifts(rows):
-    count = rows.shape[0]
-    column = iota((count, C), 0) % MW
-    return (
-        jnp.where(column == MW - 1, 0.0, pltpu.roll(rows, count - 1, 0)).astype(BF16),
-        rows.astype(BF16),
-        jnp.where(column == 0, 0.0, pltpu.roll(rows, 1, 0)).astype(BF16),
-    )
+    )(rows)
 
 
 def filter_kernel(
-    core_ref, got_ref, turned_ref, keep_ref, give_ref, own_ref, above_ref, below_ref,
-    rows_ref, cols_ref, left_ref, shifted_ref,
+    core_ref, got_ref, turned_hbm, before_ref, after_ref,
+    keep_ref, give_ref, own_hbm, above_ref, below_ref,
+    rows_ref, cols_ref, left_ref, map_ref, turned_ref, rest_ref, own_ref, sems,
 ):
+    fetch = pltpu.make_async_copy(turned_hbm, turned_ref, sems.at[0])
+    fetch.start()
     weights_of(got_ref, rows_ref, cols_ref)
-    shifted_ref[:, : 2 * MW] = jnp.zeros((3, 2 * MW, C), BF16)
-    shifted_ref[:, (2 + EXT) * MW :] = jnp.zeros((3, 3 * MW, C), BF16)
+    fetch.wait()
+    rest = jnp.concatenate([after_ref[...], before_ref[...], jnp.zeros((MW, C), BF16)], axis=0)
+    turn_rows(rest, rest_ref)
+    map_ref[: 2 * MW] = jnp.zeros((2 * MW, C), BF16)
+    map_ref[(2 + EXT) * MW :] = jnp.zeros((4 * MW, C), BF16)
     for start, count in ((0, 8), (8, 8), (16, 8), (24, 5)):
         part = rows_of(start, count, got_ref, rows_ref, cols_ref, left_ref)
-        for e, moved in enumerate(shifts(part)):
-            shifted_ref[e, (2 + start) * MW : (2 + start + count) * MW] = moved
+        map_ref[(2 + start) * MW : (2 + start + count) * MW] = part.astype(BF16)
         if start < TR:
             own_ref[start * MW : (start + count) * MW] = part
         if start == 0:
             below_ref[...] = part[:MW].astype(BF16)
+            map_ref[(4 + EXT) * MW : (5 + EXT) * MW] = part[:MW].astype(BF16)
         if start == 8:
             above_ref[:MW] = part[7 * MW :].astype(BF16)
         if start == 16:
@@ -219,42 +232,53 @@
             above_ref[MW : 9 * MW] = part.astype(BF16)
         if start == 24:
             above_ref[9 * MW :] = part.astype(BF16)
+    put = pltpu.make_async_copy(own_ref, own_hbm, sems.at[1])
+    put.start()
     first = core_ref[0] == 0
     for a in range(3):
+        part = jnp.dot(
+            turned_ref[...],
+            map_ref[(3 - a) * MW : (3 - a + TR) * MW],
+            preferred_element_type=F32,
+        ) + jnp.dot(
+            rest_ref[...],
+            map_ref[(3 - a + TR) * MW : (3 - a + 2 * TR) * MW],
+            preferred_element_type=F32,
+        )
+        part = part.reshape(3, CHIPS, 2, CIN, C)
         for e in range(3):
-            part = jnp.dot(
-                turned_ref[...],
-                shifted_ref[e, (2 - a) * MW : (2 - a) * MW + REACHED],
-                preferred_element_type=F32,
-            )
-            part = part.reshape(CHIPS, 2, CIN, C)
             at = (a * 3 + e) * CIN
-            keep_ref[:, at : at + CIN, :] = jnp.where(first, part[:, 0], part[:, 1])
-            give_ref[:, at : at + CIN, :] = jnp.where(first, part[:, 1], part[:, 0]).astype(BF16)
-
-
-def filter_part(core, got, turned):
+            keep_ref[:, at : at + CIN, :] = jnp.where(first, part[e, :, 0], part[e, :, 1])
+            give_ref[:, at : at + CIN, :] = jnp.where(first, part[e, :, 1], part[e, :, 0]).astype(BF16)
+    put.wait()
+
+
+def filter_part(core, got, turned, before, after):
     return pl.pallas_call(
         filter_kernel,
         out_shape=(
             jax.ShapeDtypeStruct((CHIPS, NPART, C), F32),
             jax.ShapeDtypeStruct((CHIPS, NPART, C), BF16),
-            jax.ShapeDtypeStruct(((TR + 1) * MW, C), F32),
+            pltpu.HBM(((TR + 1) * MW, C), F32),
             jax.ShapeDtypeStruct((REACH * MW, C), BF16),
             jax.ShapeDtypeStruct((MW, C), BF16),
         ),
-        in_specs=[pl.BlockSpec(memory_space=pltpu.SMEM), vmem(), vmem()],
-        out_specs=(vmem(),) * 5,
+        in_specs=[pl.BlockSpec(memory_space=pltpu.SMEM), vmem(), hbm(), vmem(), vmem()],
+        out_specs=(vmem(), vmem(), hbm(), vmem(), vmem()),
         scratch_shapes=[
             pltpu.VMEM((32, KDIM), F32),
             pltpu.VMEM((MW, KDIM), BF16),
             pltpu.VMEM((8 * MW, KDIM), BF16),
-            pltpu.VMEM((3, (EXT + 5) * MW, C), BF16),
+            pltpu.VMEM(((EXT + 6) * MW, C), BF16),
+            pltpu.VMEM((3 * C, TR * MW), BF16),
+            pltpu.VMEM((3 * C, TR * MW), BF16),
+            pltpu.VMEM(((TR + 1) * MW, C), F32),
+            pltpu.SemaphoreType.DMA((2,)),
         ],
         compiler_params=pltpu.CompilerParams(vmem_limit_bytes=30 << 20),
         name="filter",
-        cost_estimate=cost(2 * EXT * MW * KDIM * C + 18 * REACHED * C * C, 4 << 20),
-    )(core, got, turned)
+        cost_estimate=cost(2 * EXT * MW * KDIM * C + 36 * TR * MW * C * C, 4 << 20),
+    )(core, got, pltpu.with_memory_space_constraint(turned, pltpu.HBM), before, after)
 
 
 def input_kernel(own_ref, above_ref, below_ref, weight_ref, out_ref, shifted_ref):
@@ -267,7 +291,7 @@
         ],
         axis=0,
     )
-    for e, moved in enumerate(shifts(whole)):
+    for e, moved in shifts(whole, 2, 0).items():
         shifted_ref[e] = moved
     total = jnp.zeros((TR * MW, C), F32)
     for a in range(3):
@@ -314,7 +338,7 @@
 
 
 def pair_kernel(keep_ref, got_ref, out_ref):
-    out_ref[...] = (keep_ref[...] + got_ref[...].astype(F32)).astype(BF16)
+    out_ref[...] = (keep_ref[...].astype(F32) + got_ref[...].astype(F32)).astype(BF16)
 
 
 def sum_pair(keep, got):
@@ -342,19 +366,20 @@
     before = lax.ppermute(feature_rows[(TR - 1) * MW :], TILE_AXES, up)
     after = lax.ppermute(feature_rows[: REACH * MW], TILE_AXES, down)
     got = exchange(send, TILE_AXES)
-    turned = turn(before, feature_rows, after)
+    turned = turn(feature_rows)
     core = lax.axis_index("core").reshape(1)
-    keep, give, own, above, below = filter_part(core, got, turned)
+    keep, give, own, above, below = filter_part(core, got, turned, before, after)
     taken = lax.ppermute(give, "core", [(0, 1), (1, 0)])
     parts = exchange(sum_pair(keep, taken), "chip")
     above = lax.ppermute(above, TILE_AXES, up)
     below = lax.ppermute(below, TILE_AXES, down)
     x_grad = input_part(own, above, below, weight.reshape(9, C, C)).reshape(1, TR, MW, C)
     parts = exchange(sum_parts(parts, (4, NPART, C), BF16), "zl")
-    parts = sum_parts(parts, (1, NPART, C), BF16)
-    parts = lax.all_gather(parts, "zh", tiled=True, axis_index_groups=[[0, 1], [2, 3]])
-    parts = sum_parts(parts, (1, NPART, C), BF16)
-    parts = lax.all_gather(parts, "zh", tiled=True, axis_index_groups=[[0, 3], [1, 2]])
+    parts = sum_parts(parts, (NPART, C), BF16)
+    taken = lax.ppermute(parts, "zh", [(0, 1), (1, 0), (2, 3), (3, 2)])
+    parts = sum_pair(parts, taken)
+    parts, x_grad = lax.optimization_barrier((parts, x_grad))
+    parts = lax.all_gather(parts[None], "zh", tiled=True, axis_index_groups=[[0, 3], [1, 2]])
     total = sum_parts(parts, (NPART, C), F32, 1.0 / IMAGES)
     total = total.reshape(9, CIN, C).transpose(1, 0, 2).reshape(CIN, 3, 3, C)
     return x_grad, total

time: 106 us -> 104 us (0.981)
  the two profiles are of different devices: /device:TPU:34 before, /device:TPU:32 now
where the time goes in v4:
time: 104 us
  starting transfers between devices  40 us (38%)
  waiting for transfers between devices  34.9 us (34%)
  Pallas kernels  17.8 us (17%)
  blocking collectives  8.94 us (9%)
  local copies, waits for them, and re-layouts  1.29 us (1%)
    all_to_all x3, waiting for transfers between devices, exchange(): return lax.all_to_all(parts, axis, split_axis=0, concat_axis=0, tiled=True)  33.3 us
    all_to_all x3, starting transfers between devices, exchange(): return lax.all_to_all(parts, axis, split_axis=0, concat_axis=0, tiled=True)  20 us
    ppermute x1, starting transfers between devices, body(): taken = lax.ppermute(parts, 'zh', [(0, 1), (1, 0), (2, 3), (3, 2)])  9.1 us
    all_gather x1, blocking collectives, body(): lax.all_gather(parts[None], 'zh', tiled=True, axis_index_groups=[[0, 3],...  8.94 us
    pallas_call x1, Pallas kernels, filter_part(): pl.pallas_call(filter_kernel, out_shape=(jax.ShapeDtypeStruct((CHIPS, NPA...  7.35 us
    pallas_call x1, Pallas kernels, dispatch(): pl.pallas_call(dispatch_kernel, out_shape=jax.ShapeDtypeStruct((TILES, BL...  4.21 us
    ppermute x1, starting transfers between devices, body(): taken = lax.ppermute(give, 'core', [(0, 1), (1, 0)])  3.26 us
    ppermute x1, starting transfers between devices, body(): before = lax.ppermute(feature_rows[(TR - 1) * MW:], TILE_AXES, up)  3.03 us
  transfers between devices with their start and end apart: 9, of which 4 were waited for; matrix products, arithmetic and copies ran while one was open for 0% of the time, Pallas kernels for 4%

profile of v4, /device:TPU:32, one launch (start us, length us, event | category | flops | bytes accessed | tf_op | source)
XLA Modules:
  0.0 103.7 jit_solution(6167235777981810702)
XLA Ops:
  0.6 4.2 %dispatch.1 = bf16[32,104,256]{2,1,0:T(8,128)(2,1)} custom-call(s32[1,16]{1,0:T(1,128)} %index_hbm.1, s32[4,20000]{1,0:T(4,128)} %bitcast.27, bf16[49,16,256]{2,1,0:T(8,128)(2,1)} %bitcast.26), custom_call_target="tpu_custom_call" | custom-call | flops 1363148800 | bytes 3145728 | tf_op jit(solution)/shard_map/dispatch/pallas_call | solution.py:123
  4.9 0.0 copy-start
  4.9 7.5 %all-to-all-start = ((bf16[32,104,256]{2,1,0:T(8,128)(2,1)}), bf16[32,104,256]{2,1,0:T(8,128)(2,1)S(1)}, u32[]{:S(2)}, u32[]{:S(2)}) async-start(bf16[32,104,256]{2,1,0:T(8,128)(2,1)} %dispatch.1), calls=%async_computation | async-start | bytes 3407872 | tf_op jit(solution)/shard_map/all_to_all | solution.py:357
  12.4 1.3 %collective-permute-start.1 = (bf16[896,256]{1,0:T(8,128)(2,1)S(1)}, bf16[896,256]{1,0:T(8,128)(2,1)S(1)}, u32[]{:S(2)}, u32[]{:S(2)}) collective-permute-start(bf16[896,256]{1,0:T(8,128)(2,1)S(1)} %bitcast.24), channel_id=1, source_target_pairs={{1,0},{2,1},{3,2},{4,3},{5,4},{6,5},{7,6},{8,7},{9,8},{10,9},{11,1... | collective-permute-start | bytes 1376264 | tf_op jit(solution)/shard_map/ppermute | solution.py:367
  13.7 3.0 %collective-permute-start = (bf16[64,256]{1,0:T(8,128)(2,1)S(1)}, bf16[64,256]{1,0:T(8,128)(2,1)S(1)}, u32[]{:S(2)}, u32[]{:S(2)}) collective-permute-start(bf16[64,256]{1,0:T(8,128)(2,1)S(1)} %slice_bitcast_fusion), channel_id=1, source_target_pairs={{0,1},{1,2},{2,3},{3,4},{4,5},{5,6},{6,7},{7,8},{8,9},{9,10},{10,1... | collective-permute-start | bytes 98312 | tf_op jit(solution)/shard_map/ppermute | solution.py:366
  16.7 1.6 %turn.1.turned_hbm = bf16[768,1024]{1,0:T(8,128)(2,1)} custom-call(bf16[1024,256]{1,0:T(8,128)(2,1)S(1)} %bitcast.21), custom_call_target="tpu_custom_call" | custom-call | flops 262144 | bytes 2097152 | tf_op jit(solution)/shard_map/turn/pallas_call | solution.py:195
  18.4 0.0 collective-permute-done.before_ref
  18.4 18.5 %all-to-all-done.got_ref = bf16[32,104,256]{2,1,0:T(8,128)(2,1)S(1)} async-done(((bf16[32,104,256]{2,1,0:T(8,128)(2,1)}), bf16[32,104,256]{2,1,0:T(8,128)(2,1)S(1)}, u32[]{:S(2)}, u32[]{:S(2)}) %all-to-all-start) | async-done | bytes 1703968 | tf_op jit(solution)/shard_map/all_to_all | solution.py:357
  36.9 7.4 %filter.1 = (f32[16,72,256]{2,1,0:T(8,128)S(1)}, bf16[16,72,256]{2,1,0:T(8,128)(2,1)S(1)}, f32[1088,256]{1,0:T(8,128)}, bf16[896,256]{1,0:T(8,128)(2,1)S(1)}, bf16[64,256]{1,0:T(8,128)(2,1)S(1)}) custom-call(s32[1]{0:T(128)} %bitcast.core_ref, bf16[32,104,256]{2,1,0:T(8,128)(2,1)S(1)} %all-to-all-done.got_ref, bf16[768,1024]{1,0:T(8,128)(2,1)} %turn.1.turned_hbm, ...), custom_call_target="tpu_custom_call" | custom-call | flops 5578424320 | bytes 4194304 | tf_op jit(solution)/shard_map/filter/pallas_call | solution.py:257
  44.3 3.3 %collective-permute-start.2 = (bf16[16,72,256]{2,1,0:T(8,128)(2,1)S(1)}, bf16[16,72,256]{2,1,0:T(8,128)(2,1)S(1)}, u32[]{:S(2)}, u32[]{:S(2)}) collective-permute-start(bf16[16,72,256]{2,1,0:T(8,128)(2,1)S(1)} %get-tuple-element.10), channel_id=1, source_target_pairs={{0,1},{1,0},{2,3},{3,2},{4,5},{5,4},{6,7},{7,6},{8,9},{9,8},{10,11... | collective-permute-start | bytes 1769480 | tf_op jit(solution)/shard_map/ppermute | solution.py:372
  47.5 1.6 %collective-permute-done.2.got_ref = bf16[16,72,256]{2,1,0:T(8,128)(2,1)S(1)} collective-permute-done((bf16[16,72,256]{2,1,0:T(8,128)(2,1)S(1)}, bf16[16,72,256]{2,1,0:T(8,128)(2,1)S(1)}, u32[]{:S(2)}, u32[]{:S(2)}) %collective-permute-start.2) | collective-permute-done | bytes 589856 | tf_op jit(solution)/shard_map/ppermute | solution.py:372
  49.2 0.9 pair.2
  50.1 6.6 %all-to-all-start.1 = ((bf16[16,72,256]{2,1,0:T(8,128)(2,1)}), bf16[16,72,256]{2,1,0:T(8,128)(2,1)S(1)}, u32[]{:S(2)}, u32[]{:S(2)}) async-start(bf16[16,72,256]{2,1,0:T(8,128)(2,1)} %pair.2), calls=%async_computation.1 | async-start | bytes 1179648 | tf_op jit(solution)/shard_map/all_to_all | solution.py:357
  56.7 2.0 %collective-permute-start.4 = (bf16[896,256]{1,0:T(8,128)(2,1)S(1)}, bf16[896,256]{1,0:T(8,128)(2,1)S(1)}, u32[]{:S(2)}, u32[]{:S(2)}) collective-permute-start(bf16[896,256]{1,0:T(8,128)(2,1)S(1)} %get-tuple-element.12), channel_id=1, source_target_pairs={{0,1},{1,2},{2,3},{3,4},{4,5},{5,6},{6,7},{7,8},{8,9},{9,10},{10,1... | collective-permute-start | bytes 1376264 | tf_op jit(solution)/shard_map/ppermute | solution.py:374
  58.7 10.8 %all-to-all-done.1.parts_ref = bf16[16,72,256]{2,1,0:T(8,128)(2,1)S(1)} async-done(((bf16[16,72,256]{2,1,0:T(8,128)(2,1)}), bf16[16,72,256]{2,1,0:T(8,128)(2,1)S(1)}, u32[]{:S(2)}, u32[]{:S(2)}) %all-to-all-start.1) | async-done | bytes 589856 | tf_op jit(solution)/shard_map/all_to_all | solution.py:357
  69.4 0.7 sum.3
  70.2 6.0 %all-to-all-start.2 = ((bf16[4,72,256]{2,1,0:T(8,128)(2,1)}), bf16[4,72,256]{2,1,0:T(8,128)(2,1)S(1)}, u32[]{:S(2)}, u32[]{:S(2)}) async-start(bf16[4,72,256]{2,1,0:T(8,128)(2,1)} %sum.3), calls=%async_computation.2 | async-start | bytes 294912 | tf_op jit(solution)/shard_map/all_to_all | solution.py:357
  76.2 1.3 %collective-permute-start.5 = (bf16[64,256]{1,0:T(8,128)(2,1)S(1)}, bf16[64,256]{1,0:T(8,128)(2,1)S(1)}, u32[]{:S(2)}, u32[]{:S(2)}) collective-permute-start(bf16[64,256]{1,0:T(8,128)(2,1)S(1)} %get-tuple-element.13), channel_id=1, source_target_pairs={{1,0},{2,1},{3,2},{4,3},{5,4},{6,5},{7,6},{8,7},{9,8},{10,9},{11,1... | collective-permute-start | bytes 98312 | tf_op jit(solution)/shard_map/ppermute | solution.py:375
  77.5 4.0 %all-to-all-done.2.parts_ref = bf16[4,72,256]{2,1,0:T(8,128)(2,1)S(1)} async-done(((bf16[4,72,256]{2,1,0:T(8,128)(2,1)}), bf16[4,72,256]{2,1,0:T(8,128)(2,1)S(1)}, u32[]{:S(2)}, u32[]{:S(2)}) %all-to-all-start.2) | async-done | bytes 147488 | tf_op jit(solution)/shard_map/all_to_all | solution.py:357
  81.5 9.1 %collective-permute-start.3 = (bf16[72,256]{1,0:T(8,128)(2,1)S(1)}, bf16[72,256]{1,0:T(8,128)(2,1)S(1)}, u32[]{:S(2)}, u32[]{:S(2)}) collective-permute-start(bf16[72,256]{1,0:T(8,128)(2,1)S(1)} %sum.4.keep_ref), channel_id=1, source_target_pairs={{0,128},{128,0},{256,384},{384,256},{1,129},{129,1},{257,385},{385... | collective-permute-start | bytes 110600 | tf_op jit(solution)/shard_map/ppermute | solution.py:379
  90.6 1.2 %copy-done.2 = f32[1088,256]{1,0:T(8,128)S(1)} copy-done((f32[1088,256]{1,0:T(8,128)S(1)}, f32[1088,256]{1,0:T(8,128)}, u32[]{:S(2)}) %copy-start.2) | copy-done | bytes 1114136
  91.9 2.2 %input.1 = bf16[1024,256]{1,0:T(8,128)(2,1)} custom-call(f32[1088,256]{1,0:T(8,128)S(1)} %copy-done.2, bf16[896,256]{1,0:T(8,128)(2,1)S(1)} %collective-permute-done.4.above_ref, bf16[64,256]{1,0:T(8,128)(2,1)S(1)} %collective-permute-done.5.below_ref, bf16[9,256,256]{2,1,0:T(8,128)(2,1)S(1)} %bitcast.23), custom_call_target="tpu_custom_call" | custom-call | flops 1207959552 | bytes 4194304 | tf_op jit(solution)/shard_map/input/pallas_call | solution.py:309
  94.2 8.9 %all-gather = bf16[144,256]{1,0:T(8,128)(2,1)S(1)} all-gather(bf16[72,256]{1,0:T(8,128)(2,1)S(1)} %pair.3), channel_id=2, replica_groups={{0,384},{128,256},{1,385},{129,257},{2,386},{130,258},{3,387},{131,259}..., dimensions={0}, use_global_device_ids=true | all-gather | bytes 110592 | tf_op jit(solution)/shard_map/all_gather | solution.py:382
  103.1 0.6 sum.5
  (12 shorter events, 0.1 us)
Async XLA Ops:
  4.9 7.5 %copy-start = (bf16[1,16,64,256]{3,2,1,0:T(8,128)(2,1)S(1)}, bf16[1,16,64,256]{3,2,1,0:T(8,128)(2,1)}, u32[]{:S(2)}) copy-start(bf16[1,16,64,256]{3,2,1,0:T(8,128)(2,1)} %param.5) | copy-start | bytes 1572868
  4.9 32.1 %all-to-all-start = ((bf16[32,104,256]{2,1,0:T(8,128)(2,1)}), bf16[32,104,256]{2,1,0:T(8,128)(2,1)S(1)}, u32[]{:S(2)}, u32[]{:S(2)}) async-start(bf16[32,104,256]{2,1,0:T(8,128)(2,1)} %dispatch.1), calls=%async_computation | async-start | bytes 3407872 | tf_op jit(solution)/shard_map/all_to_all | solution.py:357
  12.4 6.0 %collective-permute-start.1 = (bf16[896,256]{1,0:T(8,128)(2,1)S(1)}, bf16[896,256]{1,0:T(8,128)(2,1)S(1)}, u32[]{:S(2)}, u32[]{:S(2)}) collective-permute-start(bf16[896,256]{1,0:T(8,128)(2,1)S(1)} %bitcast.24), channel_id=1, source_target_pairs={{1,0},{2,1},{3,2},{4,3},{5,4},{6,5},{7,6},{8,7},{9,8},{10,9},{11,1... | collective-permute-start | bytes 1376264 | tf_op jit(solution)/shard_map/ppermute | solution.py:367
  13.7 4.7 %collective-permute-start = (bf16[64,256]{1,0:T(8,128)(2,1)S(1)}, bf16[64,256]{1,0:T(8,128)(2,1)S(1)}, u32[]{:S(2)}, u32[]{:S(2)}) collective-permute-start(bf16[64,256]{1,0:T(8,128)(2,1)S(1)} %slice_bitcast_fusion), channel_id=1, source_target_pairs={{0,1},{1,2},{2,3},{3,4},{4,5},{5,6},{6,7},{7,8},{8,9},{9,10},{10,1... | collective-permute-start | bytes 98312 | tf_op jit(solution)/shard_map/ppermute | solution.py:366
  44.3 4.9 %collective-permute-start.2 = (bf16[16,72,256]{2,1,0:T(8,128)(2,1)S(1)}, bf16[16,72,256]{2,1,0:T(8,128)(2,1)S(1)}, u32[]{:S(2)}, u32[]{:S(2)}) collective-permute-start(bf16[16,72,256]{2,1,0:T(8,128)(2,1)S(1)} %get-tuple-element.10), channel_id=1, source_target_pairs={{0,1},{1,0},{2,3},{3,2},{4,5},{5,4},{6,7},{7,6},{8,9},{9,8},{10,11... | collective-permute-start | bytes 1769480 | tf_op jit(solution)/shard_map/ppermute | solution.py:372
  50.1 40.5 %copy-start.1 = (bf16[3,3,256,256]{3,2,1,0:T(8,128)(2,1)S(1)}, bf16[3,3,256,256]{3,2,1,0:T(8,128)(2,1)}, u32[]{:S(2)}) copy-start(bf16[3,3,256,256]{3,2,1,0:T(8,128)(2,1)} %param.6) | copy-start | bytes 3538948
  50.1 19.3 %all-to-all-start.1 = ((bf16[16,72,256]{2,1,0:T(8,128)(2,1)}), bf16[16,72,256]{2,1,0:T(8,128)(2,1)S(1)}, u32[]{:S(2)}, u32[]{:S(2)}) async-start(bf16[16,72,256]{2,1,0:T(8,128)(2,1)} %pair.2), calls=%async_computation.1 | async-start | bytes 1179648 | tf_op jit(solution)/shard_map/all_to_all | solution.py:357
  56.7 34.0 %collective-permute-start.4 = (bf16[896,256]{1,0:T(8,128)(2,1)S(1)}, bf16[896,256]{1,0:T(8,128)(2,1)S(1)}, u32[]{:S(2)}, u32[]{:S(2)}) collective-permute-start(bf16[896,256]{1,0:T(8,128)(2,1)S(1)} %get-tuple-element.12), channel_id=1, source_target_pairs={{0,1},{1,2},{2,3},{3,4},{4,5},{5,6},{6,7},{7,8},{8,9},{9,10},{10,1... | collective-permute-start | bytes 1376264 | tf_op jit(solution)/shard_map/ppermute | solution.py:374
  70.2 11.3 %all-to-all-start.2 = ((bf16[4,72,256]{2,1,0:T(8,128)(2,1)}), bf16[4,72,256]{2,1,0:T(8,128)(2,1)S(1)}, u32[]{:S(2)}, u32[]{:S(2)}) async-start(bf16[4,72,256]{2,1,0:T(8,128)(2,1)} %sum.3), calls=%async_computation.2 | async-start | bytes 294912 | tf_op jit(solution)/shard_map/all_to_all | solution.py:357
  76.2 14.4 %collective-permute-start.5 = (bf16[64,256]{1,0:T(8,128)(2,1)S(1)}, bf16[64,256]{1,0:T(8,128)(2,1)S(1)}, u32[]{:S(2)}, u32[]{:S(2)}) collective-permute-start(bf16[64,256]{1,0:T(8,128)(2,1)S(1)} %get-tuple-element.13), channel_id=1, source_target_pairs={{1,0},{2,1},{3,2},{4,3},{5,4},{6,5},{7,6},{8,7},{9,8},{10,9},{11,1... | collective-permute-start | bytes 98312 | tf_op jit(solution)/shard_map/ppermute | solution.py:375
  81.5 12.6 %collective-permute-start.3 = (bf16[72,256]{1,0:T(8,128)(2,1)S(1)}, bf16[72,256]{1,0:T(8,128)(2,1)S(1)}, u32[]{:S(2)}, u32[]{:S(2)}) collective-permute-start(bf16[72,256]{1,0:T(8,128)(2,1)S(1)} %sum.4.keep_ref), channel_id=1, source_target_pairs={{0,128},{128,0},{256,384},{384,256},{1,129},{129,1},{257,385},{385... | collective-permute-start | bytes 110600 | tf_op jit(solution)/shard_map/ppermute | solution.py:379
  90.6 1.2 %copy-start.2 = (f32[1088,256]{1,0:T(8,128)S(1)}, f32[1088,256]{1,0:T(8,128)}, u32[]{:S(2)}) copy-start(f32[1088,256]{1,0:T(8,128)} %get-tuple-element.11.own_ref) | copy-start | bytes 3342340

commit v5 on v4

--- a/solution.py
+++ b/solution.py
@@ -184,37 +184,16 @@
         out_ref[e * C : (e + 1) * C] = moved.T
 
 
-def turn_kernel(rows_ref, out_hbm, out_ref, sem):
-    turn_rows(rows_ref[...], out_ref)
-    copy = pltpu.make_async_copy(out_ref, out_hbm, sem)
-    copy.start()
-    copy.wait()
-
-
-def turn(rows):
-    return pl.pallas_call(
-        turn_kernel,
-        out_shape=pltpu.HBM((3 * C, TR * MW), BF16),
-        in_specs=[vmem()],
-        out_specs=hbm(),
-        scratch_shapes=[pltpu.VMEM((3 * C, TR * MW), BF16), pltpu.SemaphoreType.DMA],
-        compiler_params=pltpu.CompilerParams(vmem_limit_bytes=12 << 20),
-        name="turn",
-        cost_estimate=cost(TR * MW * C, 2 << 20),
-    )(rows)
-
-
 def filter_kernel(
-    core_ref, got_ref, turned_hbm, before_ref, after_ref,
+    core_ref, got_ref, features_ref, before_ref, after_ref,
     keep_ref, give_ref, own_hbm, above_ref, below_ref,
-    rows_ref, cols_ref, left_ref, map_ref, turned_ref, rest_ref, own_ref, sems,
+    rows_ref, cols_ref, left_ref, map_ref, turned_ref, own_ref, sem,
 ):
-    fetch = pltpu.make_async_copy(turned_hbm, turned_ref, sems.at[0])
-    fetch.start()
     weights_of(got_ref, rows_ref, cols_ref)
-    fetch.wait()
-    rest = jnp.concatenate([after_ref[...], before_ref[...], jnp.zeros((MW, C), BF16)], axis=0)
-    turn_rows(rest, rest_ref)
+    features = jnp.concatenate(
+        [features_ref[...], after_ref[...], before_ref[...], jnp.zeros((MW, C), BF16)], axis=0
+    )
+    turn_rows(features, turned_ref)
     map_ref[: 2 * MW] = jnp.zeros((2 * MW, C), BF16)
     map_ref[(2 + EXT) * MW :] = jnp.zeros((4 * MW, C), BF16)
     for start, count in ((0, 8), (8, 8), (16, 8), (24, 5)):
@@ -232,17 +211,13 @@
             above_ref[MW : 9 * MW] = part.astype(BF16)
         if start == 24:
             above_ref[9 * MW :] = part.astype(BF16)
-    put = pltpu.make_async_copy(own_ref, own_hbm, sems.at[1])
+    put = pltpu.make_async_copy(own_ref, own_hbm, sem)
     put.start()
     first = core_ref[0] == 0
     for a in range(3):
         part = jnp.dot(
             turned_ref[...],
-            map_ref[(3 - a) * MW : (3 - a + TR) * MW],
-            preferred_element_type=F32,
-        ) + jnp.dot(
-            rest_ref[...],
-            map_ref[(3 - a + TR) * MW : (3 - a + 2 * TR) * MW],
+            map_ref[(3 - a) * MW : (3 - a + 2 * TR) * MW],
             preferred_element_type=F32,
         )
         part = part.reshape(3, CHIPS, 2, CIN, C)
@@ -253,7 +228,7 @@
     put.wait()
 
 
-def filter_part(core, got, turned, before, after):
+def filter_part(core, got, features, before, after):
     return pl.pallas_call(
         filter_kernel,
         out_shape=(
@@ -263,22 +238,21 @@
             jax.ShapeDtypeStruct((REACH * MW, C), BF16),
             jax.ShapeDtypeStruct((MW, C), BF16),
         ),
-        in_specs=[pl.BlockSpec(memory_space=pltpu.SMEM), vmem(), hbm(), vmem(), vmem()],
+        in_specs=[pl.BlockSpec(memory_space=pltpu.SMEM), vmem(), vmem(), vmem(), vmem()],
         out_specs=(vmem(), vmem(), hbm(), vmem(), vmem()),
         scratch_shapes=[
             pltpu.VMEM((32, KDIM), F32),
             pltpu.VMEM((MW, KDIM), BF16),
             pltpu.VMEM((8 * MW, KDIM), BF16),
             pltpu.VMEM(((EXT + 6) * MW, C), BF16),
-            pltpu.VMEM((3 * C, TR * MW), BF16),
-            pltpu.VMEM((3 * C, TR * MW), BF16),
+            pltpu.VMEM((3 * C, 2 * TR * MW), BF16),
             pltpu.VMEM(((TR + 1) * MW, C), F32),
-            pltpu.SemaphoreType.DMA((2,)),
+            pltpu.SemaphoreType.DMA,
         ],
         compiler_params=pltpu.CompilerParams(vmem_limit_bytes=30 << 20),
         name="filter",
         cost_estimate=cost(2 * EXT * MW * KDIM * C + 36 * TR * MW * C * C, 4 << 20),
-    )(core, got, pltpu.with_memory_space_constraint(turned, pltpu.HBM), before, after)
+    )(core, got, features, before, after)
 
 
 def input_kernel(own_ref, above_ref, below_ref, weight_ref, out_ref, shifted_ref):
@@ -337,16 +311,28 @@
     )(parts)
 
 
-def pair_kernel(keep_ref, got_ref, out_ref):
-    out_ref[...] = (keep_ref[...].astype(F32) + got_ref[...].astype(F32)).astype(BF16)
+PIECES = 4
+
+
+def pair_kernel(keep_ref, got_ref, out_hbm, out_ref, sems):
+    step = CHIPS // PIECES
+    sent = []
+    for i in range(PIECES):
+        part = pl.ds(i * step, step)
+        out_ref[part] = (keep_ref[part] + got_ref[part].astype(F32)).astype(BF16)
+        sent.append(pltpu.make_async_copy(out_ref.at[part], out_hbm.at[part], sems.at[i]))
+        sent[-1].start()
+    for copy in sent:
+        copy.wait()
 
 
 def sum_pair(keep, got):
     return pl.pallas_call(
         pair_kernel,
-        out_shape=jax.ShapeDtypeStruct(keep.shape, BF16),
+        out_shape=pltpu.HBM(keep.shape, BF16),
         in_specs=[vmem()] * 2,
-        out_specs=vmem(),
+        out_specs=hbm(),
+        scratch_shapes=[pltpu.VMEM(keep.shape, BF16), pltpu.SemaphoreType.DMA((PIECES,))],
         compiler_params=pltpu.CompilerParams(vmem_limit_bytes=4 << 20),
         name="pair",
         cost_estimate=cost(keep.size, keep.size * 8),
@@ -366,20 +352,20 @@
     before = lax.ppermute(feature_rows[(TR - 1) * MW :], TILE_AXES, up)
     after = lax.ppermute(feature_rows[: REACH * MW], TILE_AXES, down)
     got = exchange(send, TILE_AXES)
-    turned = turn(feature_rows)
     core = lax.axis_index("core").reshape(1)
-    keep, give, own, above, below = filter_part(core, got, turned, before, after)
+    keep, give, own, above, below = filter_part(core, got, feature_rows, before, after)
     taken = lax.ppermute(give, "core", [(0, 1), (1, 0)])
     parts = exchange(sum_pair(keep, taken), "chip")
+    below = lax.ppermute(below, TILE_AXES, down)
+    parts, below = lax.optimization_barrier((parts, below))
+    parts = exchange(sum_parts(parts, (4, NPART, C), BF16), "zl")
     above = lax.ppermute(above, TILE_AXES, up)
-    below = lax.ppermute(below, TILE_AXES, down)
     x_grad = input_part(own, above, below, weight.reshape(9, C, C)).reshape(1, TR, MW, C)
-    parts = exchange(sum_parts(parts, (4, NPART, C), BF16), "zl")
-    parts = sum_parts(parts, (NPART, C), BF16)
-    taken = lax.ppermute(parts, "zh", [(0, 1), (1, 0), (2, 3), (3, 2)])
-    parts = sum_pair(parts, taken)
     parts, x_grad = lax.optimization_barrier((parts, x_grad))
-    parts = lax.all_gather(parts[None], "zh", tiled=True, axis_index_groups=[[0, 3], [1, 2]])
+    parts = sum_parts(parts, (1, NPART, C), BF16)
+    parts = lax.all_gather(parts, "zh", tiled=True, axis_index_groups=[[0, 1], [2, 3]])
+    parts = sum_parts(parts, (1, NPART, C), BF16)
+    parts = lax.all_gather(parts, "zh", tiled=True, axis_index_groups=[[0, 3], [1, 2]])
     total = sum_parts(parts, (NPART, C), F32, 1.0 / IMAGES)
     total = total.reshape(9, CIN, C).transpose(1, 0, 2).reshape(CIN, 3, 3, C)
     return x_grad, total

time: 104 us -> 103 us (level)
  blocking collectives: 8.94 us -> 20 us
  starting transfers between devices: 40 us -> 30.9 us
  Pallas kernels: 17.8 us -> 15.9 us
  waiting for transfers between devices: 34.9 us -> 33 us
    all_gather x1 -> x2, blocking collectives: 8.94 us -> 20 us  [the longest x1 10.4 us: body(): lax.all_gather(parts, 'zh', tiled=True, axis_index_groups=[[0, 1], [2, 3]])]
    ppermute x1 -> x0, starting transfers between devices: 9.1 us -> none  [body(): taken = lax.ppermute(parts, 'zh', [(0, 1), (1, 0), (2, 3), (3, 2)])]
    all_to_all x3, waiting for transfers between devices: 33.3 us -> 27.4 us  [exchange(): return lax.all_to_all(parts, axis, split_axis=0, concat_axis=0, tiled=True)]
    ppermute x1, waiting for transfers between devices: 0.01 us -> 3.23 us  [body(): below = lax.ppermute(below, TILE_AXES, down)]
    pallas_call x3 -> x1, Pallas kernels: 2.57 us -> 0.9 us  [sum_pair(): pl.pallas_call(pair_kernel, out_shape=pltpu.HBM(keep.shape, BF16), in_spe...]
  transfers between devices with their start and end apart: 9 -> 8, of which waited for: 4 -> 6; matrix products, arithmetic and copies ran while one was open for 0% -> 0% of each run, Pallas kernels for 4% -> 3%
where the time goes in v5:
time: 103 us; the launch traced here: 102 us
  waiting for transfers between devices  33 us (32%)
  starting transfers between devices  30.9 us (30%)
  blocking collectives  20 us (19%)
  Pallas kernels  15.9 us (15%)
  local copies, waits for them, and re-layouts  1.29 us (1%)
    all_to_all x3, waiting for transfers between devices, exchange(): return lax.all_to_all(parts, axis, split_axis=0, concat_axis=0, tiled=True)  27.4 us
    all_to_all x3, starting transfers between devices, exchange(): return lax.all_to_all(parts, axis, split_axis=0, concat_axis=0, tiled=True)  20 us
    all_gather x1, blocking collectives, body(): lax.all_gather(parts, 'zh', tiled=True, axis_index_groups=[[0, 1], [2, 3]])  10.4 us
    all_gather x1, blocking collectives, body(): lax.all_gather(parts, 'zh', tiled=True, axis_index_groups=[[0, 3], [1, 2]])  9.57 us
    pallas_call x1, Pallas kernels, filter_part(): pl.pallas_call(filter_kernel, out_shape=(jax.ShapeDtypeStruct((CHIPS, NPA...  7.15 us
    pallas_call x1, Pallas kernels, dispatch(): pl.pallas_call(dispatch_kernel, out_shape=jax.ShapeDtypeStruct((TILES, BL...  4.21 us
    ppermute x1, starting transfers between devices, body(): taken = lax.ppermute(give, 'core', [(0, 1), (1, 0)])  3.26 us
    ppermute x1, waiting for transfers between devices, body(): below = lax.ppermute(below, TILE_AXES, down)  3.23 us
  transfers between devices with their start and end apart: 8, of which 6 were waited for; matrix products, arithmetic and copies ran while one was open for 0% of the time, Pallas kernels for 3%

profile of v5, /device:TPU:32, one launch (start us, length us, event | category | flops | bytes accessed | tf_op | source)
XLA Modules:
  0.0 101.9 jit_solution(15419659477682071390)
XLA Ops:
  0.6 4.2 %dispatch.1 = bf16[32,104,256]{2,1,0:T(8,128)(2,1)} custom-call(s32[1,16]{1,0:T(1,128)} %index_hbm.1, s32[4,20000]{1,0:T(4,128)} %bitcast.25, bf16[49,16,256]{2,1,0:T(8,128)(2,1)} %bitcast.24), custom_call_target="tpu_custom_call" | custom-call | flops 1363148800 | bytes 3145728 | tf_op jit(solution)/shard_map/dispatch/pallas_call | solution.py:123
  4.9 0.0 copy-start
  4.9 7.5 %all-to-all-start = ((bf16[32,104,256]{2,1,0:T(8,128)(2,1)}), bf16[32,104,256]{2,1,0:T(8,128)(2,1)S(1)}, u32[]{:S(2)}, u32[]{:S(2)}) async-start(bf16[32,104,256]{2,1,0:T(8,128)(2,1)} %dispatch.1), calls=%async_computation | async-start | bytes 3407872 | tf_op jit(solution)/shard_map/all_to_all | solution.py:343
  12.4 1.3 %collective-permute-start.1 = (bf16[896,256]{1,0:T(8,128)(2,1)S(1)}, bf16[896,256]{1,0:T(8,128)(2,1)S(1)}, u32[]{:S(2)}, u32[]{:S(2)}) collective-permute-start(bf16[896,256]{1,0:T(8,128)(2,1)S(1)} %bitcast.22), channel_id=1, source_target_pairs={{1,0},{2,1},{3,2},{4,3},{5,4},{6,5},{7,6},{8,7},{9,8},{10,9},{11,1... | collective-permute-start | bytes 1376264 | tf_op jit(solution)/shard_map/ppermute | solution.py:353
  13.7 3.0 %collective-permute-start = (bf16[64,256]{1,0:T(8,128)(2,1)S(1)}, bf16[64,256]{1,0:T(8,128)(2,1)S(1)}, u32[]{:S(2)}, u32[]{:S(2)}) collective-permute-start(bf16[64,256]{1,0:T(8,128)(2,1)S(1)} %slice_bitcast_fusion), channel_id=1, source_target_pairs={{0,1},{1,2},{2,3},{3,4},{4,5},{5,6},{6,7},{7,8},{8,9},{9,10},{10,1... | collective-permute-start | bytes 98312 | tf_op jit(solution)/shard_map/ppermute | solution.py:352
  16.7 0.8 collective-permute-done.before_ref
  17.6 19.3 %all-to-all-done.got_ref = bf16[32,104,256]{2,1,0:T(8,128)(2,1)S(1)} async-done(((bf16[32,104,256]{2,1,0:T(8,128)(2,1)}), bf16[32,104,256]{2,1,0:T(8,128)(2,1)S(1)}, u32[]{:S(2)}, u32[]{:S(2)}) %all-to-all-start) | async-done | bytes 1703968 | tf_op jit(solution)/shard_map/all_to_all | solution.py:343
  36.9 7.2 %filter.1 = (f32[16,72,256]{2,1,0:T(8,128)S(1)}, bf16[16,72,256]{2,1,0:T(8,128)(2,1)S(1)}, f32[1088,256]{1,0:T(8,128)}, bf16[896,256]{1,0:T(8,128)(2,1)S(1)}, bf16[64,256]{1,0:T(8,128)(2,1)S(1)}) custom-call(s32[1]{0:T(128)} %bitcast.core_ref, bf16[32,104,256]{2,1,0:T(8,128)(2,1)S(1)} %all-to-all-done.got_ref, bf16[1024,256]{1,0:T(8,128)(2,1)S(1)} %bitcast.20, ...), custom_call_target="tpu_custom_call" | custom-call | flops 5578424320 | bytes 4194304 | tf_op jit(solution)/shard_map/filter/pallas_call | solution.py:232
  44.1 3.3 %collective-permute-start.2 = (bf16[16,72,256]{2,1,0:T(8,128)(2,1)S(1)}, bf16[16,72,256]{2,1,0:T(8,128)(2,1)S(1)}, u32[]{:S(2)}, u32[]{:S(2)}) collective-permute-start(bf16[16,72,256]{2,1,0:T(8,128)(2,1)S(1)} %get-tuple-element.12), channel_id=1, source_target_pairs={{0,1},{1,0},{2,3},{3,2},{4,5},{5,4},{6,7},{7,6},{8,9},{9,8},{10,11... | collective-permute-start | bytes 1769480 | tf_op jit(solution)/shard_map/ppermute | solution.py:357
  47.3 1.6 %collective-permute-done.2.got_ref = bf16[16,72,256]{2,1,0:T(8,128)(2,1)S(1)} collective-permute-done((bf16[16,72,256]{2,1,0:T(8,128)(2,1)S(1)}, bf16[16,72,256]{2,1,0:T(8,128)(2,1)S(1)}, u32[]{:S(2)}, u32[]{:S(2)}) %collective-permute-start.2) | collective-permute-done | bytes 589856 | tf_op jit(solution)/shard_map/ppermute | solution.py:357
  49.0 0.9 pair.1
  49.9 6.6 %all-to-all-start.1 = ((bf16[16,72,256]{2,1,0:T(8,128)(2,1)}), bf16[16,72,256]{2,1,0:T(8,128)(2,1)S(1)}, u32[]{:S(2)}, u32[]{:S(2)}) async-start(bf16[16,72,256]{2,1,0:T(8,128)(2,1)} %pair.1), calls=%async_computation.1 | async-start | bytes 1179648 | tf_op jit(solution)/shard_map/all_to_all | solution.py:343
  56.4 2.0 %collective-permute-start.4 = (bf16[896,256]{1,0:T(8,128)(2,1)S(1)}, bf16[896,256]{1,0:T(8,128)(2,1)S(1)}, u32[]{:S(2)}, u32[]{:S(2)}) collective-permute-start(bf16[896,256]{1,0:T(8,128)(2,1)S(1)} %get-tuple-element.16), channel_id=1, source_target_pairs={{0,1},{1,2},{2,3},{3,4},{4,5},{5,6},{6,7},{7,8},{8,9},{9,10},{10,1... | collective-permute-start | bytes 1376264 | tf_op jit(solution)/shard_map/ppermute | solution.py:362
  58.5 1.3 %collective-permute-start.3 = (bf16[64,256]{1,0:T(8,128)(2,1)S(1)}, bf16[64,256]{1,0:T(8,128)(2,1)S(1)}, u32[]{:S(2)}, u32[]{:S(2)}) collective-permute-start(bf16[64,256]{1,0:T(8,128)(2,1)S(1)} %get-tuple-element.13), channel_id=1, source_target_pairs={{1,0},{2,1},{3,2},{4,3},{5,4},{6,5},{7,6},{8,7},{9,8},{10,9},{11,1... | collective-permute-start | bytes 98312 | tf_op jit(solution)/shard_map/ppermute | solution.py:359
  59.8 3.2 %collective-permute-done.3.below_ref = bf16[64,256]{1,0:T(8,128)(2,1)S(1)} collective-permute-done((bf16[64,256]{1,0:T(8,128)(2,1)S(1)}, bf16[64,256]{1,0:T(8,128)(2,1)S(1)}, u32[]{:S(2)}, u32[]{:S(2)}) %collective-permute-start.3) | collective-permute-done | bytes 32800 | tf_op jit(solution)/shard_map/ppermute | solution.py:359
  63.0 6.2 %all-to-all-done.1.parts_ref = bf16[16,72,256]{2,1,0:T(8,128)(2,1)S(1)} async-done(((bf16[16,72,256]{2,1,0:T(8,128)(2,1)}), bf16[16,72,256]{2,1,0:T(8,128)(2,1)S(1)}, u32[]{:S(2)}, u32[]{:S(2)}) %all-to-all-start.1) | async-done | bytes 589856 | tf_op jit(solution)/shard_map/all_to_all | solution.py:343
  69.2 0.8 sum.4
  70.0 6.0 %all-to-all-start.2 = ((bf16[4,72,256]{2,1,0:T(8,128)(2,1)}), bf16[4,72,256]{2,1,0:T(8,128)(2,1)S(1)}, u32[]{:S(2)}, u32[]{:S(2)}) async-start(bf16[4,72,256]{2,1,0:T(8,128)(2,1)} %sum.4), calls=%async_computation.2 | async-start | bytes 294912 | tf_op jit(solution)/shard_map/all_to_all | solution.py:343
  76.0 1.2 %copy-done.2 = f32[1088,256]{1,0:T(8,128)S(1)} copy-done((f32[1088,256]{1,0:T(8,128)S(1)}, f32[1088,256]{1,0:T(8,128)}, u32[]{:S(2)}) %copy-start.2) | copy-done | bytes 1114136
  77.2 2.2 %input.1 = bf16[1024,256]{1,0:T(8,128)(2,1)} custom-call(f32[1088,256]{1,0:T(8,128)S(1)} %copy-done.2, bf16[896,256]{1,0:T(8,128)(2,1)S(1)} %collective-permute-done.4.above_ref, bf16[64,256]{1,0:T(8,128)(2,1)S(1)} %collective-permute-done.3.below_ref, bf16[9,256,256]{2,1,0:T(8,128)(2,1)S(1)} %bitcast.21), custom_call_target="tpu_custom_call" | custom-call | flops 1207959552 | bytes 4194304 | tf_op jit(solution)/shard_map/input/pallas_call | solution.py:283
  79.5 1.8 %all-to-all-done.2.parts_ref = bf16[4,72,256]{2,1,0:T(8,128)(2,1)S(1)} async-done(((bf16[4,72,256]{2,1,0:T(8,128)(2,1)}), bf16[4,72,256]{2,1,0:T(8,128)(2,1)S(1)}, u32[]{:S(2)}, u32[]{:S(2)}) %all-to-all-start.2) | async-done | bytes 147488 | tf_op jit(solution)/shard_map/all_to_all | solution.py:343
  81.3 10.4 %all_gather.6.parts_ref = bf16[2,72,256]{2,1,0:T(8,128)(2,1)S(1)} all-gather(bf16[1,72,256]{2,1,0:T(8,128)(2,1)S(1)} %sum.5), channel_id=1, replica_groups={{0,128},{256,384},{1,129},{257,385},{2,130},{258,386},{3,131},{259,387}..., dimensions={0}, use_global_device_ids=true | all-gather | bytes 110592 | tf_op jit(solution)/shard_map/all_gather | solution.py:366
  91.7 9.6 %all_gather.7.parts_ref = bf16[2,72,256]{2,1,0:T(8,128)(2,1)S(1)} all-gather(bf16[1,72,256]{2,1,0:T(8,128)(2,1)S(1)} %sum.6), channel_id=1, replica_groups={{0,384},{128,256},{1,385},{129,257},{2,386},{130,258},{3,387},{131,259}..., dimensions={0}, use_global_device_ids=true | all-gather | bytes 110592 | tf_op jit(solution)/shard_map/all_gather | solution.py:368
  101.3 0.6 sum.7
  (10 shorter events, 0.1 us)
Async XLA Ops:
  4.9 7.5 %copy-start = (bf16[1,16,64,256]{3,2,1,0:T(8,128)(2,1)S(1)}, bf16[1,16,64,256]{3,2,1,0:T(8,128)(2,1)}, u32[]{:S(2)}) copy-start(bf16[1,16,64,256]{3,2,1,0:T(8,128)(2,1)} %param.5) | copy-start | bytes 1572868
  4.9 32.0 %all-to-all-start = ((bf16[32,104,256]{2,1,0:T(8,128)(2,1)}), bf16[32,104,256]{2,1,0:T(8,128)(2,1)S(1)}, u32[]{:S(2)}, u32[]{:S(2)}) async-start(bf16[32,104,256]{2,1,0:T(8,128)(2,1)} %dispatch.1), calls=%async_computation | async-start | bytes 3407872 | tf_op jit(solution)/shard_map/all_to_all | solution.py:343
  12.4 5.2 %collective-permute-start.1 = (bf16[896,256]{1,0:T(8,128)(2,1)S(1)}, bf16[896,256]{1,0:T(8,128)(2,1)S(1)}, u32[]{:S(2)}, u32[]{:S(2)}) collective-permute-start(bf16[896,256]{1,0:T(8,128)(2,1)S(1)} %bitcast.22), channel_id=1, source_target_pairs={{1,0},{2,1},{3,2},{4,3},{5,4},{6,5},{7,6},{8,7},{9,8},{10,9},{11,1... | collective-permute-start | bytes 1376264 | tf_op jit(solution)/shard_map/ppermute | solution.py:353
  13.7 3.9 %collective-permute-start = (bf16[64,256]{1,0:T(8,128)(2,1)S(1)}, bf16[64,256]{1,0:T(8,128)(2,1)S(1)}, u32[]{:S(2)}, u32[]{:S(2)}) collective-permute-start(bf16[64,256]{1,0:T(8,128)(2,1)S(1)} %slice_bitcast_fusion), channel_id=1, source_target_pairs={{0,1},{1,2},{2,3},{3,4},{4,5},{5,6},{6,7},{7,8},{8,9},{9,10},{10,1... | collective-permute-start | bytes 98312 | tf_op jit(solution)/shard_map/ppermute | solution.py:352
  44.1 4.9 %collective-permute-start.2 = (bf16[16,72,256]{2,1,0:T(8,128)(2,1)S(1)}, bf16[16,72,256]{2,1,0:T(8,128)(2,1)S(1)}, u32[]{:S(2)}, u32[]{:S(2)}) collective-permute-start(bf16[16,72,256]{2,1,0:T(8,128)(2,1)S(1)} %get-tuple-element.12), channel_id=1, source_target_pairs={{0,1},{1,0},{2,3},{3,2},{4,5},{5,4},{6,7},{7,6},{8,9},{9,8},{10,11... | collective-permute-start | bytes 1769480 | tf_op jit(solution)/shard_map/ppermute | solution.py:357
  49.9 26.1 %copy-start.1 = (bf16[3,3,256,256]{3,2,1,0:T(8,128)(2,1)S(1)}, bf16[3,3,256,256]{3,2,1,0:T(8,128)(2,1)}, u32[]{:S(2)}) copy-start(bf16[3,3,256,256]{3,2,1,0:T(8,128)(2,1)} %param.6) | copy-start | bytes 3538948
  49.9 19.4 %all-to-all-start.1 = ((bf16[16,72,256]{2,1,0:T(8,128)(2,1)}), bf16[16,72,256]{2,1,0:T(8,128)(2,1)S(1)}, u32[]{:S(2)}, u32[]{:S(2)}) async-start(bf16[16,72,256]{2,1,0:T(8,128)(2,1)} %pair.1), calls=%async_computation.1 | async-start | bytes 1179648 | tf_op jit(solution)/shard_map/all_to_all | solution.py:343
  56.4 19.5 %collective-permute-start.4 = (bf16[896,256]{1,0:T(8,128)(2,1)S(1)}, bf16[896,256]{1,0:T(8,128)(2,1)S(1)}, u32[]{:S(2)}, u32[]{:S(2)}) collective-permute-start(bf16[896,256]{1,0:T(8,128)(2,1)S(1)} %get-tuple-element.16), channel_id=1, source_target_pairs={{0,1},{1,2},{2,3},{3,4},{4,5},{5,6},{6,7},{7,8},{8,9},{9,10},{10,1... | collective-permute-start | bytes 1376264 | tf_op jit(solution)/shard_map/ppermute | solution.py:362
  58.5 4.5 %collective-permute-start.3 = (bf16[64,256]{1,0:T(8,128)(2,1)S(1)}, bf16[64,256]{1,0:T(8,128)(2,1)S(1)}, u32[]{:S(2)}, u32[]{:S(2)}) collective-permute-start(bf16[64,256]{1,0:T(8,128)(2,1)S(1)} %get-tuple-element.13), channel_id=1, source_target_pairs={{1,0},{2,1},{3,2},{4,3},{5,4},{6,5},{7,6},{8,7},{9,8},{10,9},{11,1... | collective-permute-start | bytes 98312 | tf_op jit(solution)/shard_map/ppermute | solution.py:359
  70.0 11.3 %all-to-all-start.2 = ((bf16[4,72,256]{2,1,0:T(8,128)(2,1)}), bf16[4,72,256]{2,1,0:T(8,128)(2,1)S(1)}, u32[]{:S(2)}, u32[]{:S(2)}) async-start(bf16[4,72,256]{2,1,0:T(8,128)(2,1)} %sum.4), calls=%async_computation.2 | async-start | bytes 294912 | tf_op jit(solution)/shard_map/all_to_all | solution.py:343
  76.0 1.2 %copy-start.2 = (f32[1088,256]{1,0:T(8,128)S(1)}, f32[1088,256]{1,0:T(8,128)}, u32[]{:S(2)}) copy-start(f32[1088,256]{1,0:T(8,128)} %get-tuple-element.15.own_ref) | copy-start | bytes 3342340

commit v6 on v5

--- a/solution.py
+++ b/solution.py
@@ -20,6 +20,7 @@
 CHIPS = TILES // 2
 IMAGES = 16
 EXT = TR + REACH - 1
+ROWS = 2
 SLOT = CELLS + 1
 BLOCK = 104
 SLOTS = TILES * CAP
@@ -185,39 +186,50 @@
 
 
 def filter_kernel(
-    core_ref, got_ref, features_ref, before_ref, after_ref,
-    keep_ref, give_ref, own_hbm, above_ref, below_ref,
+    got_ref, features_ref,
+    part_ref, beyond_ref, own_hbm, above_ref, below_ref,
     rows_ref, cols_ref, left_ref, map_ref, turned_ref, own_ref, sem,
 ):
     weights_of(got_ref, rows_ref, cols_ref)
-    features = jnp.concatenate(
-        [features_ref[...], after_ref[...], before_ref[...], jnp.zeros((MW, C), BF16)], axis=0
-    )
-    turn_rows(features, turned_ref)
+    turn_rows(features_ref[...], turned_ref)
     map_ref[: 2 * MW] = jnp.zeros((2 * MW, C), BF16)
     map_ref[(2 + EXT) * MW :] = jnp.zeros((4 * MW, C), BF16)
-    for start, count in ((0, 8), (8, 8), (16, 8), (24, 5)):
+    for start in range(0, EXT, ROWS):
+        count = min(ROWS, EXT - start)
         part = rows_of(start, count, got_ref, rows_ref, cols_ref, left_ref)
-        map_ref[(2 + start) * MW : (2 + start + count) * MW] = part.astype(BF16)
-        if start < TR:
-            own_ref[start * MW : (start + count) * MW] = part
-        if start == 0:
-            below_ref[...] = part[:MW].astype(BF16)
-            map_ref[(4 + EXT) * MW : (5 + EXT) * MW] = part[:MW].astype(BF16)
-        if start == 8:
-            above_ref[:MW] = part[7 * MW :].astype(BF16)
-        if start == 16:
-            own_ref[TR * MW :] = part[:MW]
-            above_ref[MW : 9 * MW] = part.astype(BF16)
-        if start == 24:
-            above_ref[9 * MW :] = part.astype(BF16)
+        rounded = part.astype(BF16)
+        map_ref[(2 + start) * MW : (2 + start + count) * MW] = rounded
+        for h in range(start, start + count):
+            one = slice((h - start) * MW, (h - start + 1) * MW)
+            if h <= TR:
+                own_ref[h * MW : (h + 1) * MW] = part[one]
+            if h == 0:
+                below_ref[...] = rounded[one]
+                map_ref[(4 + EXT) * MW : (5 + EXT) * MW] = rounded[one]
+            if h >= TR - 1:
+                above_ref[(h - TR + 1) * MW : (h - TR + 2) * MW] = rounded[one]
     put = pltpu.make_async_copy(own_ref, own_hbm, sem)
     put.start()
+    beyond_ref[...] = map_ref[(1 + TR) * MW : (3 + 2 * TR) * MW]
+    for a in range(3):
+        part_ref[a] = jnp.dot(
+            turned_ref[...],
+            map_ref[(3 - a) * MW : (3 - a + TR) * MW],
+            preferred_element_type=F32,
+        )
+    put.wait()
+
+
+def beyond_kernel(
+    core_ref, part_ref, beyond_ref, before_ref, after_ref, keep_ref, give_ref, turned_ref
+):
+    rows = jnp.concatenate([after_ref[...], before_ref[...], jnp.zeros((MW, C), BF16)], axis=0)
+    turn_rows(rows, turned_ref)
     first = core_ref[0] == 0
     for a in range(3):
-        part = jnp.dot(
+        part = part_ref[a] + jnp.dot(
             turned_ref[...],
-            map_ref[(3 - a) * MW : (3 - a + 2 * TR) * MW],
+            beyond_ref[(2 - a) * MW : (2 - a + TR) * MW],
             preferred_element_type=F32,
         )
         part = part.reshape(3, CHIPS, 2, CIN, C)
@@ -225,34 +237,49 @@
             at = (a * 3 + e) * CIN
             keep_ref[:, at : at + CIN, :] = jnp.where(first, part[e, :, 0], part[e, :, 1])
             give_ref[:, at : at + CIN, :] = jnp.where(first, part[e, :, 1], part[e, :, 0]).astype(BF16)
-    put.wait()
-
-
-def filter_part(core, got, features, before, after):
-    return pl.pallas_call(
-        filter_kernel,
+
+
+def beyond_part(core, part, beyond, before, after):
+    return pl.pallas_call(
+        beyond_kernel,
         out_shape=(
             jax.ShapeDtypeStruct((CHIPS, NPART, C), F32),
             jax.ShapeDtypeStruct((CHIPS, NPART, C), BF16),
+        ),
+        in_specs=[pl.BlockSpec(memory_space=pltpu.SMEM)] + [vmem()] * 4,
+        out_specs=(vmem(), vmem()),
+        scratch_shapes=[pltpu.VMEM((3 * C, TR * MW), BF16)],
+        compiler_params=pltpu.CompilerParams(vmem_limit_bytes=16 << 20),
+        name="beyond",
+        cost_estimate=cost(18 * TR * MW * C * C, 4 << 20),
+    )(core, part, beyond, before, after)
+
+
+def filter_part(got, features):
+    return pl.pallas_call(
+        filter_kernel,
+        out_shape=(
+            jax.ShapeDtypeStruct((3, 3 * C, C), F32),
+            jax.ShapeDtypeStruct(((TR + 2) * MW, C), BF16),
             pltpu.HBM(((TR + 1) * MW, C), F32),
             jax.ShapeDtypeStruct((REACH * MW, C), BF16),
             jax.ShapeDtypeStruct((MW, C), BF16),
         ),
-        in_specs=[pl.BlockSpec(memory_space=pltpu.SMEM), vmem(), vmem(), vmem(), vmem()],
+        in_specs=[vmem(), vmem()],
         out_specs=(vmem(), vmem(), hbm(), vmem(), vmem()),
         scratch_shapes=[
             pltpu.VMEM((32, KDIM), F32),
             pltpu.VMEM((MW, KDIM), BF16),
-            pltpu.VMEM((8 * MW, KDIM), BF16),
+            pltpu.VMEM((ROWS * MW, KDIM), BF16),
             pltpu.VMEM(((EXT + 6) * MW, C), BF16),
-            pltpu.VMEM((3 * C, 2 * TR * MW), BF16),
+            pltpu.VMEM((3 * C, TR * MW), BF16),
             pltpu.VMEM(((TR + 1) * MW, C), F32),
             pltpu.SemaphoreType.DMA,
         ],
         compiler_params=pltpu.CompilerParams(vmem_limit_bytes=30 << 20),
         name="filter",
         cost_estimate=cost(2 * EXT * MW * KDIM * C + 36 * TR * MW * C * C, 4 << 20),
-    )(core, got, features, before, after)
+    )(got, features)
 
 
 def input_kernel(own_ref, above_ref, below_ref, weight_ref, out_ref, shifted_ref):
@@ -353,7 +380,8 @@
     after = lax.ppermute(feature_rows[: REACH * MW], TILE_AXES, down)
     got = exchange(send, TILE_AXES)
     core = lax.axis_index("core").reshape(1)
-    keep, give, own, above, below = filter_part(core, got, feature_rows, before, after)
+    part, beyond, own, above, below = filter_part(got, feature_rows)
+    keep, give = beyond_part(core, part, beyond, before, after)
     taken = lax.ppermute(give, "core", [(0, 1), (1, 0)])
     parts = exchange(sum_pair(keep, taken), "chip")
     below = lax.ppermute(below, TILE_AXES, down)

time: 103 us -> 98.4 us (0.955)
  starting transfers between devices: 30.9 us -> 25.8 us
    all_to_all x3, starting transfers between devices: 20 us -> 17 us  [exchange(): return lax.all_to_all(parts, axis, split_axis=0, concat_axis=0, tiled=True)]
    ppermute x1, starting transfers between devices: 3.26 us -> 1.92 us  [body(): taken = lax.ppermute(give, 'core', [(0, 1), (1, 0)])]
    all_to_all x3, waiting for transfers between devices: 27.4 us -> 28.5 us  [exchange(): return lax.all_to_all(parts, axis, split_axis=0, concat_axis=0, tiled=True)]
    pallas_call x1 -> x2, Pallas kernels: 7.15 us -> 6.95 us  [the longest x1 5.5 us: filter_part(): pl.pallas_call(filter_kernel, out_shape=(jax.ShapeDtypeStruct((3, 3 * C,...]
  transfers between devices with their start and end apart: 8 -> 8, of which waited for: 6 -> 5; matrix products, arithmetic and copies ran while one was open for 0% -> 1% of each run, Pallas kernels for 3% -> 9%
where the time goes in v6:
time: 98.4 us; the launch traced here: 97.8 us
  waiting for transfers between devices  33.5 us (34%)
  starting transfers between devices  25.8 us (26%)
  blocking collectives  20 us (20%)
  Pallas kernels  15.7 us (16%)
  local copies, waits for them, and re-layouts  2.06 us (2%)
    all_to_all x3, waiting for transfers between devices, exchange(): return lax.all_to_all(parts, axis, split_axis=0, concat_axis=0, tiled=True)  28.5 us
    all_to_all x3, starting transfers between devices, exchange(): return lax.all_to_all(parts, axis, split_axis=0, concat_axis=0, tiled=True)  17 us
    all_gather x1, blocking collectives, body(): lax.all_gather(parts, 'zh', tiled=True, axis_index_groups=[[0, 1], [2, 3]])  10.4 us
    all_gather x1, blocking collectives, body(): lax.all_gather(parts, 'zh', tiled=True, axis_index_groups=[[0, 3], [1, 2]])  9.58 us
    pallas_call x1, Pallas kernels, filter_part(): pl.pallas_call(filter_kernel, out_shape=(jax.ShapeDtypeStruct((3, 3 * C,...  5.5 us
    pallas_call x1, Pallas kernels, dispatch(): pl.pallas_call(dispatch_kernel, out_shape=jax.ShapeDtypeStruct((TILES, BL...  4.21 us
    ppermute x1, waiting for transfers between devices, body(): below = lax.ppermute(below, TILE_AXES, down)  3.05 us
    pallas_call x1, Pallas kernels, input_part(): pl.pallas_call(input_kernel, out_shape=jax.ShapeDtypeStruct((TR * MW, C),...  2.23 us
  transfers between devices with their start and end apart: 8, of which 5 were waited for; matrix products, arithmetic and copies ran while one was open for 1% of the time, Pallas kernels for 9%

profile of v6, /device:TPU:32, one launch (start us, length us, event | category | flops | bytes accessed | tf_op | source)
XLA Modules:
  0.0 97.8 jit_solution(16561585725738633085)
XLA Ops:
  0.6 4.2 %dispatch.1 = bf16[32,104,256]{2,1,0:T(8,128)(2,1)} custom-call(s32[1,16]{1,0:T(1,128)} %index_hbm.1, s32[4,20000]{1,0:T(4,128)} %bitcast.24, bf16[49,16,256]{2,1,0:T(8,128)(2,1)} %bitcast.23), custom_call_target="tpu_custom_call" | custom-call | flops 1363148800 | bytes 3145728 | tf_op jit(solution)/shard_map/dispatch/pallas_call | solution.py:124
  4.9 7.5 %all-to-all-start = ((bf16[32,104,256]{2,1,0:T(8,128)(2,1)}), bf16[32,104,256]{2,1,0:T(8,128)(2,1)S(1)}, u32[]{:S(2)}, u32[]{:S(2)}) async-start(bf16[32,104,256]{2,1,0:T(8,128)(2,1)} %dispatch.1), calls=%async_computation | async-start | bytes 3407872 | tf_op jit(solution)/shard_map/all_to_all | solution.py:370
  12.4 2.2 %collective-permute-start = (bf16[64,256]{1,0:T(8,128)(2,1)S(1)}, bf16[64,256]{1,0:T(8,128)(2,1)S(1)}, u32[]{:S(2)}, u32[]{:S(2)}) collective-permute-start(bf16[64,256]{1,0:T(8,128)(2,1)S(1)} %slice_bitcast_fusion), channel_id=1, source_target_pairs={{0,1},{1,2},{2,3},{3,4},{4,5},{5,6},{6,7},{7,8},{8,9},{9,10},{10,1... | collective-permute-start | bytes 98312 | tf_op jit(solution)/shard_map/ppermute | solution.py:379
  14.5 0.8 slice.14
  15.3 1.3 %collective-permute-start.1 = (bf16[896,256]{1,0:T(8,128)(2,1)}, bf16[896,256]{1,0:T(8,128)(2,1)S(1)}, u32[]{:S(2)}, u32[]{:S(2)}) collective-permute-start(bf16[896,256]{1,0:T(8,128)(2,1)} %bitcast.8), channel_id=1, source_target_pairs={{1,0},{2,1},{3,2},{4,3},{5,4},{6,5},{7,6},{8,7},{9,8},{10,9},{11,1... | collective-permute-start | bytes 1376264 | tf_op jit(solution)/shard_map/ppermute | solution.py:380
  16.6 20.3 %all-to-all-done.got_ref = bf16[32,104,256]{2,1,0:T(8,128)(2,1)S(1)} async-done(((bf16[32,104,256]{2,1,0:T(8,128)(2,1)}), bf16[32,104,256]{2,1,0:T(8,128)(2,1)S(1)}, u32[]{:S(2)}, u32[]{:S(2)}) %all-to-all-start) | async-done | bytes 1703968 | tf_op jit(solution)/shard_map/all_to_all | solution.py:370
  36.9 5.5 %filter.1 = (f32[3,768,256]{2,1,0:T(8,128)S(1)}, bf16[1152,256]{1,0:T(8,128)(2,1)S(1)}, f32[1088,256]{1,0:T(8,128)}, bf16[896,256]{1,0:T(8,128)(2,1)S(1)}, bf16[64,256]{1,0:T(8,128)(2,1)S(1)}) custom-call(bf16[32,104,256]{2,1,0:T(8,128)(2,1)S(1)} %all-to-all-done.got_ref, bf16[1024,256]{1,0:T(8,128)(2,1)S(1)} %bitcast.20), custom_call_target="tpu_custom_call" | custom-call | flops 5578424320 | bytes 4194304 | tf_op jit(solution)/shard_map/filter/pallas_call | solution.py:259
  42.4 1.4 %beyond.1 = (f32[16,72,256]{2,1,0:T(8,128)S(1)}, bf16[16,72,256]{2,1,0:T(8,128)(2,1)S(1)}) custom-call(s32[1]{0:T(128)} %bitcast.core_ref, f32[3,768,256]{2,1,0:T(8,128)S(1)} %get-tuple-element.13.part_ref, bf16[1152,256]{1,0:T(8,128)(2,1)S(1)} %get-tuple-element.14.beyond_ref, bf16[64,256]{1,0:T(8,128)(2,1)S(1)} %collective-permute-done.before_ref, ...), custom_call_target="tpu_custom_call" | custom-call | flops 1207959552 | bytes 4194304 | tf_op jit(solution)/shard_map/beyond/pallas_call | solution.py:243
  43.9 1.9 %collective-permute-start.2 = (bf16[16,72,256]{2,1,0:T(8,128)(2,1)S(1)}, bf16[16,72,256]{2,1,0:T(8,128)(2,1)S(1)}, u32[]{:S(2)}, u32[]{:S(2)}) collective-permute-start(bf16[16,72,256]{2,1,0:T(8,128)(2,1)S(1)} %get-tuple-element.16), channel_id=1, source_target_pairs={{0,1},{1,0},{2,3},{3,2},{4,5},{5,4},{6,7},{7,6},{8,9},{9,8},{10,11... | collective-permute-start | bytes 1769480 | tf_op jit(solution)/shard_map/ppermute | solution.py:385
  45.8 2.0 %collective-permute-done.2.got_ref = bf16[16,72,256]{2,1,0:T(8,128)(2,1)S(1)} collective-permute-done((bf16[16,72,256]{2,1,0:T(8,128)(2,1)S(1)}, bf16[16,72,256]{2,1,0:T(8,128)(2,1)S(1)}, u32[]{:S(2)}, u32[]{:S(2)}) %collective-permute-start.2) | collective-permute-done | bytes 589856 | tf_op jit(solution)/shard_map/ppermute | solution.py:385
  47.8 0.9 pair.1
  48.7 3.6 %all-to-all-start.1 = ((bf16[16,72,256]{2,1,0:T(8,128)(2,1)}), bf16[16,72,256]{2,1,0:T(8,128)(2,1)S(1)}, u32[]{:S(2)}, u32[]{:S(2)}) async-start(bf16[16,72,256]{2,1,0:T(8,128)(2,1)} %pair.1), calls=%async_computation.1 | async-start | bytes 1179648 | tf_op jit(solution)/shard_map/all_to_all | solution.py:370
  52.3 2.1 %collective-permute-start.4 = (bf16[896,256]{1,0:T(8,128)(2,1)S(1)}, bf16[896,256]{1,0:T(8,128)(2,1)S(1)}, u32[]{:S(2)}, u32[]{:S(2)}) collective-permute-start(bf16[896,256]{1,0:T(8,128)(2,1)S(1)} %get-tuple-element.20), channel_id=1, source_target_pairs={{0,1},{1,2},{2,3},{3,4},{4,5},{5,6},{6,7},{7,8},{8,9},{9,10},{10,1... | collective-permute-start | bytes 1376264 | tf_op jit(solution)/shard_map/ppermute | solution.py:390
  54.4 1.3 %collective-permute-start.3 = (bf16[64,256]{1,0:T(8,128)(2,1)S(1)}, bf16[64,256]{1,0:T(8,128)(2,1)S(1)}, u32[]{:S(2)}, u32[]{:S(2)}) collective-permute-start(bf16[64,256]{1,0:T(8,128)(2,1)S(1)} %get-tuple-element.17), channel_id=1, source_target_pairs={{1,0},{2,1},{3,2},{4,3},{5,4},{6,5},{7,6},{8,7},{9,8},{10,9},{11,1... | collective-permute-start | bytes 98312 | tf_op jit(solution)/shard_map/ppermute | solution.py:387
  55.7 3.1 %collective-permute-done.3.below_ref = bf16[64,256]{1,0:T(8,128)(2,1)S(1)} collective-permute-done((bf16[64,256]{1,0:T(8,128)(2,1)S(1)}, bf16[64,256]{1,0:T(8,128)(2,1)S(1)}, u32[]{:S(2)}, u32[]{:S(2)}) %collective-permute-start.3) | collective-permute-done | bytes 32800 | tf_op jit(solution)/shard_map/ppermute | solution.py:387
  58.7 6.4 %all-to-all-done.1.parts_ref = bf16[16,72,256]{2,1,0:T(8,128)(2,1)S(1)} async-done(((bf16[16,72,256]{2,1,0:T(8,128)(2,1)}), bf16[16,72,256]{2,1,0:T(8,128)(2,1)S(1)}, u32[]{:S(2)}, u32[]{:S(2)}) %all-to-all-start.1) | async-done | bytes 589856 | tf_op jit(solution)/shard_map/all_to_all | solution.py:370
  65.1 0.8 sum.4
  65.9 6.0 %all-to-all-start.2 = ((bf16[4,72,256]{2,1,0:T(8,128)(2,1)}), bf16[4,72,256]{2,1,0:T(8,128)(2,1)S(1)}, u32[]{:S(2)}, u32[]{:S(2)}) async-start(bf16[4,72,256]{2,1,0:T(8,128)(2,1)} %sum.4), calls=%async_computation.2 | async-start | bytes 294912 | tf_op jit(solution)/shard_map/all_to_all | solution.py:370
  71.9 1.2 %copy-done.2 = f32[1088,256]{1,0:T(8,128)S(1)} copy-done((f32[1088,256]{1,0:T(8,128)S(1)}, f32[1088,256]{1,0:T(8,128)}, u32[]{:S(2)}) %copy-start.2) | copy-done | bytes 1114136
  73.1 2.2 %input.1 = bf16[1024,256]{1,0:T(8,128)(2,1)} custom-call(f32[1088,256]{1,0:T(8,128)S(1)} %copy-done.2, bf16[896,256]{1,0:T(8,128)(2,1)S(1)} %collective-permute-done.4.above_ref, bf16[64,256]{1,0:T(8,128)(2,1)S(1)} %collective-permute-done.3.below_ref, bf16[9,256,256]{2,1,0:T(8,128)(2,1)S(1)} %bitcast.21), custom_call_target="tpu_custom_call" | custom-call | flops 1207959552 | bytes 4194304 | tf_op jit(solution)/shard_map/input/pallas_call | solution.py:310
  75.3 1.8 %all-to-all-done.2.parts_ref = bf16[4,72,256]{2,1,0:T(8,128)(2,1)S(1)} async-done(((bf16[4,72,256]{2,1,0:T(8,128)(2,1)}), bf16[4,72,256]{2,1,0:T(8,128)(2,1)S(1)}, u32[]{:S(2)}, u32[]{:S(2)}) %all-to-all-start.2) | async-done | bytes 147488 | tf_op jit(solution)/shard_map/all_to_all | solution.py:370
  77.2 10.4 %all_gather.6.parts_ref = bf16[2,72,256]{2,1,0:T(8,128)(2,1)S(1)} all-gather(bf16[1,72,256]{2,1,0:T(8,128)(2,1)S(1)} %sum.5), channel_id=1, replica_groups={{0,128},{256,384},{1,129},{257,385},{2,130},{258,386},{3,131},{259,387}..., dimensions={0}, use_global_device_ids=true | all-gather | bytes 110592 | tf_op jit(solution)/shard_map/all_gather | solution.py:394
  87.6 9.6 %all_gather.7.parts_ref = bf16[2,72,256]{2,1,0:T(8,128)(2,1)S(1)} all-gather(bf16[1,72,256]{2,1,0:T(8,128)(2,1)S(1)} %sum.6), channel_id=1, replica_groups={{0,384},{128,256},{1,385},{129,257},{2,386},{130,258},{3,387},{131,259}..., dimensions={0}, use_global_device_ids=true | all-gather | bytes 110592 | tf_op jit(solution)/shard_map/all_gather | solution.py:396
  97.2 0.6 sum.7
  (11 shorter events, 0.1 us)
Async XLA Ops:
  4.9 7.5 %copy-start = (bf16[1,16,64,256]{3,2,1,0:T(8,128)(2,1)S(1)}, bf16[1,16,64,256]{3,2,1,0:T(8,128)(2,1)}, u32[]{:S(2)}) copy-start(bf16[1,16,64,256]{3,2,1,0:T(8,128)(2,1)} %param.5) | copy-start | bytes 1572868
  4.9 32.1 %all-to-all-start = ((bf16[32,104,256]{2,1,0:T(8,128)(2,1)}), bf16[32,104,256]{2,1,0:T(8,128)(2,1)S(1)}, u32[]{:S(2)}, u32[]{:S(2)}) async-start(bf16[32,104,256]{2,1,0:T(8,128)(2,1)} %dispatch.1), calls=%async_computation | async-start | bytes 3407872 | tf_op jit(solution)/shard_map/all_to_all | solution.py:370
  12.4 30.1 %collective-permute-start = (bf16[64,256]{1,0:T(8,128)(2,1)S(1)}, bf16[64,256]{1,0:T(8,128)(2,1)S(1)}, u32[]{:S(2)}, u32[]{:S(2)}) collective-permute-start(bf16[64,256]{1,0:T(8,128)(2,1)S(1)} %slice_bitcast_fusion), channel_id=1, source_target_pairs={{0,1},{1,2},{2,3},{3,4},{4,5},{5,6},{6,7},{7,8},{8,9},{9,10},{10,1... | collective-permute-start | bytes 98312 | tf_op jit(solution)/shard_map/ppermute | solution.py:379
  15.3 27.1 %collective-permute-start.1 = (bf16[896,256]{1,0:T(8,128)(2,1)}, bf16[896,256]{1,0:T(8,128)(2,1)S(1)}, u32[]{:S(2)}, u32[]{:S(2)}) collective-permute-start(bf16[896,256]{1,0:T(8,128)(2,1)} %bitcast.8), channel_id=1, source_target_pairs={{1,0},{2,1},{3,2},{4,3},{5,4},{6,5},{7,6},{8,7},{9,8},{10,9},{11,1... | collective-permute-start | bytes 1376264 | tf_op jit(solution)/shard_map/ppermute | solution.py:380
  43.9 3.9 %collective-permute-start.2 = (bf16[16,72,256]{2,1,0:T(8,128)(2,1)S(1)}, bf16[16,72,256]{2,1,0:T(8,128)(2,1)S(1)}, u32[]{:S(2)}, u32[]{:S(2)}) collective-permute-start(bf16[16,72,256]{2,1,0:T(8,128)(2,1)S(1)} %get-tuple-element.16), channel_id=1, source_target_pairs={{0,1},{1,0},{2,3},{3,2},{4,5},{5,4},{6,7},{7,6},{8,9},{9,8},{10,11... | collective-permute-start | bytes 1769480 | tf_op jit(solution)/shard_map/ppermute | solution.py:385
  47.8 24.1 %copy-start.1 = (bf16[3,3,256,256]{3,2,1,0:T(8,128)(2,1)S(1)}, bf16[3,3,256,256]{3,2,1,0:T(8,128)(2,1)}, u32[]{:S(2)}) copy-start(bf16[3,3,256,256]{3,2,1,0:T(8,128)(2,1)} %param.6) | copy-start | bytes 3538948
  48.7 16.4 %all-to-all-start.1 = ((bf16[16,72,256]{2,1,0:T(8,128)(2,1)}), bf16[16,72,256]{2,1,0:T(8,128)(2,1)S(1)}, u32[]{:S(2)}, u32[]{:S(2)}) async-start(bf16[16,72,256]{2,1,0:T(8,128)(2,1)} %pair.1), calls=%async_computation.1 | async-start | bytes 1179648 | tf_op jit(solution)/shard_map/all_to_all | solution.py:370
  52.3 19.5 %collective-permute-start.4 = (bf16[896,256]{1,0:T(8,128)(2,1)S(1)}, bf16[896,256]{1,0:T(8,128)(2,1)S(1)}, u32[]{:S(2)}, u32[]{:S(2)}) collective-permute-start(bf16[896,256]{1,0:T(8,128)(2,1)S(1)} %get-tuple-element.20), channel_id=1, source_target_pairs={{0,1},{1,2},{2,3},{3,4},{4,5},{5,6},{6,7},{7,8},{8,9},{9,10},{10,1... | collective-permute-start | bytes 1376264 | tf_op jit(solution)/shard_map/ppermute | solution.py:390
  54.4 4.4 %collective-permute-start.3 = (bf16[64,256]{1,0:T(8,128)(2,1)S(1)}, bf16[64,256]{1,0:T(8,128)(2,1)S(1)}, u32[]{:S(2)}, u32[]{:S(2)}) collective-permute-start(bf16[64,256]{1,0:T(8,128)(2,1)S(1)} %get-tuple-element.17), channel_id=1, source_target_pairs={{1,0},{2,1},{3,2},{4,3},{5,4},{6,5},{7,6},{8,7},{9,8},{10,9},{11,1... | collective-permute-start | bytes 98312 | tf_op jit(solution)/shard_map/ppermute | solution.py:387
  65.9 11.3 %all-to-all-start.2 = ((bf16[4,72,256]{2,1,0:T(8,128)(2,1)}), bf16[4,72,256]{2,1,0:T(8,128)(2,1)S(1)}, u32[]{:S(2)}, u32[]{:S(2)}) async-start(bf16[4,72,256]{2,1,0:T(8,128)(2,1)} %sum.4), calls=%async_computation.2 | async-start | bytes 294912 | tf_op jit(solution)/shard_map/all_to_all | solution.py:370
  71.9 1.2 %copy-start.2 = (f32[1088,256]{1,0:T(8,128)S(1)}, f32[1088,256]{1,0:T(8,128)}, u32[]{:S(2)}) copy-start(f32[1088,256]{1,0:T(8,128)} %get-tuple-element.19.own_ref) | copy-start | bytes 3342340

commit v7 on v6

--- a/solution.py
+++ b/solution.py
@@ -20,7 +20,7 @@
 CHIPS = TILES // 2
 IMAGES = 16
 EXT = TR + REACH - 1
-ROWS = 2
+ROWS = 3
 SLOT = CELLS + 1
 BLOCK = 104
 SLOTS = TILES * CAP
@@ -39,10 +39,6 @@
     return pl.BlockSpec(memory_space=pltpu.VMEM)
 
 
-def hbm():
-    return pl.BlockSpec(memory_space=pltpu.HBM)
-
-
 def cost(flops, moved):
     return pl.CostEstimate(flops=flops, bytes_accessed=moved, transcendentals=0)
 
@@ -51,18 +47,7 @@
     return lax.broadcasted_iota(I32, shape, dim)
 
 
-def dispatch_kernel(
-    index_hbm, boxes_hbm, grad_hbm, out_hbm, index_ref, boxes_ref, source_ref, sent_ref, sems
-):
-    copies = [
-        pltpu.make_async_copy(index_hbm, index_ref, sems.at[0]),
-        pltpu.make_async_copy(boxes_hbm, boxes_ref, sems.at[1]),
-        pltpu.make_async_copy(grad_hbm, source_ref.at[:CELLS], sems.at[2]),
-    ]
-    for copy in copies:
-        copy.start()
-    copies[0].wait()
-    copies[1].wait()
+def dispatch_kernel(index_ref, boxes_ref, grad_ref, out_ref):
     lane16 = iota((4, ROI_DEV), 1)
     lanes = iota((4, LANES), 1)
     tail = jnp.concatenate(
@@ -95,48 +80,35 @@
     box_rows = jnp.zeros((ROI_DEV, C), F32)
     for f, row in enumerate((local_top, chosen[1:2], chosen[2:3], chosen[3:4])):
         box_rows = jnp.where(field == f, column(row), box_rows)
-    source_ref[CELLS] = box_rows.astype(BF16)
     depth = SLOT * ROI_DEV
     wide = jnp.concatenate([owner, rank, jnp.zeros((6, ROI_DEV), F32)], axis=0).astype(BF16)
     spreading = iota((ROI_DEV, depth), 1) % ROI_DEV == iota((ROI_DEV, depth), 0)
     spread = jnp.dot(wide, spreading.astype(F32).astype(BF16), preferred_element_type=F32)
     cell = (iota((1, depth), 1) // ROI_DEV).astype(F32)
     goal = (spread[0:1] * BLOCK + spread[1:2] * SLOT + cell).astype(I32)
-    copies[2].wait()
-    source = source_ref[...].reshape(depth, C)
+    source = jnp.concatenate(
+        [grad_ref[...].reshape(CELLS * ROI_DEV, C), box_rows.astype(BF16)], axis=0
+    )
     step = KDIM // 8
-    sent = []
     for m in range(8):
-        part = pl.ds(m * (TILES // 8), TILES // 8)
         place = iota((step, depth), 0) == goal - m * step
-        sent_ref[part] = (
+        out_ref[m * (TILES // 8) : (m + 1) * (TILES // 8)] = (
             jnp.dot(place.astype(F32).astype(BF16), source, preferred_element_type=F32)
             .astype(BF16)
             .reshape(TILES // 8, BLOCK, C)
         )
-        sent.append(pltpu.make_async_copy(sent_ref.at[part], out_hbm.at[part], sems.at[3 + m]))
-        sent[-1].start()
-    for copy in sent:
-        copy.wait()
 
 
 def dispatch(index, boxes_t, grads):
     return pl.pallas_call(
         dispatch_kernel,
         out_shape=jax.ShapeDtypeStruct((TILES, BLOCK, C), BF16),
-        in_specs=[pl.BlockSpec(memory_space=pl.ANY)] * 3,
-        out_specs=pl.BlockSpec(memory_space=pl.ANY),
-        scratch_shapes=[
-            pltpu.SMEM((1, ROI_DEV), I32),
-            pltpu.VMEM((4, PROPS), I32),
-            pltpu.VMEM((SLOT, ROI_DEV, C), BF16),
-            pltpu.VMEM((TILES, BLOCK, C), BF16),
-            pltpu.SemaphoreType.DMA((11,)),
-        ],
+        in_specs=[pl.BlockSpec(memory_space=pltpu.SMEM), vmem(), vmem()],
+        out_specs=vmem(),
         compiler_params=pltpu.CompilerParams(vmem_limit_bytes=60 << 20),
         name="dispatch",
         cost_estimate=cost(2 * KDIM * SLOT * ROI_DEV * C, 3 << 20),
-    )(*(pltpu.with_memory_space_constraint(x, pltpu.HBM) for x in (index, boxes_t, grads)))
+    )(index, boxes_t, grads)
 
 
 def weights_of(got_ref, rows_ref, cols_ref):
@@ -187,8 +159,8 @@
 
 def filter_kernel(
     got_ref, features_ref,
-    part_ref, beyond_ref, own_hbm, above_ref, below_ref,
-    rows_ref, cols_ref, left_ref, map_ref, turned_ref, own_ref, sem,
+    part_ref, beyond_ref, own_ref, above_ref, below_ref,
+    rows_ref, cols_ref, left_ref, map_ref, turned_ref,
 ):
     weights_of(got_ref, rows_ref, cols_ref)
     turn_rows(features_ref[...], turned_ref)
@@ -208,8 +180,6 @@
                 map_ref[(4 + EXT) * MW : (5 + EXT) * MW] = rounded[one]
             if h >= TR - 1:
                 above_ref[(h - TR + 1) * MW : (h - TR + 2) * MW] = rounded[one]
-    put = pltpu.make_async_copy(own_ref, own_hbm, sem)
-    put.start()
     beyond_ref[...] = map_ref[(1 + TR) * MW : (3 + 2 * TR) * MW]
     for a in range(3):
         part_ref[a] = jnp.dot(
@@ -217,7 +187,6 @@
             map_ref[(3 - a) * MW : (3 - a + TR) * MW],
             preferred_element_type=F32,
         )
-    put.wait()
 
 
 def beyond_kernel(
@@ -261,20 +230,18 @@
         out_shape=(
             jax.ShapeDtypeStruct((3, 3 * C, C), F32),
             jax.ShapeDtypeStruct(((TR + 2) * MW, C), BF16),
-            pltpu.HBM(((TR + 1) * MW, C), F32),
+            jax.ShapeDtypeStruct(((TR + 1) * MW, C), F32),
             jax.ShapeDtypeStruct((REACH * MW, C), BF16),
             jax.ShapeDtypeStruct((MW, C), BF16),
         ),
         in_specs=[vmem(), vmem()],
-        out_specs=(vmem(), vmem(), hbm(), vmem(), vmem()),
+        out_specs=(vmem(),) * 5,
         scratch_shapes=[
             pltpu.VMEM((32, KDIM), F32),
             pltpu.VMEM((MW, KDIM), BF16),
             pltpu.VMEM((ROWS * MW, KDIM), BF16),
             pltpu.VMEM(((EXT + 6) * MW, C), BF16),
             pltpu.VMEM((3 * C, TR * MW), BF16),
-            pltpu.VMEM(((TR + 1) * MW, C), F32),
-            pltpu.SemaphoreType.DMA,
         ],
         compiler_params=pltpu.CompilerParams(vmem_limit_bytes=30 << 20),
         name="filter",
@@ -338,28 +305,16 @@
     )(parts)
 
 
-PIECES = 4
-
-
-def pair_kernel(keep_ref, got_ref, out_hbm, out_ref, sems):
-    step = CHIPS // PIECES
-    sent = []
-    for i in range(PIECES):
-        part = pl.ds(i * step, step)
-        out_ref[part] = (keep_ref[part] + got_ref[part].astype(F32)).astype(BF16)
-        sent.append(pltpu.make_async_copy(out_ref.at[part], out_hbm.at[part], sems.at[i]))
-        sent[-1].start()
-    for copy in sent:
-        copy.wait()
+def pair_kernel(keep_ref, got_ref, out_ref):
+    out_ref[...] = (keep_ref[...] + got_ref[...].astype(F32)).astype(BF16)
 
 
 def sum_pair(keep, got):
     return pl.pallas_call(
         pair_kernel,
-        out_shape=pltpu.HBM(keep.shape, BF16),
+        out_shape=jax.ShapeDtypeStruct(keep.shape, BF16),
         in_specs=[vmem()] * 2,
-        out_specs=hbm(),
-        scratch_shapes=[pltpu.VMEM(keep.shape, BF16), pltpu.SemaphoreType.DMA((PIECES,))],
+        out_specs=vmem(),
         compiler_params=pltpu.CompilerParams(vmem_limit_bytes=4 << 20),
         name="pair",
         cost_estimate=cost(keep.size, keep.size * 8),

time: 98.4 us -> 98.6 us (level)
  transfers between devices with their start and end apart: 8 -> 8, of which waited for: 5 -> 5; matrix products, arithmetic and copies ran while one was open for 1% -> 1% of each run, Pallas kernels for 9% -> 8%
where the time goes in v7:
time: 98.6 us; the launch traced here: 98 us
  waiting for transfers between devices  33.5 us (34%)
  starting transfers between devices  25.8 us (26%)
  blocking collectives  20 us (20%)
  Pallas kernels  15.9 us (16%)
  local copies, waits for them, and re-layouts  2.06 us (2%)
    all_to_all x3, waiting for transfers between devices, exchange(): return lax.all_to_all(parts, axis, split_axis=0, concat_axis=0, tiled=True)  28.5 us
    all_to_all x3, starting transfers between devices, exchange(): return lax.all_to_all(parts, axis, split_axis=0, concat_axis=0, tiled=True)  17.1 us
    all_gather x1, blocking collectives, body(): lax.all_gather(parts, 'zh', tiled=True, axis_index_groups=[[0, 1], [2, 3]])  10.4 us
    all_gather x1, blocking collectives, body(): lax.all_gather(parts, 'zh', tiled=True, axis_index_groups=[[0, 3], [1, 2]])  9.58 us
    pallas_call x1, Pallas kernels, filter_part(): pl.pallas_call(filter_kernel, out_shape=(jax.ShapeDtypeStruct((3, 3 * C,...  5.31 us
    pallas_call x1, Pallas kernels, dispatch(): pl.pallas_call(dispatch_kernel, out_shape=jax.ShapeDtypeStruct((TILES, BL...  4.61 us
    ppermute x1, waiting for transfers between devices, body(): below = lax.ppermute(below, TILE_AXES, down)  3.05 us
    pallas_call x1, Pallas kernels, input_part(): pl.pallas_call(input_kernel, out_shape=jax.ShapeDtypeStruct((TR * MW, C),...  2.23 us
  transfers between devices with their start and end apart: 8, of which 5 were waited for; matrix products, arithmetic and copies ran while one was open for 1% of the time, Pallas kernels for 8%

profile of v7, /device:TPU:32, one launch (start us, length us, event | category | flops | bytes accessed | tf_op | source)
XLA Modules:
  0.0 98.0 jit_solution(15583553252439425864)
XLA Ops:
  0.6 4.6 %dispatch.1 = bf16[32,104,256]{2,1,0:T(8,128)(2,1)} custom-call(s32[1,16]{1,0:T(1,128)} %index_ref.1, s32[4,20000]{1,0:T(4,128)} %bitcast.24, bf16[49,16,256]{2,1,0:T(8,128)(2,1)} %bitcast.23), custom_call_target="tpu_custom_call" | custom-call | flops 1363148800 | bytes 3145728 | tf_op jit(solution)/shard_map/dispatch/pallas_call | solution.py:103
  5.2 7.5 %all-to-all-start = ((bf16[32,104,256]{2,1,0:T(8,128)(2,1)}), bf16[32,104,256]{2,1,0:T(8,128)(2,1)S(1)}, u32[]{:S(2)}, u32[]{:S(2)}) async-start(bf16[32,104,256]{2,1,0:T(8,128)(2,1)} %dispatch.1), calls=%async_computation | async-start | bytes 3407872 | tf_op jit(solution)/shard_map/all_to_all | solution.py:325
  12.7 2.2 %collective-permute-start = (bf16[64,256]{1,0:T(8,128)(2,1)S(1)}, bf16[64,256]{1,0:T(8,128)(2,1)S(1)}, u32[]{:S(2)}, u32[]{:S(2)}) collective-permute-start(bf16[64,256]{1,0:T(8,128)(2,1)S(1)} %slice_bitcast_fusion), channel_id=1, source_target_pairs={{0,1},{1,2},{2,3},{3,4},{4,5},{5,6},{6,7},{7,8},{8,9},{9,10},{10,1... | collective-permute-start | bytes 98312 | tf_op jit(solution)/shard_map/ppermute | solution.py:334
  14.9 0.8 slice.14
  15.7 1.3 %collective-permute-start.1 = (bf16[896,256]{1,0:T(8,128)(2,1)}, bf16[896,256]{1,0:T(8,128)(2,1)S(1)}, u32[]{:S(2)}, u32[]{:S(2)}) collective-permute-start(bf16[896,256]{1,0:T(8,128)(2,1)} %bitcast.8), channel_id=1, source_target_pairs={{1,0},{2,1},{3,2},{4,3},{5,4},{6,5},{7,6},{8,7},{9,8},{10,9},{11,1... | collective-permute-start | bytes 1376264 | tf_op jit(solution)/shard_map/ppermute | solution.py:335
  17.0 20.3 %all-to-all-done.got_ref = bf16[32,104,256]{2,1,0:T(8,128)(2,1)S(1)} async-done(((bf16[32,104,256]{2,1,0:T(8,128)(2,1)}), bf16[32,104,256]{2,1,0:T(8,128)(2,1)S(1)}, u32[]{:S(2)}, u32[]{:S(2)}) %all-to-all-start) | async-done | bytes 1703968 | tf_op jit(solution)/shard_map/all_to_all | solution.py:325
  37.3 5.3 %filter.1 = (f32[3,768,256]{2,1,0:T(8,128)S(1)}, bf16[1152,256]{1,0:T(8,128)(2,1)S(1)}, f32[1088,256]{1,0:T(8,128)S(1)}, bf16[896,256]{1,0:T(8,128)(2,1)S(1)}, bf16[64,256]{1,0:T(8,128)(2,1)S(1)}) custom-call(bf16[32,104,256]{2,1,0:T(8,128)(2,1)S(1)} %all-to-all-done.got_ref, bf16[1024,256]{1,0:T(8,128)(2,1)S(1)} %bitcast.20), custom_call_target="tpu_custom_call" | custom-call | flops 5578424320 | bytes 4194304 | tf_op jit(solution)/shard_map/filter/pallas_call | solution.py:228
  42.6 1.4 %beyond.1 = (f32[16,72,256]{2,1,0:T(8,128)S(1)}, bf16[16,72,256]{2,1,0:T(8,128)(2,1)S(1)}) custom-call(s32[1]{0:T(128)} %bitcast.core_ref, f32[3,768,256]{2,1,0:T(8,128)S(1)} %get-tuple-element.13.part_ref, bf16[1152,256]{1,0:T(8,128)(2,1)S(1)} %get-tuple-element.14.beyond_ref, bf16[64,256]{1,0:T(8,128)(2,1)S(1)} %collective-permute-done.before_ref, ...), custom_call_target="tpu_custom_call" | custom-call | flops 1207959552 | bytes 4194304 | tf_op jit(solution)/shard_map/beyond/pallas_call | solution.py:212
  44.1 1.9 %collective-permute-start.2 = (bf16[16,72,256]{2,1,0:T(8,128)(2,1)S(1)}, bf16[16,72,256]{2,1,0:T(8,128)(2,1)S(1)}, u32[]{:S(2)}, u32[]{:S(2)}) collective-permute-start(bf16[16,72,256]{2,1,0:T(8,128)(2,1)S(1)} %get-tuple-element.16), channel_id=1, source_target_pairs={{0,1},{1,0},{2,3},{3,2},{4,5},{5,4},{6,7},{7,6},{8,9},{9,8},{10,11... | collective-permute-start | bytes 1769480 | tf_op jit(solution)/shard_map/ppermute | solution.py:340
  46.0 2.0 %collective-permute-done.2.got_ref = bf16[16,72,256]{2,1,0:T(8,128)(2,1)S(1)} collective-permute-done((bf16[16,72,256]{2,1,0:T(8,128)(2,1)S(1)}, bf16[16,72,256]{2,1,0:T(8,128)(2,1)S(1)}, u32[]{:S(2)}, u32[]{:S(2)}) %collective-permute-start.2) | collective-permute-done | bytes 589856 | tf_op jit(solution)/shard_map/ppermute | solution.py:340
  48.0 0.9 pair.1
  48.9 3.6 %all-to-all-start.1 = ((bf16[16,72,256]{2,1,0:T(8,128)(2,1)}), bf16[16,72,256]{2,1,0:T(8,128)(2,1)S(1)}, u32[]{:S(2)}, u32[]{:S(2)}) async-start(bf16[16,72,256]{2,1,0:T(8,128)(2,1)} %pair.1), calls=%async_computation.1 | async-start | bytes 1179648 | tf_op jit(solution)/shard_map/all_to_all | solution.py:325
  52.5 2.1 %collective-permute-start.4 = (bf16[896,256]{1,0:T(8,128)(2,1)S(1)}, bf16[896,256]{1,0:T(8,128)(2,1)S(1)}, u32[]{:S(2)}, u32[]{:S(2)}) collective-permute-start(bf16[896,256]{1,0:T(8,128)(2,1)S(1)} %get-tuple-element.20), channel_id=1, source_target_pairs={{0,1},{1,2},{2,3},{3,4},{4,5},{5,6},{6,7},{7,8},{8,9},{9,10},{10,1... | collective-permute-start | bytes 1376264 | tf_op jit(solution)/shard_map/ppermute | solution.py:345
  54.6 1.3 %collective-permute-start.3 = (bf16[64,256]{1,0:T(8,128)(2,1)S(1)}, bf16[64,256]{1,0:T(8,128)(2,1)S(1)}, u32[]{:S(2)}, u32[]{:S(2)}) collective-permute-start(bf16[64,256]{1,0:T(8,128)(2,1)S(1)} %get-tuple-element.17), channel_id=1, source_target_pairs={{1,0},{2,1},{3,2},{4,3},{5,4},{6,5},{7,6},{8,7},{9,8},{10,9},{11,1... | collective-permute-start | bytes 98312 | tf_op jit(solution)/shard_map/ppermute | solution.py:342
  55.9 3.1 %collective-permute-done.3.below_ref = bf16[64,256]{1,0:T(8,128)(2,1)S(1)} collective-permute-done((bf16[64,256]{1,0:T(8,128)(2,1)S(1)}, bf16[64,256]{1,0:T(8,128)(2,1)S(1)}, u32[]{:S(2)}, u32[]{:S(2)}) %collective-permute-start.3) | collective-permute-done | bytes 32800 | tf_op jit(solution)/shard_map/ppermute | solution.py:342
  58.9 6.4 %all-to-all-done.1.parts_ref = bf16[16,72,256]{2,1,0:T(8,128)(2,1)S(1)} async-done(((bf16[16,72,256]{2,1,0:T(8,128)(2,1)}), bf16[16,72,256]{2,1,0:T(8,128)(2,1)S(1)}, u32[]{:S(2)}, u32[]{:S(2)}) %all-to-all-start.1) | async-done | bytes 589856 | tf_op jit(solution)/shard_map/all_to_all | solution.py:325
  65.3 0.7 sum.4
  66.0 6.0 %all-to-all-start.2 = ((bf16[4,72,256]{2,1,0:T(8,128)(2,1)}), bf16[4,72,256]{2,1,0:T(8,128)(2,1)S(1)}, u32[]{:S(2)}, u32[]{:S(2)}) async-start(bf16[4,72,256]{2,1,0:T(8,128)(2,1)} %sum.4), calls=%async_computation.2 | async-start | bytes 294912 | tf_op jit(solution)/shard_map/all_to_all | solution.py:325
  72.1 1.2 %copy-done.3 = f32[1088,256]{1,0:T(8,128)S(1)} copy-done((f32[1088,256]{1,0:T(8,128)S(1)}, f32[1088,256]{1,0:T(8,128)}, u32[]{:S(2)}) %copy-start.3) | copy-done | bytes 1114136
  73.3 2.2 %input.1 = bf16[1024,256]{1,0:T(8,128)(2,1)} custom-call(f32[1088,256]{1,0:T(8,128)S(1)} %copy-done.3, bf16[896,256]{1,0:T(8,128)(2,1)S(1)} %collective-permute-done.4.above_ref, bf16[64,256]{1,0:T(8,128)(2,1)S(1)} %collective-permute-done.3.below_ref, bf16[9,256,256]{2,1,0:T(8,128)(2,1)S(1)} %bitcast.21), custom_call_target="tpu_custom_call" | custom-call | flops 1207959552 | bytes 4194304 | tf_op jit(solution)/shard_map/input/pallas_call | solution.py:277
  75.5 1.8 %all-to-all-done.2.parts_ref = bf16[4,72,256]{2,1,0:T(8,128)(2,1)S(1)} async-done(((bf16[4,72,256]{2,1,0:T(8,128)(2,1)}), bf16[4,72,256]{2,1,0:T(8,128)(2,1)S(1)}, u32[]{:S(2)}, u32[]{:S(2)}) %all-to-all-start.2) | async-done | bytes 147488 | tf_op jit(solution)/shard_map/all_to_all | solution.py:325
  77.4 10.4 %all_gather.6.parts_ref = bf16[2,72,256]{2,1,0:T(8,128)(2,1)S(1)} all-gather(bf16[1,72,256]{2,1,0:T(8,128)(2,1)S(1)} %sum.5), channel_id=1, replica_groups={{0,128},{256,384},{1,129},{257,385},{2,130},{258,386},{3,131},{259,387}..., dimensions={0}, use_global_device_ids=true | all-gather | bytes 110592 | tf_op jit(solution)/shard_map/all_gather | solution.py:349
  87.8 9.6 %all_gather.7.parts_ref = bf16[2,72,256]{2,1,0:T(8,128)(2,1)S(1)} all-gather(bf16[1,72,256]{2,1,0:T(8,128)(2,1)S(1)} %sum.6), channel_id=1, replica_groups={{0,384},{128,256},{1,385},{129,257},{2,386},{130,258},{3,387},{131,259}..., dimensions={0}, use_global_device_ids=true | all-gather | bytes 110592 | tf_op jit(solution)/shard_map/all_gather | solution.py:351
  97.3 0.6 sum.7
  (13 shorter events, 0.1 us)
Async XLA Ops:
  5.2 7.5 %copy-start = (bf16[1,16,64,256]{3,2,1,0:T(8,128)(2,1)S(1)}, bf16[1,16,64,256]{3,2,1,0:T(8,128)(2,1)}, u32[]{:S(2)}) copy-start(bf16[1,16,64,256]{3,2,1,0:T(8,128)(2,1)} %param.5) | copy-start | bytes 1572868
  5.2 32.0 %all-to-all-start = ((bf16[32,104,256]{2,1,0:T(8,128)(2,1)}), bf16[32,104,256]{2,1,0:T(8,128)(2,1)S(1)}, u32[]{:S(2)}, u32[]{:S(2)}) async-start(bf16[32,104,256]{2,1,0:T(8,128)(2,1)} %dispatch.1), calls=%async_computation | async-start | bytes 3407872 | tf_op jit(solution)/shard_map/all_to_all | solution.py:325
  12.7 29.9 %collective-permute-start = (bf16[64,256]{1,0:T(8,128)(2,1)S(1)}, bf16[64,256]{1,0:T(8,128)(2,1)S(1)}, u32[]{:S(2)}, u32[]{:S(2)}) collective-permute-start(bf16[64,256]{1,0:T(8,128)(2,1)S(1)} %slice_bitcast_fusion), channel_id=1, source_target_pairs={{0,1},{1,2},{2,3},{3,4},{4,5},{5,6},{6,7},{7,8},{8,9},{9,10},{10,1... | collective-permute-start | bytes 98312 | tf_op jit(solution)/shard_map/ppermute | solution.py:334
  15.7 26.9 %collective-permute-start.1 = (bf16[896,256]{1,0:T(8,128)(2,1)}, bf16[896,256]{1,0:T(8,128)(2,1)S(1)}, u32[]{:S(2)}, u32[]{:S(2)}) collective-permute-start(bf16[896,256]{1,0:T(8,128)(2,1)} %bitcast.8), channel_id=1, source_target_pairs={{1,0},{2,1},{3,2},{4,3},{5,4},{6,5},{7,6},{8,7},{9,8},{10,9},{11,1... | collective-permute-start | bytes 1376264 | tf_op jit(solution)/shard_map/ppermute | solution.py:335
  42.6 1.5 %copy-start.2 = (f32[1088,256]{1,0:T(8,128)}, f32[1088,256]{1,0:T(8,128)S(1)}, u32[]{:S(2)}) copy-start(f32[1088,256]{1,0:T(8,128)S(1)} %get-tuple-element.19.own_ref) | copy-start | bytes 3342340
  44.1 3.9 %collective-permute-start.2 = (bf16[16,72,256]{2,1,0:T(8,128)(2,1)S(1)}, bf16[16,72,256]{2,1,0:T(8,128)(2,1)S(1)}, u32[]{:S(2)}, u32[]{:S(2)}) collective-permute-start(bf16[16,72,256]{2,1,0:T(8,128)(2,1)S(1)} %get-tuple-element.16), channel_id=1, source_target_pairs={{0,1},{1,0},{2,3},{3,2},{4,5},{5,4},{6,7},{7,6},{8,9},{9,8},{10,11... | collective-permute-start | bytes 1769480 | tf_op jit(solution)/shard_map/ppermute | solution.py:340
  48.0 24.1 %copy-start.1 = (bf16[3,3,256,256]{3,2,1,0:T(8,128)(2,1)S(1)}, bf16[3,3,256,256]{3,2,1,0:T(8,128)(2,1)}, u32[]{:S(2)}) copy-start(bf16[3,3,256,256]{3,2,1,0:T(8,128)(2,1)} %param.6) | copy-start | bytes 3538948
  48.9 16.4 %all-to-all-start.1 = ((bf16[16,72,256]{2,1,0:T(8,128)(2,1)}), bf16[16,72,256]{2,1,0:T(8,128)(2,1)S(1)}, u32[]{:S(2)}, u32[]{:S(2)}) async-start(bf16[16,72,256]{2,1,0:T(8,128)(2,1)} %pair.1), calls=%async_computation.1 | async-start | bytes 1179648 | tf_op jit(solution)/shard_map/all_to_all | solution.py:325
  52.5 19.6 %collective-permute-start.4 = (bf16[896,256]{1,0:T(8,128)(2,1)S(1)}, bf16[896,256]{1,0:T(8,128)(2,1)S(1)}, u32[]{:S(2)}, u32[]{:S(2)}) collective-permute-start(bf16[896,256]{1,0:T(8,128)(2,1)S(1)} %get-tuple-element.20), channel_id=1, source_target_pairs={{0,1},{1,2},{2,3},{3,4},{4,5},{5,6},{6,7},{7,8},{8,9},{9,10},{10,1... | collective-permute-start | bytes 1376264 | tf_op jit(solution)/shard_map/ppermute | solution.py:345
  54.6 4.4 %collective-permute-start.3 = (bf16[64,256]{1,0:T(8,128)(2,1)S(1)}, bf16[64,256]{1,0:T(8,128)(2,1)S(1)}, u32[]{:S(2)}, u32[]{:S(2)}) collective-permute-start(bf16[64,256]{1,0:T(8,128)(2,1)S(1)} %get-tuple-element.17), channel_id=1, source_target_pairs={{1,0},{2,1},{3,2},{4,3},{5,4},{6,5},{7,6},{8,7},{9,8},{10,9},{11,1... | collective-permute-start | bytes 98312 | tf_op jit(solution)/shard_map/ppermute | solution.py:342
  66.0 11.3 %all-to-all-start.2 = ((bf16[4,72,256]{2,1,0:T(8,128)(2,1)}), bf16[4,72,256]{2,1,0:T(8,128)(2,1)S(1)}, u32[]{:S(2)}, u32[]{:S(2)}) async-start(bf16[4,72,256]{2,1,0:T(8,128)(2,1)} %sum.4), calls=%async_computation.2 | async-start | bytes 294912 | tf_op jit(solution)/shard_map/all_to_all | solution.py:325
  72.1 1.2 %copy-start.3 = (f32[1088,256]{1,0:T(8,128)S(1)}, f32[1088,256]{1,0:T(8,128)}, u32[]{:S(2)}) copy-start(f32[1088,256]{1,0:T(8,128)} %copy-done.2) | copy-start | bytes 3342340

commit v8 on v6

--- a/solution.py
+++ b/solution.py
@@ -20,7 +20,7 @@
 CHIPS = TILES // 2
 IMAGES = 16
 EXT = TR + REACH - 1
-ROWS = 2
+ROWS = 3
 SLOT = CELLS + 1
 BLOCK = 104
 SLOTS = TILES * CAP
@@ -187,8 +187,8 @@
 
 def filter_kernel(
     got_ref, features_ref,
-    part_ref, beyond_ref, own_hbm, above_ref, below_ref,
-    rows_ref, cols_ref, left_ref, map_ref, turned_ref, own_ref, sem,
+    part_ref, beyond_ref, own_ref, above_ref, below_ref,
+    rows_ref, cols_ref, left_ref, map_ref, turned_ref,
 ):
     weights_of(got_ref, rows_ref, cols_ref)
     turn_rows(features_ref[...], turned_ref)
@@ -208,8 +208,6 @@
                 map_ref[(4 + EXT) * MW : (5 + EXT) * MW] = rounded[one]
             if h >= TR - 1:
                 above_ref[(h - TR + 1) * MW : (h - TR + 2) * MW] = rounded[one]
-    put = pltpu.make_async_copy(own_ref, own_hbm, sem)
-    put.start()
     beyond_ref[...] = map_ref[(1 + TR) * MW : (3 + 2 * TR) * MW]
     for a in range(3):
         part_ref[a] = jnp.dot(
@@ -217,7 +215,6 @@
             map_ref[(3 - a) * MW : (3 - a + TR) * MW],
             preferred_element_type=F32,
         )
-    put.wait()
 
 
 def beyond_kernel(
@@ -261,20 +258,18 @@
         out_shape=(
             jax.ShapeDtypeStruct((3, 3 * C, C), F32),
             jax.ShapeDtypeStruct(((TR + 2) * MW, C), BF16),
-            pltpu.HBM(((TR + 1) * MW, C), F32),
+            jax.ShapeDtypeStruct(((TR + 1) * MW, C), F32),
             jax.ShapeDtypeStruct((REACH * MW, C), BF16),
             jax.ShapeDtypeStruct((MW, C), BF16),
         ),
         in_specs=[vmem(), vmem()],
-        out_specs=(vmem(), vmem(), hbm(), vmem(), vmem()),
+        out_specs=(vmem(),) * 5,
         scratch_shapes=[
             pltpu.VMEM((32, KDIM), F32),
             pltpu.VMEM((MW, KDIM), BF16),
             pltpu.VMEM((ROWS * MW, KDIM), BF16),
             pltpu.VMEM(((EXT + 6) * MW, C), BF16),
             pltpu.VMEM((3 * C, TR * MW), BF16),
-            pltpu.VMEM(((TR + 1) * MW, C), F32),
-            pltpu.SemaphoreType.DMA,
         ],
         compiler_params=pltpu.CompilerParams(vmem_limit_bytes=30 << 20),
         name="filter",
@@ -338,28 +333,16 @@
     )(parts)
 
 
-PIECES = 4
-
-
-def pair_kernel(keep_ref, got_ref, out_hbm, out_ref, sems):
-    step = CHIPS // PIECES
-    sent = []
-    for i in range(PIECES):
-        part = pl.ds(i * step, step)
-        out_ref[part] = (keep_ref[part] + got_ref[part].astype(F32)).astype(BF16)
-        sent.append(pltpu.make_async_copy(out_ref.at[part], out_hbm.at[part], sems.at[i]))
-        sent[-1].start()
-    for copy in sent:
-        copy.wait()
+def pair_kernel(keep_ref, got_ref, out_ref):
+    out_ref[...] = (keep_ref[...] + got_ref[...].astype(F32)).astype(BF16)
 
 
 def sum_pair(keep, got):
     return pl.pallas_call(
         pair_kernel,
-        out_shape=pltpu.HBM(keep.shape, BF16),
+        out_shape=jax.ShapeDtypeStruct(keep.shape, BF16),
         in_specs=[vmem()] * 2,
-        out_specs=hbm(),
-        scratch_shapes=[pltpu.VMEM(keep.shape, BF16), pltpu.SemaphoreType.DMA((PIECES,))],
+        out_specs=vmem(),
         compiler_params=pltpu.CompilerParams(vmem_limit_bytes=4 << 20),
         name="pair",
         cost_estimate=cost(keep.size, keep.size * 8),

time: 98.4 us -> 98.2 us (level)
  transfers between devices with their start and end apart: 8 -> 8, of which waited for: 5 -> 5; matrix products, arithmetic and copies ran while one was open for 1% -> 1% of each run, Pallas kernels for 9% -> 8%
where the time goes in v8:
time: 98.2 us; the launch traced here: 97.6 us
  waiting for transfers between devices  33.5 us (34%)
  starting transfers between devices  25.8 us (26%)
  blocking collectives  20 us (20%)
  Pallas kernels  15.5 us (16%)
  local copies, waits for them, and re-layouts  2.06 us (2%)
    all_to_all x3, waiting for transfers between devices, exchange(): return lax.all_to_all(parts, axis, split_axis=0, concat_axis=0, tiled=True)  28.5 us
    all_to_all x3, starting transfers between devices, exchange(): return lax.all_to_all(parts, axis, split_axis=0, concat_axis=0, tiled=True)  17 us
    all_gather x1, blocking collectives, body(): lax.all_gather(parts, 'zh', tiled=True, axis_index_groups=[[0, 1], [2, 3]])  10.4 us
    all_gather x1, blocking collectives, body(): lax.all_gather(parts, 'zh', tiled=True, axis_index_groups=[[0, 3], [1, 2]])  9.56 us
    pallas_call x1, Pallas kernels, filter_part(): pl.pallas_call(filter_kernel, out_shape=(jax.ShapeDtypeStruct((3, 3 * C,...  5.3 us
    pallas_call x1, Pallas kernels, dispatch(): pl.pallas_call(dispatch_kernel, out_shape=jax.ShapeDtypeStruct((TILES, BL...  4.21 us
    ppermute x1, waiting for transfers between devices, body(): below = lax.ppermute(below, TILE_AXES, down)  3.05 us
    pallas_call x1, Pallas kernels, input_part(): pl.pallas_call(input_kernel, out_shape=jax.ShapeDtypeStruct((TR * MW, C),...  2.23 us
  transfers between devices with their start and end apart: 8, of which 5 were waited for; matrix products, arithmetic and copies ran while one was open for 1% of the time, Pallas kernels for 8%

profile of v8, /device:TPU:32, one launch (start us, length us, event | category | flops | bytes accessed | tf_op | source)
XLA Modules:
  0.0 97.6 jit_solution(456097655568880761)
XLA Ops:
  0.6 4.2 %dispatch.1 = bf16[32,104,256]{2,1,0:T(8,128)(2,1)} custom-call(s32[1,16]{1,0:T(1,128)} %index_hbm.1, s32[4,20000]{1,0:T(4,128)} %bitcast.24, bf16[49,16,256]{2,1,0:T(8,128)(2,1)} %bitcast.23), custom_call_target="tpu_custom_call" | custom-call | flops 1363148800 | bytes 3145728 | tf_op jit(solution)/shard_map/dispatch/pallas_call | solution.py:124
  4.9 7.5 %all-to-all-start = ((bf16[32,104,256]{2,1,0:T(8,128)(2,1)}), bf16[32,104,256]{2,1,0:T(8,128)(2,1)S(1)}, u32[]{:S(2)}, u32[]{:S(2)}) async-start(bf16[32,104,256]{2,1,0:T(8,128)(2,1)} %dispatch.1), calls=%async_computation | async-start | bytes 3407872 | tf_op jit(solution)/shard_map/all_to_all | solution.py:353
  12.4 2.2 %collective-permute-start = (bf16[64,256]{1,0:T(8,128)(2,1)S(1)}, bf16[64,256]{1,0:T(8,128)(2,1)S(1)}, u32[]{:S(2)}, u32[]{:S(2)}) collective-permute-start(bf16[64,256]{1,0:T(8,128)(2,1)S(1)} %slice_bitcast_fusion), channel_id=1, source_target_pairs={{0,1},{1,2},{2,3},{3,4},{4,5},{5,6},{6,7},{7,8},{8,9},{9,10},{10,1... | collective-permute-start | bytes 98312 | tf_op jit(solution)/shard_map/ppermute | solution.py:362
  14.5 0.8 slice.14
  15.3 1.3 %collective-permute-start.1 = (bf16[896,256]{1,0:T(8,128)(2,1)}, bf16[896,256]{1,0:T(8,128)(2,1)S(1)}, u32[]{:S(2)}, u32[]{:S(2)}) collective-permute-start(bf16[896,256]{1,0:T(8,128)(2,1)} %bitcast.8), channel_id=1, source_target_pairs={{1,0},{2,1},{3,2},{4,3},{5,4},{6,5},{7,6},{8,7},{9,8},{10,9},{11,1... | collective-permute-start | bytes 1376264 | tf_op jit(solution)/shard_map/ppermute | solution.py:363
  16.6 20.3 %all-to-all-done.got_ref = bf16[32,104,256]{2,1,0:T(8,128)(2,1)S(1)} async-done(((bf16[32,104,256]{2,1,0:T(8,128)(2,1)}), bf16[32,104,256]{2,1,0:T(8,128)(2,1)S(1)}, u32[]{:S(2)}, u32[]{:S(2)}) %all-to-all-start) | async-done | bytes 1703968 | tf_op jit(solution)/shard_map/all_to_all | solution.py:353
  36.9 5.3 %filter.1 = (f32[3,768,256]{2,1,0:T(8,128)S(1)}, bf16[1152,256]{1,0:T(8,128)(2,1)S(1)}, f32[1088,256]{1,0:T(8,128)S(1)}, bf16[896,256]{1,0:T(8,128)(2,1)S(1)}, bf16[64,256]{1,0:T(8,128)(2,1)S(1)}) custom-call(bf16[32,104,256]{2,1,0:T(8,128)(2,1)S(1)} %all-to-all-done.got_ref, bf16[1024,256]{1,0:T(8,128)(2,1)S(1)} %bitcast.20), custom_call_target="tpu_custom_call" | custom-call | flops 5578424320 | bytes 4194304 | tf_op jit(solution)/shard_map/filter/pallas_call | solution.py:256
  42.3 1.4 %beyond.1 = (f32[16,72,256]{2,1,0:T(8,128)S(1)}, bf16[16,72,256]{2,1,0:T(8,128)(2,1)S(1)}) custom-call(s32[1]{0:T(128)} %bitcast.core_ref, f32[3,768,256]{2,1,0:T(8,128)S(1)} %get-tuple-element.13.part_ref, bf16[1152,256]{1,0:T(8,128)(2,1)S(1)} %get-tuple-element.14.beyond_ref, bf16[64,256]{1,0:T(8,128)(2,1)S(1)} %collective-permute-done.before_ref, ...), custom_call_target="tpu_custom_call" | custom-call | flops 1207959552 | bytes 4194304 | tf_op jit(solution)/shard_map/beyond/pallas_call | solution.py:240
  43.7 1.9 %collective-permute-start.2 = (bf16[16,72,256]{2,1,0:T(8,128)(2,1)S(1)}, bf16[16,72,256]{2,1,0:T(8,128)(2,1)S(1)}, u32[]{:S(2)}, u32[]{:S(2)}) collective-permute-start(bf16[16,72,256]{2,1,0:T(8,128)(2,1)S(1)} %get-tuple-element.16), channel_id=1, source_target_pairs={{0,1},{1,0},{2,3},{3,2},{4,5},{5,4},{6,7},{7,6},{8,9},{9,8},{10,11... | collective-permute-start | bytes 1769480 | tf_op jit(solution)/shard_map/ppermute | solution.py:368
  45.6 2.0 %collective-permute-done.2.got_ref = bf16[16,72,256]{2,1,0:T(8,128)(2,1)S(1)} collective-permute-done((bf16[16,72,256]{2,1,0:T(8,128)(2,1)S(1)}, bf16[16,72,256]{2,1,0:T(8,128)(2,1)S(1)}, u32[]{:S(2)}, u32[]{:S(2)}) %collective-permute-start.2) | collective-permute-done | bytes 589856 | tf_op jit(solution)/shard_map/ppermute | solution.py:368
  47.6 0.9 pair.1
  48.5 3.6 %all-to-all-start.1 = ((bf16[16,72,256]{2,1,0:T(8,128)(2,1)}), bf16[16,72,256]{2,1,0:T(8,128)(2,1)S(1)}, u32[]{:S(2)}, u32[]{:S(2)}) async-start(bf16[16,72,256]{2,1,0:T(8,128)(2,1)} %pair.1), calls=%async_computation.1 | async-start | bytes 1179648 | tf_op jit(solution)/shard_map/all_to_all | solution.py:353
  52.1 2.1 %collective-permute-start.4 = (bf16[896,256]{1,0:T(8,128)(2,1)S(1)}, bf16[896,256]{1,0:T(8,128)(2,1)S(1)}, u32[]{:S(2)}, u32[]{:S(2)}) collective-permute-start(bf16[896,256]{1,0:T(8,128)(2,1)S(1)} %get-tuple-element.20), channel_id=1, source_target_pairs={{0,1},{1,2},{2,3},{3,4},{4,5},{5,6},{6,7},{7,8},{8,9},{9,10},{10,1... | collective-permute-start | bytes 1376264 | tf_op jit(solution)/shard_map/ppermute | solution.py:373
  54.2 1.3 %collective-permute-start.3 = (bf16[64,256]{1,0:T(8,128)(2,1)S(1)}, bf16[64,256]{1,0:T(8,128)(2,1)S(1)}, u32[]{:S(2)}, u32[]{:S(2)}) collective-permute-start(bf16[64,256]{1,0:T(8,128)(2,1)S(1)} %get-tuple-element.17), channel_id=1, source_target_pairs={{1,0},{2,1},{3,2},{4,3},{5,4},{6,5},{7,6},{8,7},{9,8},{10,9},{11,1... | collective-permute-start | bytes 98312 | tf_op jit(solution)/shard_map/ppermute | solution.py:370
  55.5 3.1 %collective-permute-done.3.below_ref = bf16[64,256]{1,0:T(8,128)(2,1)S(1)} collective-permute-done((bf16[64,256]{1,0:T(8,128)(2,1)S(1)}, bf16[64,256]{1,0:T(8,128)(2,1)S(1)}, u32[]{:S(2)}, u32[]{:S(2)}) %collective-permute-start.3) | collective-permute-done | bytes 32800 | tf_op jit(solution)/shard_map/ppermute | solution.py:370
  58.6 6.4 %all-to-all-done.1.parts_ref = bf16[16,72,256]{2,1,0:T(8,128)(2,1)S(1)} async-done(((bf16[16,72,256]{2,1,0:T(8,128)(2,1)}), bf16[16,72,256]{2,1,0:T(8,128)(2,1)S(1)}, u32[]{:S(2)}, u32[]{:S(2)}) %all-to-all-start.1) | async-done | bytes 589856 | tf_op jit(solution)/shard_map/all_to_all | solution.py:353
  64.9 0.7 sum.4
  65.7 6.0 %all-to-all-start.2 = ((bf16[4,72,256]{2,1,0:T(8,128)(2,1)}), bf16[4,72,256]{2,1,0:T(8,128)(2,1)S(1)}, u32[]{:S(2)}, u32[]{:S(2)}) async-start(bf16[4,72,256]{2,1,0:T(8,128)(2,1)} %sum.4), calls=%async_computation.2 | async-start | bytes 294912 | tf_op jit(solution)/shard_map/all_to_all | solution.py:353
  71.7 1.2 %copy-done.3 = f32[1088,256]{1,0:T(8,128)S(1)} copy-done((f32[1088,256]{1,0:T(8,128)S(1)}, f32[1088,256]{1,0:T(8,128)}, u32[]{:S(2)}) %copy-start.3) | copy-done | bytes 1114136
  72.9 2.2 %input.1 = bf16[1024,256]{1,0:T(8,128)(2,1)} custom-call(f32[1088,256]{1,0:T(8,128)S(1)} %copy-done.3, bf16[896,256]{1,0:T(8,128)(2,1)S(1)} %collective-permute-done.4.above_ref, bf16[64,256]{1,0:T(8,128)(2,1)S(1)} %collective-permute-done.3.below_ref, bf16[9,256,256]{2,1,0:T(8,128)(2,1)S(1)} %bitcast.21), custom_call_target="tpu_custom_call" | custom-call | flops 1207959552 | bytes 4194304 | tf_op jit(solution)/shard_map/input/pallas_call | solution.py:305
  75.2 1.8 %all-to-all-done.2.parts_ref = bf16[4,72,256]{2,1,0:T(8,128)(2,1)S(1)} async-done(((bf16[4,72,256]{2,1,0:T(8,128)(2,1)}), bf16[4,72,256]{2,1,0:T(8,128)(2,1)S(1)}, u32[]{:S(2)}, u32[]{:S(2)}) %all-to-all-start.2) | async-done | bytes 147488 | tf_op jit(solution)/shard_map/all_to_all | solution.py:353
  77.0 10.4 %all_gather.6.parts_ref = bf16[2,72,256]{2,1,0:T(8,128)(2,1)S(1)} all-gather(bf16[1,72,256]{2,1,0:T(8,128)(2,1)S(1)} %sum.5), channel_id=1, replica_groups={{0,128},{256,384},{1,129},{257,385},{2,130},{258,386},{3,131},{259,387}..., dimensions={0}, use_global_device_ids=true | all-gather | bytes 110592 | tf_op jit(solution)/shard_map/all_gather | solution.py:377
  87.4 9.6 %all_gather.7.parts_ref = bf16[2,72,256]{2,1,0:T(8,128)(2,1)S(1)} all-gather(bf16[1,72,256]{2,1,0:T(8,128)(2,1)S(1)} %sum.6), channel_id=1, replica_groups={{0,384},{128,256},{1,385},{129,257},{2,386},{130,258},{3,387},{131,259}..., dimensions={0}, use_global_device_ids=true | all-gather | bytes 110592 | tf_op jit(solution)/shard_map/all_gather | solution.py:379
  97.0 0.6 sum.7
  (13 shorter events, 0.1 us)
Async XLA Ops:
  4.9 7.5 %copy-start = (bf16[1,16,64,256]{3,2,1,0:T(8,128)(2,1)S(1)}, bf16[1,16,64,256]{3,2,1,0:T(8,128)(2,1)}, u32[]{:S(2)}) copy-start(bf16[1,16,64,256]{3,2,1,0:T(8,128)(2,1)} %param.5) | copy-start | bytes 1572868
  4.9 32.1 %all-to-all-start = ((bf16[32,104,256]{2,1,0:T(8,128)(2,1)}), bf16[32,104,256]{2,1,0:T(8,128)(2,1)S(1)}, u32[]{:S(2)}, u32[]{:S(2)}) async-start(bf16[32,104,256]{2,1,0:T(8,128)(2,1)} %dispatch.1), calls=%async_computation | async-start | bytes 3407872 | tf_op jit(solution)/shard_map/all_to_all | solution.py:353
  12.4 29.9 %collective-permute-start = (bf16[64,256]{1,0:T(8,128)(2,1)S(1)}, bf16[64,256]{1,0:T(8,128)(2,1)S(1)}, u32[]{:S(2)}, u32[]{:S(2)}) collective-permute-start(bf16[64,256]{1,0:T(8,128)(2,1)S(1)} %slice_bitcast_fusion), channel_id=1, source_target_pairs={{0,1},{1,2},{2,3},{3,4},{4,5},{5,6},{6,7},{7,8},{8,9},{9,10},{10,1... | collective-permute-start | bytes 98312 | tf_op jit(solution)/shard_map/ppermute | solution.py:362
  15.3 26.9 %collective-permute-start.1 = (bf16[896,256]{1,0:T(8,128)(2,1)}, bf16[896,256]{1,0:T(8,128)(2,1)S(1)}, u32[]{:S(2)}, u32[]{:S(2)}) collective-permute-start(bf16[896,256]{1,0:T(8,128)(2,1)} %bitcast.8), channel_id=1, source_target_pairs={{1,0},{2,1},{3,2},{4,3},{5,4},{6,5},{7,6},{8,7},{9,8},{10,9},{11,1... | collective-permute-start | bytes 1376264 | tf_op jit(solution)/shard_map/ppermute | solution.py:363
  42.2 1.5 %copy-start.2 = (f32[1088,256]{1,0:T(8,128)}, f32[1088,256]{1,0:T(8,128)S(1)}, u32[]{:S(2)}) copy-start(f32[1088,256]{1,0:T(8,128)S(1)} %get-tuple-element.19.own_ref) | copy-start | bytes 3342340
  43.7 3.9 %collective-permute-start.2 = (bf16[16,72,256]{2,1,0:T(8,128)(2,1)S(1)}, bf16[16,72,256]{2,1,0:T(8,128)(2,1)S(1)}, u32[]{:S(2)}, u32[]{:S(2)}) collective-permute-start(bf16[16,72,256]{2,1,0:T(8,128)(2,1)S(1)} %get-tuple-element.16), channel_id=1, source_target_pairs={{0,1},{1,0},{2,3},{3,2},{4,5},{5,4},{6,7},{7,6},{8,9},{9,8},{10,11... | collective-permute-start | bytes 1769480 | tf_op jit(solution)/shard_map/ppermute | solution.py:368
  47.6 24.1 %copy-start.1 = (bf16[3,3,256,256]{3,2,1,0:T(8,128)(2,1)S(1)}, bf16[3,3,256,256]{3,2,1,0:T(8,128)(2,1)}, u32[]{:S(2)}) copy-start(bf16[3,3,256,256]{3,2,1,0:T(8,128)(2,1)} %param.6) | copy-start | bytes 3538948
  48.5 16.4 %all-to-all-start.1 = ((bf16[16,72,256]{2,1,0:T(8,128)(2,1)}), bf16[16,72,256]{2,1,0:T(8,128)(2,1)S(1)}, u32[]{:S(2)}, u32[]{:S(2)}) async-start(bf16[16,72,256]{2,1,0:T(8,128)(2,1)} %pair.1), calls=%async_computation.1 | async-start | bytes 1179648 | tf_op jit(solution)/shard_map/all_to_all | solution.py:353
  52.1 19.6 %collective-permute-start.4 = (bf16[896,256]{1,0:T(8,128)(2,1)S(1)}, bf16[896,256]{1,0:T(8,128)(2,1)S(1)}, u32[]{:S(2)}, u32[]{:S(2)}) collective-permute-start(bf16[896,256]{1,0:T(8,128)(2,1)S(1)} %get-tuple-element.20), channel_id=1, source_target_pairs={{0,1},{1,2},{2,3},{3,4},{4,5},{5,6},{6,7},{7,8},{8,9},{9,10},{10,1... | collective-permute-start | bytes 1376264 | tf_op jit(solution)/shard_map/ppermute | solution.py:373
  54.2 4.4 %collective-permute-start.3 = (bf16[64,256]{1,0:T(8,128)(2,1)S(1)}, bf16[64,256]{1,0:T(8,128)(2,1)S(1)}, u32[]{:S(2)}, u32[]{:S(2)}) collective-permute-start(bf16[64,256]{1,0:T(8,128)(2,1)S(1)} %get-tuple-element.17), channel_id=1, source_target_pairs={{1,0},{2,1},{3,2},{4,3},{5,4},{6,5},{7,6},{8,7},{9,8},{10,9},{11,1... | collective-permute-start | bytes 98312 | tf_op jit(solution)/shard_map/ppermute | solution.py:370
  65.7 11.3 %all-to-all-start.2 = ((bf16[4,72,256]{2,1,0:T(8,128)(2,1)}), bf16[4,72,256]{2,1,0:T(8,128)(2,1)S(1)}, u32[]{:S(2)}, u32[]{:S(2)}) async-start(bf16[4,72,256]{2,1,0:T(8,128)(2,1)} %sum.4), calls=%async_computation.2 | async-start | bytes 294912 | tf_op jit(solution)/shard_map/all_to_all | solution.py:353
  71.7 1.2 %copy-start.3 = (f32[1088,256]{1,0:T(8,128)S(1)}, f32[1088,256]{1,0:T(8,128)}, u32[]{:S(2)}) copy-start(f32[1088,256]{1,0:T(8,128)} %copy-done.2) | copy-start | bytes 3342340

commit v9 on v7

--- a/solution.py
+++ b/solution.py
@@ -112,19 +112,19 @@
 
 
 def weights_of(got_ref, rows_ref, cols_ref):
-    slot = iota((SLOTS, KDIM), 0)
-    cell = iota((SLOTS, KDIM), 1)
-    first = (slot % TILES) * BLOCK + (slot // TILES) * SLOT
+    lane = iota((1, KDIM), 1)
+    source = lane // BLOCK
+    within = lane - source * BLOCK
+    later = (within >= SLOT).astype(I32)
+    within = within - later * SLOT
+    inside = within < CELLS
+    slot = jnp.where(inside, source + later * TILES, -1)
     box = jnp.concatenate(
         [got_ref[:, s * SLOT + CELLS, :LANES].astype(F32) for s in range(CAP)], axis=0
     )
     box = box.T[:8].astype(BF16)
-    cover = ((cell >= first) & (cell < first + CELLS)).astype(F32).astype(BF16)
+    cover = (iota((SLOTS, KDIM), 0) == slot).astype(F32).astype(BF16)
     field = jnp.dot(box, cover, preferred_element_type=F32).astype(I32)
-    within = iota((1, KDIM), 1) % BLOCK
-    inside = within < CAP * SLOT
-    within = within % SLOT
-    inside = inside & (within < CELLS)
     row_bin = within // BINS
     col_bin = within - row_bin * BINS
     row = jnp.where(inside, field[0:1] + row_bin * field[2:3], -9)

time: 98.6 us -> 98.4 us (level)
  no operation moved by 1% of the time
where the time goes in v9:
time: 98.4 us; the launch traced here: 97.8 us
  waiting for transfers between devices  33.5 us (34%)
  starting transfers between devices  25.8 us (26%)
  blocking collectives  20 us (20%)
  Pallas kernels  15.8 us (16%)
  local copies, waits for them, and re-layouts  2.06 us (2%)
    all_to_all x3, waiting for transfers between devices, exchange(): return lax.all_to_all(parts, axis, split_axis=0, concat_axis=0, tiled=True)  28.5 us
    all_to_all x3, starting transfers between devices, exchange(): return lax.all_to_all(parts, axis, split_axis=0, concat_axis=0, tiled=True)  17 us
    all_gather x1, blocking collectives, body(): lax.all_gather(parts, 'zh', tiled=True, axis_index_groups=[[0, 1], [2, 3]])  10.4 us
    all_gather x1, blocking collectives, body(): lax.all_gather(parts, 'zh', tiled=True, axis_index_groups=[[0, 3], [1, 2]])  9.58 us
    pallas_call x1, Pallas kernels, filter_part(): pl.pallas_call(filter_kernel, out_shape=(jax.ShapeDtypeStruct((3, 3 * C,...  5.13 us
    pallas_call x1, Pallas kernels, dispatch(): pl.pallas_call(dispatch_kernel, out_shape=jax.ShapeDtypeStruct((TILES, BL...  4.61 us
    ppermute x1, waiting for transfers between devices, body(): below = lax.ppermute(below, TILE_AXES, down)  3.05 us
    pallas_call x1, Pallas kernels, input_part(): pl.pallas_call(input_kernel, out_shape=jax.ShapeDtypeStruct((TR * MW, C),...  2.23 us
  transfers between devices with their start and end apart: 8, of which 5 were waited for; matrix products, arithmetic and copies ran while one was open for 1% of the time, Pallas kernels for 8%

profile of v9, /device:TPU:32, one launch (start us, length us, event | category | flops | bytes accessed | tf_op | source)
XLA Modules:
  0.0 97.8 jit_solution(7703270436939945900)
XLA Ops:
  0.6 4.6 %dispatch.1 = bf16[32,104,256]{2,1,0:T(8,128)(2,1)} custom-call(s32[1,16]{1,0:T(1,128)} %index_ref.1, s32[4,20000]{1,0:T(4,128)} %bitcast.24, bf16[49,16,256]{2,1,0:T(8,128)(2,1)} %bitcast.23), custom_call_target="tpu_custom_call" | custom-call | flops 1363148800 | bytes 3145728 | tf_op jit(solution)/shard_map/dispatch/pallas_call | solution.py:103
  5.2 7.5 %all-to-all-start = ((bf16[32,104,256]{2,1,0:T(8,128)(2,1)}), bf16[32,104,256]{2,1,0:T(8,128)(2,1)S(1)}, u32[]{:S(2)}, u32[]{:S(2)}) async-start(bf16[32,104,256]{2,1,0:T(8,128)(2,1)} %dispatch.1), calls=%async_computation | async-start | bytes 3407872 | tf_op jit(solution)/shard_map/all_to_all | solution.py:325
  12.7 2.2 %collective-permute-start = (bf16[64,256]{1,0:T(8,128)(2,1)S(1)}, bf16[64,256]{1,0:T(8,128)(2,1)S(1)}, u32[]{:S(2)}, u32[]{:S(2)}) collective-permute-start(bf16[64,256]{1,0:T(8,128)(2,1)S(1)} %slice_bitcast_fusion), channel_id=1, source_target_pairs={{0,1},{1,2},{2,3},{3,4},{4,5},{5,6},{6,7},{7,8},{8,9},{9,10},{10,1... | collective-permute-start | bytes 98312 | tf_op jit(solution)/shard_map/ppermute | solution.py:334
  14.9 0.8 slice.14
  15.7 1.3 %collective-permute-start.1 = (bf16[896,256]{1,0:T(8,128)(2,1)}, bf16[896,256]{1,0:T(8,128)(2,1)S(1)}, u32[]{:S(2)}, u32[]{:S(2)}) collective-permute-start(bf16[896,256]{1,0:T(8,128)(2,1)} %bitcast.8), channel_id=1, source_target_pairs={{1,0},{2,1},{3,2},{4,3},{5,4},{6,5},{7,6},{8,7},{9,8},{10,9},{11,1... | collective-permute-start | bytes 1376264 | tf_op jit(solution)/shard_map/ppermute | solution.py:335
  17.0 20.3 %all-to-all-done.got_ref = bf16[32,104,256]{2,1,0:T(8,128)(2,1)S(1)} async-done(((bf16[32,104,256]{2,1,0:T(8,128)(2,1)}), bf16[32,104,256]{2,1,0:T(8,128)(2,1)S(1)}, u32[]{:S(2)}, u32[]{:S(2)}) %all-to-all-start) | async-done | bytes 1703968 | tf_op jit(solution)/shard_map/all_to_all | solution.py:325
  37.3 5.1 %filter.1 = (f32[3,768,256]{2,1,0:T(8,128)S(1)}, bf16[1152,256]{1,0:T(8,128)(2,1)S(1)}, f32[1088,256]{1,0:T(8,128)S(1)}, bf16[896,256]{1,0:T(8,128)(2,1)S(1)}, bf16[64,256]{1,0:T(8,128)(2,1)S(1)}) custom-call(bf16[32,104,256]{2,1,0:T(8,128)(2,1)S(1)} %all-to-all-done.got_ref, bf16[1024,256]{1,0:T(8,128)(2,1)S(1)} %bitcast.20), custom_call_target="tpu_custom_call" | custom-call | flops 5578424320 | bytes 4194304 | tf_op jit(solution)/shard_map/filter/pallas_call | solution.py:228
  42.5 1.4 %beyond.1 = (f32[16,72,256]{2,1,0:T(8,128)S(1)}, bf16[16,72,256]{2,1,0:T(8,128)(2,1)S(1)}) custom-call(s32[1]{0:T(128)} %bitcast.core_ref, f32[3,768,256]{2,1,0:T(8,128)S(1)} %get-tuple-element.13.part_ref, bf16[1152,256]{1,0:T(8,128)(2,1)S(1)} %get-tuple-element.14.beyond_ref, bf16[64,256]{1,0:T(8,128)(2,1)S(1)} %collective-permute-done.before_ref, ...), custom_call_target="tpu_custom_call" | custom-call | flops 1207959552 | bytes 4194304 | tf_op jit(solution)/shard_map/beyond/pallas_call | solution.py:212
  43.9 1.9 %collective-permute-start.2 = (bf16[16,72,256]{2,1,0:T(8,128)(2,1)S(1)}, bf16[16,72,256]{2,1,0:T(8,128)(2,1)S(1)}, u32[]{:S(2)}, u32[]{:S(2)}) collective-permute-start(bf16[16,72,256]{2,1,0:T(8,128)(2,1)S(1)} %get-tuple-element.16), channel_id=1, source_target_pairs={{0,1},{1,0},{2,3},{3,2},{4,5},{5,4},{6,7},{7,6},{8,9},{9,8},{10,11... | collective-permute-start | bytes 1769480 | tf_op jit(solution)/shard_map/ppermute | solution.py:340
  45.8 2.0 %collective-permute-done.2.got_ref = bf16[16,72,256]{2,1,0:T(8,128)(2,1)S(1)} collective-permute-done((bf16[16,72,256]{2,1,0:T(8,128)(2,1)S(1)}, bf16[16,72,256]{2,1,0:T(8,128)(2,1)S(1)}, u32[]{:S(2)}, u32[]{:S(2)}) %collective-permute-start.2) | collective-permute-done | bytes 589856 | tf_op jit(solution)/shard_map/ppermute | solution.py:340
  47.8 0.9 pair.1
  48.7 3.6 %all-to-all-start.1 = ((bf16[16,72,256]{2,1,0:T(8,128)(2,1)}), bf16[16,72,256]{2,1,0:T(8,128)(2,1)S(1)}, u32[]{:S(2)}, u32[]{:S(2)}) async-start(bf16[16,72,256]{2,1,0:T(8,128)(2,1)} %pair.1), calls=%async_computation.1 | async-start | bytes 1179648 | tf_op jit(solution)/shard_map/all_to_all | solution.py:325
  52.3 2.1 %collective-permute-start.4 = (bf16[896,256]{1,0:T(8,128)(2,1)S(1)}, bf16[896,256]{1,0:T(8,128)(2,1)S(1)}, u32[]{:S(2)}, u32[]{:S(2)}) collective-permute-start(bf16[896,256]{1,0:T(8,128)(2,1)S(1)} %get-tuple-element.20), channel_id=1, source_target_pairs={{0,1},{1,2},{2,3},{3,4},{4,5},{5,6},{6,7},{7,8},{8,9},{9,10},{10,1... | collective-permute-start | bytes 1376264 | tf_op jit(solution)/shard_map/ppermute | solution.py:345
  54.4 1.3 %collective-permute-start.3 = (bf16[64,256]{1,0:T(8,128)(2,1)S(1)}, bf16[64,256]{1,0:T(8,128)(2,1)S(1)}, u32[]{:S(2)}, u32[]{:S(2)}) collective-permute-start(bf16[64,256]{1,0:T(8,128)(2,1)S(1)} %get-tuple-element.17), channel_id=1, source_target_pairs={{1,0},{2,1},{3,2},{4,3},{5,4},{6,5},{7,6},{8,7},{9,8},{10,9},{11,1... | collective-permute-start | bytes 98312 | tf_op jit(solution)/shard_map/ppermute | solution.py:342
  55.7 3.1 %collective-permute-done.3.below_ref = bf16[64,256]{1,0:T(8,128)(2,1)S(1)} collective-permute-done((bf16[64,256]{1,0:T(8,128)(2,1)S(1)}, bf16[64,256]{1,0:T(8,128)(2,1)S(1)}, u32[]{:S(2)}, u32[]{:S(2)}) %collective-permute-start.3) | collective-permute-done | bytes 32800 | tf_op jit(solution)/shard_map/ppermute | solution.py:342
  58.8 6.4 %all-to-all-done.1.parts_ref = bf16[16,72,256]{2,1,0:T(8,128)(2,1)S(1)} async-done(((bf16[16,72,256]{2,1,0:T(8,128)(2,1)}), bf16[16,72,256]{2,1,0:T(8,128)(2,1)S(1)}, u32[]{:S(2)}, u32[]{:S(2)}) %all-to-all-start.1) | async-done | bytes 589856 | tf_op jit(solution)/shard_map/all_to_all | solution.py:325
  65.1 0.7 sum.4
  65.9 6.0 %all-to-all-start.2 = ((bf16[4,72,256]{2,1,0:T(8,128)(2,1)}), bf16[4,72,256]{2,1,0:T(8,128)(2,1)S(1)}, u32[]{:S(2)}, u32[]{:S(2)}) async-start(bf16[4,72,256]{2,1,0:T(8,128)(2,1)} %sum.4), calls=%async_computation.2 | async-start | bytes 294912 | tf_op jit(solution)/shard_map/all_to_all | solution.py:325
  71.9 1.2 %copy-done.3 = f32[1088,256]{1,0:T(8,128)S(1)} copy-done((f32[1088,256]{1,0:T(8,128)S(1)}, f32[1088,256]{1,0:T(8,128)}, u32[]{:S(2)}) %copy-start.3) | copy-done | bytes 1114136
  73.1 2.2 %input.1 = bf16[1024,256]{1,0:T(8,128)(2,1)} custom-call(f32[1088,256]{1,0:T(8,128)S(1)} %copy-done.3, bf16[896,256]{1,0:T(8,128)(2,1)S(1)} %collective-permute-done.4.above_ref, bf16[64,256]{1,0:T(8,128)(2,1)S(1)} %collective-permute-done.3.below_ref, bf16[9,256,256]{2,1,0:T(8,128)(2,1)S(1)} %bitcast.21), custom_call_target="tpu_custom_call" | custom-call | flops 1207959552 | bytes 4194304 | tf_op jit(solution)/shard_map/input/pallas_call | solution.py:277
  75.4 1.8 %all-to-all-done.2.parts_ref = bf16[4,72,256]{2,1,0:T(8,128)(2,1)S(1)} async-done(((bf16[4,72,256]{2,1,0:T(8,128)(2,1)}), bf16[4,72,256]{2,1,0:T(8,128)(2,1)S(1)}, u32[]{:S(2)}, u32[]{:S(2)}) %all-to-all-start.2) | async-done | bytes 147488 | tf_op jit(solution)/shard_map/all_to_all | solution.py:325
  77.2 10.4 %all_gather.6.parts_ref = bf16[2,72,256]{2,1,0:T(8,128)(2,1)S(1)} all-gather(bf16[1,72,256]{2,1,0:T(8,128)(2,1)S(1)} %sum.5), channel_id=1, replica_groups={{0,128},{256,384},{1,129},{257,385},{2,130},{258,386},{3,131},{259,387}..., dimensions={0}, use_global_device_ids=true | all-gather | bytes 110592 | tf_op jit(solution)/shard_map/all_gather | solution.py:349
  87.6 9.6 %all_gather.7.parts_ref = bf16[2,72,256]{2,1,0:T(8,128)(2,1)S(1)} all-gather(bf16[1,72,256]{2,1,0:T(8,128)(2,1)S(1)} %sum.6), channel_id=1, replica_groups={{0,384},{128,256},{1,385},{129,257},{2,386},{130,258},{3,387},{131,259}..., dimensions={0}, use_global_device_ids=true | all-gather | bytes 110592 | tf_op jit(solution)/shard_map/all_gather | solution.py:351
  97.2 0.6 sum.7
  (13 shorter events, 0.1 us)
Async XLA Ops:
  5.2 7.5 %copy-start = (bf16[1,16,64,256]{3,2,1,0:T(8,128)(2,1)S(1)}, bf16[1,16,64,256]{3,2,1,0:T(8,128)(2,1)}, u32[]{:S(2)}) copy-start(bf16[1,16,64,256]{3,2,1,0:T(8,128)(2,1)} %param.5) | copy-start | bytes 1572868
  5.2 32.0 %all-to-all-start = ((bf16[32,104,256]{2,1,0:T(8,128)(2,1)}), bf16[32,104,256]{2,1,0:T(8,128)(2,1)S(1)}, u32[]{:S(2)}, u32[]{:S(2)}) async-start(bf16[32,104,256]{2,1,0:T(8,128)(2,1)} %dispatch.1), calls=%async_computation | async-start | bytes 3407872 | tf_op jit(solution)/shard_map/all_to_all | solution.py:325
  12.7 29.7 %collective-permute-start = (bf16[64,256]{1,0:T(8,128)(2,1)S(1)}, bf16[64,256]{1,0:T(8,128)(2,1)S(1)}, u32[]{:S(2)}, u32[]{:S(2)}) collective-permute-start(bf16[64,256]{1,0:T(8,128)(2,1)S(1)} %slice_bitcast_fusion), channel_id=1, source_target_pairs={{0,1},{1,2},{2,3},{3,4},{4,5},{5,6},{6,7},{7,8},{8,9},{9,10},{10,1... | collective-permute-start | bytes 98312 | tf_op jit(solution)/shard_map/ppermute | solution.py:334
  15.7 26.7 %collective-permute-start.1 = (bf16[896,256]{1,0:T(8,128)(2,1)}, bf16[896,256]{1,0:T(8,128)(2,1)S(1)}, u32[]{:S(2)}, u32[]{:S(2)}) collective-permute-start(bf16[896,256]{1,0:T(8,128)(2,1)} %bitcast.8), channel_id=1, source_target_pairs={{1,0},{2,1},{3,2},{4,3},{5,4},{6,5},{7,6},{8,7},{9,8},{10,9},{11,1... | collective-permute-start | bytes 1376264 | tf_op jit(solution)/shard_map/ppermute | solution.py:335
  42.4 1.5 %copy-start.2 = (f32[1088,256]{1,0:T(8,128)}, f32[1088,256]{1,0:T(8,128)S(1)}, u32[]{:S(2)}) copy-start(f32[1088,256]{1,0:T(8,128)S(1)} %get-tuple-element.19.own_ref) | copy-start | bytes 3342340
  43.9 3.9 %collective-permute-start.2 = (bf16[16,72,256]{2,1,0:T(8,128)(2,1)S(1)}, bf16[16,72,256]{2,1,0:T(8,128)(2,1)S(1)}, u32[]{:S(2)}, u32[]{:S(2)}) collective-permute-start(bf16[16,72,256]{2,1,0:T(8,128)(2,1)S(1)} %get-tuple-element.16), channel_id=1, source_target_pairs={{0,1},{1,0},{2,3},{3,2},{4,5},{5,4},{6,7},{7,6},{8,9},{9,8},{10,11... | collective-permute-start | bytes 1769480 | tf_op jit(solution)/shard_map/ppermute | solution.py:340
  47.8 24.1 %copy-start.1 = (bf16[3,3,256,256]{3,2,1,0:T(8,128)(2,1)S(1)}, bf16[3,3,256,256]{3,2,1,0:T(8,128)(2,1)}, u32[]{:S(2)}) copy-start(bf16[3,3,256,256]{3,2,1,0:T(8,128)(2,1)} %param.6) | copy-start | bytes 3538948
  48.7 16.4 %all-to-all-start.1 = ((bf16[16,72,256]{2,1,0:T(8,128)(2,1)}), bf16[16,72,256]{2,1,0:T(8,128)(2,1)S(1)}, u32[]{:S(2)}, u32[]{:S(2)}) async-start(bf16[16,72,256]{2,1,0:T(8,128)(2,1)} %pair.1), calls=%async_computation.1 | async-start | bytes 1179648 | tf_op jit(solution)/shard_map/all_to_all | solution.py:325
  52.3 19.6 %collective-permute-start.4 = (bf16[896,256]{1,0:T(8,128)(2,1)S(1)}, bf16[896,256]{1,0:T(8,128)(2,1)S(1)}, u32[]{:S(2)}, u32[]{:S(2)}) collective-permute-start(bf16[896,256]{1,0:T(8,128)(2,1)S(1)} %get-tuple-element.20), channel_id=1, source_target_pairs={{0,1},{1,2},{2,3},{3,4},{4,5},{5,6},{6,7},{7,8},{8,9},{9,10},{10,1... | collective-permute-start | bytes 1376264 | tf_op jit(solution)/shard_map/ppermute | solution.py:345
  54.4 4.4 %collective-permute-start.3 = (bf16[64,256]{1,0:T(8,128)(2,1)S(1)}, bf16[64,256]{1,0:T(8,128)(2,1)S(1)}, u32[]{:S(2)}, u32[]{:S(2)}) collective-permute-start(bf16[64,256]{1,0:T(8,128)(2,1)S(1)} %get-tuple-element.17), channel_id=1, source_target_pairs={{1,0},{2,1},{3,2},{4,3},{5,4},{6,5},{7,6},{8,7},{9,8},{10,9},{11,1... | collective-permute-start | bytes 98312 | tf_op jit(solution)/shard_map/ppermute | solution.py:342
  65.9 11.3 %all-to-all-start.2 = ((bf16[4,72,256]{2,1,0:T(8,128)(2,1)}), bf16[4,72,256]{2,1,0:T(8,128)(2,1)S(1)}, u32[]{:S(2)}, u32[]{:S(2)}) async-start(bf16[4,72,256]{2,1,0:T(8,128)(2,1)} %sum.4), calls=%async_computation.2 | async-start | bytes 294912 | tf_op jit(solution)/shard_map/all_to_all | solution.py:325
  71.9 1.2 %copy-start.3 = (f32[1088,256]{1,0:T(8,128)S(1)}, f32[1088,256]{1,0:T(8,128)}, u32[]{:S(2)}) copy-start(f32[1088,256]{1,0:T(8,128)} %copy-done.2) | copy-start | bytes 3342340

commit v10 on v8

--- a/solution.py
+++ b/solution.py
@@ -140,19 +140,19 @@
 
 
 def weights_of(got_ref, rows_ref, cols_ref):
-    slot = iota((SLOTS, KDIM), 0)
-    cell = iota((SLOTS, KDIM), 1)
-    first = (slot % TILES) * BLOCK + (slot // TILES) * SLOT
+    lane = iota((1, KDIM), 1)
+    source = lane // BLOCK
+    within = lane - source * BLOCK
+    later = (within >= SLOT).astype(I32)
+    within = within - later * SLOT
+    inside = within < CELLS
+    slot = jnp.where(inside, source + later * TILES, -1)
     box = jnp.concatenate(
         [got_ref[:, s * SLOT + CELLS, :LANES].astype(F32) for s in range(CAP)], axis=0
     )
     box = box.T[:8].astype(BF16)
-    cover = ((cell >= first) & (cell < first + CELLS)).astype(F32).astype(BF16)
+    cover = (iota((SLOTS, KDIM), 0) == slot).astype(F32).astype(BF16)
     field = jnp.dot(box, cover, preferred_element_type=F32).astype(I32)
-    within = iota((1, KDIM), 1) % BLOCK
-    inside = within < CAP * SLOT
-    within = within % SLOT
-    inside = inside & (within < CELLS)
     row_bin = within // BINS
     col_bin = within - row_bin * BINS
     row = jnp.where(inside, field[0:1] + row_bin * field[2:3], -9)

time: 98.2 us -> 98 us (level)
  no operation moved by 1% of the time
where the time goes in v10:
time: 98 us; the launch traced here: 97.5 us
  waiting for transfers between devices  33.5 us (34%)
  starting transfers between devices  25.8 us (26%)
  blocking collectives  20 us (20%)
  Pallas kernels  15.4 us (16%)
  local copies, waits for them, and re-layouts  2.06 us (2%)
    all_to_all x3, waiting for transfers between devices, exchange(): return lax.all_to_all(parts, axis, split_axis=0, concat_axis=0, tiled=True)  28.5 us
    all_to_all x3, starting transfers between devices, exchange(): return lax.all_to_all(parts, axis, split_axis=0, concat_axis=0, tiled=True)  17 us
    all_gather x1, blocking collectives, body(): lax.all_gather(parts, 'zh', tiled=True, axis_index_groups=[[0, 1], [2, 3]])  10.4 us
    all_gather x1, blocking collectives, body(): lax.all_gather(parts, 'zh', tiled=True, axis_index_groups=[[0, 3], [1, 2]])  9.58 us
    pallas_call x1, Pallas kernels, filter_part(): pl.pallas_call(filter_kernel, out_shape=(jax.ShapeDtypeStruct((3, 3 * C,...  5.13 us
    pallas_call x1, Pallas kernels, dispatch(): pl.pallas_call(dispatch_kernel, out_shape=jax.ShapeDtypeStruct((TILES, BL...  4.21 us
    ppermute x1, waiting for transfers between devices, body(): below = lax.ppermute(below, TILE_AXES, down)  3.05 us
    pallas_call x1, Pallas kernels, input_part(): pl.pallas_call(input_kernel, out_shape=jax.ShapeDtypeStruct((TR * MW, C),...  2.23 us
  transfers between devices with their start and end apart: 8, of which 5 were waited for; matrix products, arithmetic and copies ran while one was open for 1% of the time, Pallas kernels for 8%

profile of v10, /device:TPU:32, one launch (start us, length us, event | category | flops | bytes accessed | tf_op | source)
XLA Modules:
  0.0 97.5 jit_solution(16391351835487960607)
XLA Ops:
  0.6 4.2 %dispatch.1 = bf16[32,104,256]{2,1,0:T(8,128)(2,1)} custom-call(s32[1,16]{1,0:T(1,128)} %index_hbm.1, s32[4,20000]{1,0:T(4,128)} %bitcast.24, bf16[49,16,256]{2,1,0:T(8,128)(2,1)} %bitcast.23), custom_call_target="tpu_custom_call" | custom-call | flops 1363148800 | bytes 3145728 | tf_op jit(solution)/shard_map/dispatch/pallas_call | solution.py:124
  4.9 7.5 %all-to-all-start = ((bf16[32,104,256]{2,1,0:T(8,128)(2,1)}), bf16[32,104,256]{2,1,0:T(8,128)(2,1)S(1)}, u32[]{:S(2)}, u32[]{:S(2)}) async-start(bf16[32,104,256]{2,1,0:T(8,128)(2,1)} %dispatch.1), calls=%async_computation | async-start | bytes 3407872 | tf_op jit(solution)/shard_map/all_to_all | solution.py:353
  12.4 2.2 %collective-permute-start = (bf16[64,256]{1,0:T(8,128)(2,1)S(1)}, bf16[64,256]{1,0:T(8,128)(2,1)S(1)}, u32[]{:S(2)}, u32[]{:S(2)}) collective-permute-start(bf16[64,256]{1,0:T(8,128)(2,1)S(1)} %slice_bitcast_fusion), channel_id=1, source_target_pairs={{0,1},{1,2},{2,3},{3,4},{4,5},{5,6},{6,7},{7,8},{8,9},{9,10},{10,1... | collective-permute-start | bytes 98312 | tf_op jit(solution)/shard_map/ppermute | solution.py:362
  14.5 0.8 slice.14
  15.3 1.3 %collective-permute-start.1 = (bf16[896,256]{1,0:T(8,128)(2,1)}, bf16[896,256]{1,0:T(8,128)(2,1)S(1)}, u32[]{:S(2)}, u32[]{:S(2)}) collective-permute-start(bf16[896,256]{1,0:T(8,128)(2,1)} %bitcast.8), channel_id=1, source_target_pairs={{1,0},{2,1},{3,2},{4,3},{5,4},{6,5},{7,6},{8,7},{9,8},{10,9},{11,1... | collective-permute-start | bytes 1376264 | tf_op jit(solution)/shard_map/ppermute | solution.py:363
  16.6 20.3 %all-to-all-done.got_ref = bf16[32,104,256]{2,1,0:T(8,128)(2,1)S(1)} async-done(((bf16[32,104,256]{2,1,0:T(8,128)(2,1)}), bf16[32,104,256]{2,1,0:T(8,128)(2,1)S(1)}, u32[]{:S(2)}, u32[]{:S(2)}) %all-to-all-start) | async-done | bytes 1703968 | tf_op jit(solution)/shard_map/all_to_all | solution.py:353
  36.9 5.1 %filter.1 = (f32[3,768,256]{2,1,0:T(8,128)S(1)}, bf16[1152,256]{1,0:T(8,128)(2,1)S(1)}, f32[1088,256]{1,0:T(8,128)S(1)}, bf16[896,256]{1,0:T(8,128)(2,1)S(1)}, bf16[64,256]{1,0:T(8,128)(2,1)S(1)}) custom-call(bf16[32,104,256]{2,1,0:T(8,128)(2,1)S(1)} %all-to-all-done.got_ref, bf16[1024,256]{1,0:T(8,128)(2,1)S(1)} %bitcast.20), custom_call_target="tpu_custom_call" | custom-call | flops 5578424320 | bytes 4194304 | tf_op jit(solution)/shard_map/filter/pallas_call | solution.py:256
  42.1 1.4 %beyond.1 = (f32[16,72,256]{2,1,0:T(8,128)S(1)}, bf16[16,72,256]{2,1,0:T(8,128)(2,1)S(1)}) custom-call(s32[1]{0:T(128)} %bitcast.core_ref, f32[3,768,256]{2,1,0:T(8,128)S(1)} %get-tuple-element.13.part_ref, bf16[1152,256]{1,0:T(8,128)(2,1)S(1)} %get-tuple-element.14.beyond_ref, bf16[64,256]{1,0:T(8,128)(2,1)S(1)} %collective-permute-done.before_ref, ...), custom_call_target="tpu_custom_call" | custom-call | flops 1207959552 | bytes 4194304 | tf_op jit(solution)/shard_map/beyond/pallas_call | solution.py:240
  43.6 1.9 %collective-permute-start.2 = (bf16[16,72,256]{2,1,0:T(8,128)(2,1)S(1)}, bf16[16,72,256]{2,1,0:T(8,128)(2,1)S(1)}, u32[]{:S(2)}, u32[]{:S(2)}) collective-permute-start(bf16[16,72,256]{2,1,0:T(8,128)(2,1)S(1)} %get-tuple-element.16), channel_id=1, source_target_pairs={{0,1},{1,0},{2,3},{3,2},{4,5},{5,4},{6,7},{7,6},{8,9},{9,8},{10,11... | collective-permute-start | bytes 1769480 | tf_op jit(solution)/shard_map/ppermute | solution.py:368
  45.5 2.0 %collective-permute-done.2.got_ref = bf16[16,72,256]{2,1,0:T(8,128)(2,1)S(1)} collective-permute-done((bf16[16,72,256]{2,1,0:T(8,128)(2,1)S(1)}, bf16[16,72,256]{2,1,0:T(8,128)(2,1)S(1)}, u32[]{:S(2)}, u32[]{:S(2)}) %collective-permute-start.2) | collective-permute-done | bytes 589856 | tf_op jit(solution)/shard_map/ppermute | solution.py:368
  47.5 0.9 pair.1
  48.4 3.6 %all-to-all-start.1 = ((bf16[16,72,256]{2,1,0:T(8,128)(2,1)}), bf16[16,72,256]{2,1,0:T(8,128)(2,1)S(1)}, u32[]{:S(2)}, u32[]{:S(2)}) async-start(bf16[16,72,256]{2,1,0:T(8,128)(2,1)} %pair.1), calls=%async_computation.1 | async-start | bytes 1179648 | tf_op jit(solution)/shard_map/all_to_all | solution.py:353
  52.0 2.1 %collective-permute-start.4 = (bf16[896,256]{1,0:T(8,128)(2,1)S(1)}, bf16[896,256]{1,0:T(8,128)(2,1)S(1)}, u32[]{:S(2)}, u32[]{:S(2)}) collective-permute-start(bf16[896,256]{1,0:T(8,128)(2,1)S(1)} %get-tuple-element.20), channel_id=1, source_target_pairs={{0,1},{1,2},{2,3},{3,4},{4,5},{5,6},{6,7},{7,8},{8,9},{9,10},{10,1... | collective-permute-start | bytes 1376264 | tf_op jit(solution)/shard_map/ppermute | solution.py:373
  54.0 1.3 %collective-permute-start.3 = (bf16[64,256]{1,0:T(8,128)(2,1)S(1)}, bf16[64,256]{1,0:T(8,128)(2,1)S(1)}, u32[]{:S(2)}, u32[]{:S(2)}) collective-permute-start(bf16[64,256]{1,0:T(8,128)(2,1)S(1)} %get-tuple-element.17), channel_id=1, source_target_pairs={{1,0},{2,1},{3,2},{4,3},{5,4},{6,5},{7,6},{8,7},{9,8},{10,9},{11,1... | collective-permute-start | bytes 98312 | tf_op jit(solution)/shard_map/ppermute | solution.py:370
  55.3 3.1 %collective-permute-done.3.below_ref = bf16[64,256]{1,0:T(8,128)(2,1)S(1)} collective-permute-done((bf16[64,256]{1,0:T(8,128)(2,1)S(1)}, bf16[64,256]{1,0:T(8,128)(2,1)S(1)}, u32[]{:S(2)}, u32[]{:S(2)}) %collective-permute-start.3) | collective-permute-done | bytes 32800 | tf_op jit(solution)/shard_map/ppermute | solution.py:370
  58.4 6.4 %all-to-all-done.1.parts_ref = bf16[16,72,256]{2,1,0:T(8,128)(2,1)S(1)} async-done(((bf16[16,72,256]{2,1,0:T(8,128)(2,1)}), bf16[16,72,256]{2,1,0:T(8,128)(2,1)S(1)}, u32[]{:S(2)}, u32[]{:S(2)}) %all-to-all-start.1) | async-done | bytes 589856 | tf_op jit(solution)/shard_map/all_to_all | solution.py:353
  64.8 0.7 sum.4
  65.5 6.0 %all-to-all-start.2 = ((bf16[4,72,256]{2,1,0:T(8,128)(2,1)}), bf16[4,72,256]{2,1,0:T(8,128)(2,1)S(1)}, u32[]{:S(2)}, u32[]{:S(2)}) async-start(bf16[4,72,256]{2,1,0:T(8,128)(2,1)} %sum.4), calls=%async_computation.2 | async-start | bytes 294912 | tf_op jit(solution)/shard_map/all_to_all | solution.py:353
  71.5 1.2 %copy-done.3 = f32[1088,256]{1,0:T(8,128)S(1)} copy-done((f32[1088,256]{1,0:T(8,128)S(1)}, f32[1088,256]{1,0:T(8,128)}, u32[]{:S(2)}) %copy-start.3) | copy-done | bytes 1114136
  72.8 2.2 %input.1 = bf16[1024,256]{1,0:T(8,128)(2,1)} custom-call(f32[1088,256]{1,0:T(8,128)S(1)} %copy-done.3, bf16[896,256]{1,0:T(8,128)(2,1)S(1)} %collective-permute-done.4.above_ref, bf16[64,256]{1,0:T(8,128)(2,1)S(1)} %collective-permute-done.3.below_ref, bf16[9,256,256]{2,1,0:T(8,128)(2,1)S(1)} %bitcast.21), custom_call_target="tpu_custom_call" | custom-call | flops 1207959552 | bytes 4194304 | tf_op jit(solution)/shard_map/input/pallas_call | solution.py:305
  75.0 1.8 %all-to-all-done.2.parts_ref = bf16[4,72,256]{2,1,0:T(8,128)(2,1)S(1)} async-done(((bf16[4,72,256]{2,1,0:T(8,128)(2,1)}), bf16[4,72,256]{2,1,0:T(8,128)(2,1)S(1)}, u32[]{:S(2)}, u32[]{:S(2)}) %all-to-all-start.2) | async-done | bytes 147488 | tf_op jit(solution)/shard_map/all_to_all | solution.py:353
  76.8 10.4 %all_gather.6.parts_ref = bf16[2,72,256]{2,1,0:T(8,128)(2,1)S(1)} all-gather(bf16[1,72,256]{2,1,0:T(8,128)(2,1)S(1)} %sum.5), channel_id=1, replica_groups={{0,128},{256,384},{1,129},{257,385},{2,130},{258,386},{3,131},{259,387}..., dimensions={0}, use_global_device_ids=true | all-gather | bytes 110592 | tf_op jit(solution)/shard_map/all_gather | solution.py:377
  87.2 9.6 %all_gather.7.parts_ref = bf16[2,72,256]{2,1,0:T(8,128)(2,1)S(1)} all-gather(bf16[1,72,256]{2,1,0:T(8,128)(2,1)S(1)} %sum.6), channel_id=1, replica_groups={{0,384},{128,256},{1,385},{129,257},{2,386},{130,258},{3,387},{131,259}..., dimensions={0}, use_global_device_ids=true | all-gather | bytes 110592 | tf_op jit(solution)/shard_map/all_gather | solution.py:379
  96.8 0.6 sum.7
  (13 shorter events, 0.1 us)
Async XLA Ops:
  4.9 7.5 %copy-start = (bf16[1,16,64,256]{3,2,1,0:T(8,128)(2,1)S(1)}, bf16[1,16,64,256]{3,2,1,0:T(8,128)(2,1)}, u32[]{:S(2)}) copy-start(bf16[1,16,64,256]{3,2,1,0:T(8,128)(2,1)} %param.5) | copy-start | bytes 1572868
  4.9 32.1 %all-to-all-start = ((bf16[32,104,256]{2,1,0:T(8,128)(2,1)}), bf16[32,104,256]{2,1,0:T(8,128)(2,1)S(1)}, u32[]{:S(2)}, u32[]{:S(2)}) async-start(bf16[32,104,256]{2,1,0:T(8,128)(2,1)} %dispatch.1), calls=%async_computation | async-start | bytes 3407872 | tf_op jit(solution)/shard_map/all_to_all | solution.py:353
  12.4 29.7 %collective-permute-start = (bf16[64,256]{1,0:T(8,128)(2,1)S(1)}, bf16[64,256]{1,0:T(8,128)(2,1)S(1)}, u32[]{:S(2)}, u32[]{:S(2)}) collective-permute-start(bf16[64,256]{1,0:T(8,128)(2,1)S(1)} %slice_bitcast_fusion), channel_id=1, source_target_pairs={{0,1},{1,2},{2,3},{3,4},{4,5},{5,6},{6,7},{7,8},{8,9},{9,10},{10,1... | collective-permute-start | bytes 98312 | tf_op jit(solution)/shard_map/ppermute | solution.py:362
  15.3 26.7 %collective-permute-start.1 = (bf16[896,256]{1,0:T(8,128)(2,1)}, bf16[896,256]{1,0:T(8,128)(2,1)S(1)}, u32[]{:S(2)}, u32[]{:S(2)}) collective-permute-start(bf16[896,256]{1,0:T(8,128)(2,1)} %bitcast.8), channel_id=1, source_target_pairs={{1,0},{2,1},{3,2},{4,3},{5,4},{6,5},{7,6},{8,7},{9,8},{10,9},{11,1... | collective-permute-start | bytes 1376264 | tf_op jit(solution)/shard_map/ppermute | solution.py:363
  42.1 1.5 %copy-start.2 = (f32[1088,256]{1,0:T(8,128)}, f32[1088,256]{1,0:T(8,128)S(1)}, u32[]{:S(2)}) copy-start(f32[1088,256]{1,0:T(8,128)S(1)} %get-tuple-element.19.own_ref) | copy-start | bytes 3342340
  43.6 3.9 %collective-permute-start.2 = (bf16[16,72,256]{2,1,0:T(8,128)(2,1)S(1)}, bf16[16,72,256]{2,1,0:T(8,128)(2,1)S(1)}, u32[]{:S(2)}, u32[]{:S(2)}) collective-permute-start(bf16[16,72,256]{2,1,0:T(8,128)(2,1)S(1)} %get-tuple-element.16), channel_id=1, source_target_pairs={{0,1},{1,0},{2,3},{3,2},{4,5},{5,4},{6,7},{7,6},{8,9},{9,8},{10,11... | collective-permute-start | bytes 1769480 | tf_op jit(solution)/shard_map/ppermute | solution.py:368
  47.5 24.1 %copy-start.1 = (bf16[3,3,256,256]{3,2,1,0:T(8,128)(2,1)S(1)}, bf16[3,3,256,256]{3,2,1,0:T(8,128)(2,1)}, u32[]{:S(2)}) copy-start(bf16[3,3,256,256]{3,2,1,0:T(8,128)(2,1)} %param.6) | copy-start | bytes 3538948
  48.4 16.4 %all-to-all-start.1 = ((bf16[16,72,256]{2,1,0:T(8,128)(2,1)}), bf16[16,72,256]{2,1,0:T(8,128)(2,1)S(1)}, u32[]{:S(2)}, u32[]{:S(2)}) async-start(bf16[16,72,256]{2,1,0:T(8,128)(2,1)} %pair.1), calls=%async_computation.1 | async-start | bytes 1179648 | tf_op jit(solution)/shard_map/all_to_all | solution.py:353
  52.0 19.5 %collective-permute-start.4 = (bf16[896,256]{1,0:T(8,128)(2,1)S(1)}, bf16[896,256]{1,0:T(8,128)(2,1)S(1)}, u32[]{:S(2)}, u32[]{:S(2)}) collective-permute-start(bf16[896,256]{1,0:T(8,128)(2,1)S(1)} %get-tuple-element.20), channel_id=1, source_target_pairs={{0,1},{1,2},{2,3},{3,4},{4,5},{5,6},{6,7},{7,8},{8,9},{9,10},{10,1... | collective-permute-start | bytes 1376264 | tf_op jit(solution)/shard_map/ppermute | solution.py:373
  54.0 4.4 %collective-permute-start.3 = (bf16[64,256]{1,0:T(8,128)(2,1)S(1)}, bf16[64,256]{1,0:T(8,128)(2,1)S(1)}, u32[]{:S(2)}, u32[]{:S(2)}) collective-permute-start(bf16[64,256]{1,0:T(8,128)(2,1)S(1)} %get-tuple-element.17), channel_id=1, source_target_pairs={{1,0},{2,1},{3,2},{4,3},{5,4},{6,5},{7,6},{8,7},{9,8},{10,9},{11,1... | collective-permute-start | bytes 98312 | tf_op jit(solution)/shard_map/ppermute | solution.py:370
  65.5 11.3 %all-to-all-start.2 = ((bf16[4,72,256]{2,1,0:T(8,128)(2,1)}), bf16[4,72,256]{2,1,0:T(8,128)(2,1)S(1)}, u32[]{:S(2)}, u32[]{:S(2)}) async-start(bf16[4,72,256]{2,1,0:T(8,128)(2,1)} %sum.4), calls=%async_computation.2 | async-start | bytes 294912 | tf_op jit(solution)/shard_map/all_to_all | solution.py:353
  71.5 1.2 %copy-start.3 = (f32[1088,256]{1,0:T(8,128)S(1)}, f32[1088,256]{1,0:T(8,128)}, u32[]{:S(2)}) copy-start(f32[1088,256]{1,0:T(8,128)} %copy-done.2) | copy-start | bytes 3342340
